TPU v7x, 128 devices: a whole 4x4x4 slice. The times are simulated.
128 devices in a mesh: lon: 16 (over y, x_lo, core), ens: 8 (over x_hi, z).
Axes of the slice: x: 4 (x_hi: 2, x_lo: 2; x = x_hi * 2 + x_lo), y: 4, z: 4, core: 2. Of those that a mesh axis runs over, the one named last changes fastest.
Arguments:
- members_in: bfloat16 [8, 64, 8, 4096], P('ens', None, None, 'lon'), may hold values from -6 to 6
- cotangent: bfloat16 [8, 64, 8, 4096], P('ens', None, None, 'lon'), may hold values from -6 to 6
- conv_weight: bfloat16 [4, 64, 576], replicated, may hold values from -0.25 to 0.25
- expand_weight: bfloat16 [4, 256, 64], replicated, may hold values from -0.75 to 0.75
- expand_bias: float32 [4, 256], replicated, may hold values from -3 to 3
- project_weight: bfloat16 [4, 64, 256], replicated, may hold values from -0.375 to 0.375
- orient: int32 [16], replicated, may hold values from 0 to 1
Outputs:
- section_out: bfloat16 [8, 64, 8, 4096], P('ens', None, None, 'lon')
- input_grad: bfloat16 [8, 64, 8, 4096], P('ens', None, None, 'lon')
- conv_grad: float32 [4, 64, 576], P(None, 'ens')
- expand_grad: float32 [4, 256, 64], P(None, 'ens')
- project_grad: float32 [4, 64, 256], P(None, 'ens')
Inputs may be any that keep to these rules, and one draw needn't show every extreme that they name: `orient`: 1 where a sector stores its latitude rows in reversed order.
All inputs are finite; a program needn't handle non-finite values.
Results may differ from a plain program's by a relative error of at most 0.034.
Values may be sent and summed in bfloat16 or wider, within the bound.
No kernel may reach another device: no remote copies, remote signals or barrier semaphores. Data moves between devices by JAX's collectives and lax.ppermute only.
A program may use at most 128 MiB of HBM per device.

v0:
```python
import jax
import jax.numpy as jnp
from jax import lax
from jax.sharding import PartitionSpec as P

SQRT_HALF = 0.7071067811865476
INV_ROOT_TAU = 0.3989422804014327


def extended(block, sides, width):
    for axis, dim in sides:
        count = lax.axis_size(axis)
        forward = [(i, i + 1) for i in range(count - 1)]
        forward.append((count - 1, 0))
        backward = [(target, source) for source, target in forward]
        low = lax.ppermute(
            lax.slice_in_dim(block, block.shape[dim] - width, None, axis=dim), axis, forward
        )
        high = lax.ppermute(lax.slice_in_dim(block, 0, width, axis=dim), axis, backward)
        block = jnp.concatenate([low, block, high], axis=dim)
    return block


def gelu_curve(value):
    return 0.5 * value * (1.0 + jax.scipy.special.erf(value * SQRT_HALF))


def gelu_slope(value):
    return 0.5 * (1.0 + jax.scipy.special.erf(value * SQRT_HALF)) + value * INV_ROOT_TAU * jnp.exp(
        -0.5 * value * value
    )


def pad_rows(block):
    return jnp.pad(block, ((0, 0), (1, 1), (0, 0)))


def outer_sum(left, right):
    return lax.dot_general(
        left, right, (((1,), (1,)), ((), ())), preferred_element_type=jnp.float32
    )


def conv_forward(padded, kernel, count_rows, count_cols):
    channels = kernel.shape[0]
    running = jnp.zeros((channels, count_rows * count_cols), jnp.float32)
    for row_step in range(3):
        for col_step in range(3):
            offset = 3 * row_step + col_step
            window = padded[
                :, row_step : row_step + count_rows, col_step : col_step + count_cols
            ].reshape(channels, -1)
            running = running + jnp.dot(
                kernel[:, offset * channels : (offset + 1) * channels],
                window,
                preferred_element_type=jnp.float32,
            )
    return running


def conv_transpose(padded, kernel, count_rows, count_cols):
    channels = kernel.shape[0]
    running = jnp.zeros((channels, count_rows * count_cols), jnp.float32)
    for row_step in range(3):
        for col_step in range(3):
            offset = 3 * row_step + col_step
            window = padded[
                :,
                2 - row_step : 2 - row_step + count_rows,
                2 - col_step : 2 - col_step + count_cols,
            ].reshape(channels, -1)
            running = running + jnp.dot(
                kernel[:, offset * channels : (offset + 1) * channels].T,
                window,
                preferred_element_type=jnp.float32,
            )
    return running


def kernel_grad(slope, padded, count_rows, count_cols):
    channels = slope.shape[0]
    terms = []
    for row_step in range(3):
        for col_step in range(3):
            window = padded[
                :, row_step : row_step + count_rows, col_step : col_step + count_cols
            ].reshape(channels, -1)
            terms.append(outer_sum(slope, window))
    return jnp.concatenate(terms, axis=1)


def block_forward(field_flat, padded, kernel, expand, bias, project, count_rows, count_cols):
    hidden = conv_forward(padded, kernel, count_rows, count_cols).astype(jnp.bfloat16)
    inner = jnp.dot(expand, hidden, preferred_element_type=jnp.float32) + bias[:, None]
    active = gelu_curve(inner).astype(jnp.bfloat16)
    output = (
        field_flat.astype(jnp.float32)
        + jnp.dot(project, active, preferred_element_type=jnp.float32)
    ).astype(jnp.bfloat16)
    return (hidden, inner, active, output)


def block_backward(
    upstream,
    hidden,
    inner,
    active,
    padded,
    kernel,
    expand,
    project,
    count_rows,
    count_cols,
    surround_slope,
):
    channels = kernel.shape[0]
    d_active = jnp.dot(project.T, upstream, preferred_element_type=jnp.float32)
    d_inner = (d_active * gelu_slope(inner)).astype(jnp.bfloat16)
    project_term = outer_sum(upstream, active)
    expand_term = outer_sum(d_inner, hidden)
    d_hidden = jnp.dot(expand.T, d_inner, preferred_element_type=jnp.float32).astype(jnp.bfloat16)
    kernel_term = kernel_grad(d_hidden, padded, count_rows, count_cols)
    widened = surround_slope(d_hidden.reshape(channels, count_rows, count_cols))
    d_field = (
        upstream.astype(jnp.float32) + conv_transpose(widened, kernel, count_rows, count_cols)
    ).astype(jnp.bfloat16)
    return (d_field, kernel_term, expand_term, project_term)


def surround_field(block):
    return pad_rows(extended(block, (("lon", 2),), 1))


def surround_slope(block):
    return pad_rows(extended(block, (("lon", 2),), 1))


def share_grads(grads):
    summed = (
        lax.psum(grads[0].astype(jnp.bfloat16), "lon").astype(jnp.float32),
        lax.psum(grads[1].astype(jnp.bfloat16), "lon").astype(jnp.float32),
        lax.psum(grads[2].astype(jnp.bfloat16), "lon").astype(jnp.float32),
    )
    return (
        lax.psum_scatter(
            summed[0].astype(jnp.bfloat16), "ens", scatter_dimension=0, tiled=True
        ).astype(jnp.float32),
        lax.psum_scatter(
            summed[1].astype(jnp.bfloat16), "ens", scatter_dimension=0, tiled=True
        ).astype(jnp.float32),
        lax.psum_scatter(
            summed[2].astype(jnp.bfloat16), "ens", scatter_dimension=0, tiled=True
        ).astype(jnp.float32),
    )


def local(members_in, cotangent, conv_weight, expand_weight, expand_bias, project_weight, orient):
    channels = members_in.shape[1]
    count_rows = members_in.shape[2]
    count_cols = members_in.shape[3]
    block_count = conv_weight.shape[0]
    sector_index = lax.axis_index("lon")
    sectors = jnp.arange(orient.shape[0], dtype=jnp.int32)
    own_flip = jnp.sum(jnp.where(sectors == sector_index, orient, 0)) == 1

    def to_frame(block):
        return jnp.where(own_flip, block[:, ::-1, :], block)

    field = to_frame(members_in[0])
    saved = []
    for block_index in range(block_count):
        padded = surround_field(field)
        hidden, inner, active, output = block_forward(
            field.reshape(channels, -1),
            padded,
            conv_weight[block_index],
            expand_weight[block_index],
            expand_bias[block_index],
            project_weight[block_index],
            count_rows,
            count_cols,
        )
        saved.append((padded, hidden, inner, active))
        field = output.reshape(channels, count_rows, count_cols)
    upstream = to_frame(cotangent[0]).reshape(channels, -1)
    kernel_shares = [None] * block_count
    expand_shares = [None] * block_count
    project_shares = [None] * block_count
    for block_index in reversed(range(block_count)):
        padded, hidden, inner, active = saved[block_index]
        upstream, kernel_term, expand_term, project_term = block_backward(
            upstream,
            hidden,
            inner,
            active,
            padded,
            conv_weight[block_index],
            expand_weight[block_index],
            project_weight[block_index],
            count_rows,
            count_cols,
            surround_slope,
        )
        kernel_shares[block_index], expand_shares[block_index], project_shares[block_index] = (
            share_grads((kernel_term, expand_term, project_term))
        )
    section_out = to_frame(field)[None]
    input_grad = to_frame(upstream.reshape(channels, count_rows, count_cols))[None]
    return (
        section_out,
        input_grad,
        jnp.stack(kernel_shares),
        jnp.stack(expand_shares),
        jnp.stack(project_shares),
    )


def solution(mesh):
    in_specs = (P("ens", None, None, "lon"), P("ens", None, None, "lon"), P(), P(), P(), P(), P())
    out_specs = (
        P("ens", None, None, "lon"),
        P("ens", None, None, "lon"),
        P(None, "ens", None),
        P(None, "ens", None),
        P(None, "ens", None),
    )
    return jax.shard_map(local, mesh=mesh, in_specs=in_specs, out_specs=out_specs, check_vma=False)
```

profile of v0, /device:TPU:1, one launch (start us, length us, event | category | flops | bytes accessed | tf_op | source)
XLA Modules:
  0.0 925.5 jit_solution(13699672397639537790)
XLA Ops:
  8.3 1.3 fusion.161
  11.3 2.7 collective-permute-start
  14.0 1.7 slice_bitcast_fusion
  15.9 3.1 collective-permute-done.1
  23.6 2.0 multiply_convert_fusion.3
  26.8 1.4 collective-permute-done.2
  28.2 4.3 collective-permute-done.3
  36.9 2.0 multiply_convert_fusion.2
  40.2 1.5 collective-permute-start.5
  43.3 2.4 collective-permute-done.5
  45.7 1.3 pad_maximum_fusion.10
  47.1 1.8 select_maximum_fusion.10
  52.2 2.0 multiply_convert_fusion.1
  54.2 1.3 fusion.26
  57.0 4.6 collective-permute-start.7
  63.9 1.4 pad_maximum_fusion.8
  65.4 1.8 select_maximum_fusion.8
  71.0 1.7 multiply_convert_fusion
  72.8 1.9 fusion.8
  80.9 4.9 collective-permute-start.9
  86.6 1.5 concatenate.115
  88.5 1.4 pad_maximum_fusion.6
  90.0 1.8 select_maximum_fusion.6
  96.6 2.0 fusion.9
  98.7 1.5 convolution_convert_fusion.2
  105.9 4.6 collective-permute-start.11
  111.3 1.5 concatenate.114
  112.9 1.4 pad_maximum_fusion.4
  114.4 1.8 select_maximum_fusion.4
  121.1 2.0 fusion.10
  123.1 1.4 convolution_convert_fusion.1
  130.3 6.1 collective-permute-start.13
  137.2 1.5 concatenate.113
  138.7 1.4 pad_maximum_fusion.2
  140.3 1.8 select_maximum_fusion.2
  146.9 2.0 fusion.11
  149.0 1.4 convolution_convert_fusion
  155.5 1.5 concatenate.112
  157.1 2.4 convolution_convert_fusion.4
  159.5 2.4 fusion.27
  162.0 2.2 convolution_convert_fusion.8
  164.2 1.7 copy.48
  165.9 1.7 rev.13
  167.6 2.4 convolution_convert_fusion.5
  170.1 1.8 convolution_convert_fusion.9
  172.0 2.5 convolution_convert_fusion.6
  174.5 1.8 convolution_convert_fusion.10
  176.5 2.0 convolution_convert_fusion.7
  178.8 5.3 collective-permute-start.15
  190.5 52.6 %all-reduce.19.cloned.1.call-done = (bf16[64,576]{1,0:T(8,128)(2,1)}, bf16[64,576]{1,0:T(8,128)(2,1)}, bf16[64,576]{1,0:T(8,128)(2,1)}, bf16[64,576]{1,0:T(8,128)(2,1)}) async-done(((bf16[64,576]{1,0:T(8,128)(2,1)}, bf16[64,576]{1,0:T(8,128)(2,1)}, bf16[64,576]{1,0:T(8,128)(2,1)}, bf16[64,576]{1,0:T(8,128)(2,1)}), (bf16[64,576]{1,0:T(8,128)(2,1)}, bf16[64,576]{1,0:T(8,128)(2,1)}, bf16[64,576]{1,0:T(8,128)(2,1)}, ...) | async-done | bytes 294928
  243.1 1.3 constant_dynamic-slice_fusion
  244.4 1.3 constant_dynamic-slice_fusion.2
  245.7 73.2 %reduce-scatter.15.cloned.1.call-done = bf16[32,64]{1,0:T(8,128)(2,1)} async-done(((bf16[256,64]{1,0:T(8,128)(2,1)}), bf16[32,64]{1,0:T(8,128)(2,1)}) %reduce-scatter.15.cloned.1.call-update) | async-done | bytes 4112 | tf_op jit(solution)/shard_map/reduce_scatter | solution.py:148
  319.0 65.3 %reduce-scatter.23.cloned.1.call-done = bf16[8,256]{1,0:T(8,128)(2,1)} async-done(((bf16[64,256]{1,0:T(8,128)(2,1)}), bf16[8,256]{1,0:T(8,128)(2,1)}) %reduce-scatter.23.cloned.1.call-update) | async-done | bytes 4112 | tf_op jit(solution)/shard_map/reduce_scatter | solution.py:151
  384.3 72.7 %reduce-scatter.13.cloned.1.call-done = bf16[32,64]{1,0:T(8,128)(2,1)} async-done(((bf16[256,64]{1,0:T(8,128)(2,1)}), bf16[32,64]{1,0:T(8,128)(2,1)}) %reduce-scatter.13.cloned.1.call-update) | async-done | bytes 4112 | tf_op jit(solution)/shard_map/reduce_scatter | solution.py:148
  457.0 64.6 %reduce-scatter.21.cloned.1.call-done = bf16[8,256]{1,0:T(8,128)(2,1)} async-done(((bf16[64,256]{1,0:T(8,128)(2,1)}), bf16[8,256]{1,0:T(8,128)(2,1)}) %reduce-scatter.21.cloned.1.call-update) | async-done | bytes 4112 | tf_op jit(solution)/shard_map/reduce_scatter | solution.py:151
  521.5 72.7 %reduce-scatter.11.cloned.1.call-done = bf16[32,64]{1,0:T(8,128)(2,1)} async-done(((bf16[256,64]{1,0:T(8,128)(2,1)}), bf16[32,64]{1,0:T(8,128)(2,1)}) %reduce-scatter.11.cloned.1.call-update) | async-done | bytes 4112 | tf_op jit(solution)/shard_map/reduce_scatter | solution.py:148
  594.2 64.7 %reduce-scatter.19.cloned.1.call-done = bf16[8,256]{1,0:T(8,128)(2,1)} async-done(((bf16[64,256]{1,0:T(8,128)(2,1)}), bf16[8,256]{1,0:T(8,128)(2,1)}) %reduce-scatter.19.cloned.1.call-update) | async-done | bytes 4112 | tf_op jit(solution)/shard_map/reduce_scatter | solution.py:151
  659.0 72.9 %reduce-scatter.9.cloned.1.call-done = bf16[32,64]{1,0:T(8,128)(2,1)} async-done(((bf16[256,64]{1,0:T(8,128)(2,1)}), bf16[32,64]{1,0:T(8,128)(2,1)}) %reduce-scatter.9.cloned.1.call-update) | async-done | bytes 4112 | tf_op jit(solution)/shard_map/reduce_scatter | solution.py:148
  731.8 65.4 %reduce-scatter.17.cloned.1.call-done = bf16[8,256]{1,0:T(8,128)(2,1)} async-done(((bf16[64,256]{1,0:T(8,128)(2,1)}), bf16[8,256]{1,0:T(8,128)(2,1)}) %reduce-scatter.17.cloned.1.call-update) | async-done | bytes 4112 | tf_op jit(solution)/shard_map/reduce_scatter | solution.py:151
  798.1 116.2 %all-reduce.17.cloned.1.call-done = (bf16[8,576]{1,0:T(8,128)(2,1)}, bf16[8,576]{1,0:T(8,128)(2,1)}, bf16[8,576]{1,0:T(8,128)(2,1)}, bf16[8,576]{1,0:T(8,128)(2,...) async-done(((bf16[8,576]{1,0:T(8,128)(2,1)}, ...) | async-done | bytes 69648 | tf_op jit(solution)/shard_map/psum | solution.py:140
  914.3 1.3 maximum_convert_fusion.2
  915.6 1.4 maximum_convert_fusion
  917.0 1.4 maximum_convert_fusion.1
  (463 shorter events, 72.5 us)
Async XLA Ops:
  7.2 8.5 copy-start.101
  7.2 235.9 %all-reduce.19.cloned.1.call-start = ((), (), s32[]{:S(2)}) async-start(), calls=%async_computation.17 | async-start | bytes 655360
  11.3 4.6 collective-permute-start
  14.0 5.0 collective-permute-start.1
  15.7 21.0 %copy-start.86 = (bf16[64,576]{1,0:T(8,128)(2,1)}, bf16[64,576]{1,0:T(8,128)(2,1)S(1)}, u32[]{:S(2)}) copy-start(bf16[64,576]{1,0:T(8,128)(2,1)S(1)} %get-tuple-element.70) | copy-start | bytes 221188
  15.7 36.2 %copy-start.88 = (bf16[64,576]{1,0:T(8,128)(2,1)}, bf16[64,576]{1,0:T(8,128)(2,1)S(1)}, u32[]{:S(2)}) copy-start(bf16[64,576]{1,0:T(8,128)(2,1)S(1)} %get-tuple-element.72) | copy-start | bytes 221188
  15.8 9.8 %copy-start.12 = (bf16[8,8,8,256]{3,1,2,0:T(8,128)(2,1)}, bf16[8,8,8,256]{3,1,2,0:T(8,128)(2,1)S(1)}, u32[]{:S(2)}) copy-start(bf16[8,8,8,256]{3,1,2,0:T(8,128)(2,1)S(1)} %copy.12) | copy-start | bytes 786436
  26.0 12.9 %copy-start.2 = (bf16[64,2048]{1,0:T(8,128)(2,1)}, bf16[64,2048]{1,0:T(8,128)(2,1)S(1)}, u32[]{:S(2)}) copy-start(bf16[64,2048]{1,0:T(8,128)(2,1)S(1)} %fusion.24) | copy-start | bytes 786436
  26.2 2.0 collective-permute-start.2
  26.3 6.2 collective-permute-start.3
  39.4 11.5 %copy-start.4 = (bf16[64,2048]{1,0:T(8,128)(2,1)}, bf16[64,2048]{1,0:T(8,128)(2,1)S(1)}, u32[]{:S(2)}) copy-start(bf16[64,2048]{1,0:T(8,128)(2,1)S(1)} %fusion.25) | copy-start | bytes 786436
  40.2 2.4 collective-permute-start.4
  40.2 5.5 collective-permute-start.5
  47.0 4.1 copy-start.62
  47.1 3.5 copy-start.60
  52.1 3.3 copy-start.44
  54.2 7.4 copy-start.93
  54.2 7.4 copy-start.95
  54.2 8.2 copy-start.102
  55.5 14.1 %copy-start = (bf16[64,2048]{1,0:T(8,128)(2,1)}, bf16[64,2048]{1,0:T(8,128)(2,1)S(1)}, u32[]{:S(2)}) copy-start(bf16[64,2048]{1,0:T(8,128)(2,1)S(1)} %fusion.26) | copy-start | bytes 786436
  57.0 6.6 collective-permute-start.6
  57.0 6.9 collective-permute-start.7
  75.6 10.2 %copy-start.1 = (bf16[64,2048]{1,0:T(8,128)(2,1)S(1)}, bf16[64,2048]{1,0:T(8,128)(2,1)}, u32[]{:S(2)}) copy-start(bf16[64,2048]{1,0:T(8,128)(2,1)} %copy-done) | copy-start | bytes 786436
  80.9 7.2 collective-permute-start.8
  80.9 7.6 collective-permute-start.9
  96.6 3.5 copy-start.70
  96.6 3.8 copy-start.72
  98.6 4.1 copy-start.8
  98.7 3.3 copy-start.61
  98.7 4.1 copy-start.66
  100.2 3.4 copy-start.68
  100.6 9.9 %copy-start.27 = (bf16[8,8,8,256]{3,1,2,0:T(8,128)(2,1)S(1)}, bf16[8,8,8,256]{3,1,2,0:T(8,128)(2,1)}, u32[]{:S(2)}) copy-start(bf16[8,8,8,256]{3,1,2,0:T(8,128)(2,1)} %copy-done.26) | copy-start | bytes 786436
  105.9 7.0 collective-permute-start.10
  105.9 7.0 collective-permute-start.11
  121.1 3.5 copy-start.54
  121.1 3.7 copy-start.56
  123.1 4.1 copy-start.9
  123.1 3.2 copy-start.46
  123.1 4.1 copy-start.50
  124.6 3.4 copy-start.52
  125.0 11.4 %copy-start.25 = (bf16[8,8,8,256]{3,1,2,0:T(8,128)(2,1)S(1)}, bf16[8,8,8,256]{3,1,2,0:T(8,128)(2,1)}, u32[]{:S(2)}) copy-start(bf16[8,8,8,256]{3,1,2,0:T(8,128)(2,1)} %copy-done.24) | copy-start | bytes 786436
  130.3 8.4 collective-permute-start.12
  130.3 8.4 collective-permute-start.13
  146.9 3.5 copy-start.38
  146.9 3.7 copy-start.40
  148.9 4.1 copy-start.10
  149.0 4.1 copy-start.34
  150.4 3.4 copy-start.36
  150.4 4.2 copy-start.23
  157.0 161.9 %reduce-scatter.15.cloned.1.call-start = ((), (), s32[]{:S(2)}) async-start(), calls=%async_computation.11 | async-start | bytes 73728 | tf_op jit(solution)/shard_map/reduce_scatter | solution.py:148
  161.9 222.3 %reduce-scatter.23.cloned.1.call-start = ((), (), s32[]{:S(2)}) async-start(), calls=%async_computation.15 | async-start | bytes 36864 | tf_op jit(solution)/shard_map/reduce_scatter | solution.py:151
  167.6 289.4 %reduce-scatter.13.cloned.1.call-start = ((), (), s32[]{:S(2)}) async-start(), calls=%async_computation.10 | async-start | bytes 73728 | tf_op jit(solution)/shard_map/reduce_scatter | solution.py:148
  170.0 351.5 %reduce-scatter.21.cloned.1.call-start = ((), (), s32[]{:S(2)}) async-start(), calls=%async_computation.14 | async-start | bytes 36864 | tf_op jit(solution)/shard_map/reduce_scatter | solution.py:151
  171.9 4.5 copy-start.11
  172.0 422.3 %reduce-scatter.11.cloned.1.call-start = ((), (), s32[]{:S(2)}) async-start(), calls=%async_computation.9 | async-start | bytes 73728 | tf_op jit(solution)/shard_map/reduce_scatter | solution.py:148
  174.5 484.5 %reduce-scatter.19.cloned.1.call-start = ((), (), s32[]{:S(2)}) async-start(), calls=%async_computation.13 | async-start | bytes 36864 | tf_op jit(solution)/shard_map/reduce_scatter | solution.py:151
  176.4 7.8 copy-start.80
  176.4 555.4 %reduce-scatter.9.cloned.1.call-start = ((), (), s32[]{:S(2)}) async-start(), calls=%async_computation.8 | async-start | bytes 73728 | tf_op jit(solution)/shard_map/reduce_scatter | solution.py:148
  178.7 6.7 collective-permute-start.14
  178.8 6.6 collective-permute-start.15
  184.1 613.0 %reduce-scatter.17.cloned.1.call-start = ((), (), s32[]{:S(2)}) async-start(), calls=%async_computation.12 | async-start | bytes 36864 | tf_op jit(solution)/shard_map/reduce_scatter | solution.py:151
  185.1 729.2 %all-reduce.17.cloned.1.call-start = ((), (), s32[]{:S(2)}) async-start(), calls=%async_computation.16 | async-start | bytes 180224 | tf_op jit(solution)/shard_map/psum | solution.py:140
  189.6 607.6 %copy-start.64 = (bf16[8,8,8,256]{3,2,1,0:T(8,128)(2,1)S(1)}, bf16[8,8,8,256]{3,2,1,0:T(8,128)(2,1)}, u32[]{:S(2)}) copy-start(bf16[8,8,8,256]{3,2,1,0:T(8,128)(2,1)} %copy.48) | copy-start | bytes 786436
  189.6 607.6 %copy-start.94 = (bf16[64,8,256]{2,1,0:T(8,128)(2,1)S(1)}, bf16[64,8,256]{2,1,0:T(8,128)(2,1)}, u32[]{:S(2)}) copy-start(bf16[64,8,256]{2,1,0:T(8,128)(2,1)} %rev.13) | copy-start | bytes 786436
  (65 other events, 113.9 us)
Sparse Core Ops, SparseCore 0:
  157.2 85.8 all-reduce.18
  247.6 71.3 reduce-scatter.14
  323.2 60.9 reduce-scatter.22
  388.0 68.9 reduce-scatter.12
  460.5 60.9 reduce-scatter.20
  525.3 68.9 reduce-scatter.10
  597.9 60.9 reduce-scatter.18
  662.9 68.9 reduce-scatter.8
  736.1 61.0 reduce-scatter.16
  801.5 112.7 all-reduce.16
where the time goes:
time: 935 us; the launch traced here: 925 us
  waiting for transfers between devices  733 us (78%)
  matrix products  80.2 us (9%)
  local copies, waits for them, and re-layouts  37.5 us (4%)
  starting transfers between devices  30.9 us (3%)
  other arithmetic  26.3 us (3%)
  between operations  18.1 us (2%)
    reduce_scatter x4, waiting for transfers between devices, share_grads(): lax.psum_scatter(summed[1].astype(jnp.bfloat16), 'ens', scatter_dimension...  291 us
    reduce_scatter x4, waiting for transfers between devices, share_grads(): lax.psum_scatter(summed[2].astype(jnp.bfloat16), 'ens', scatter_dimension...  260 us
    psum x1, waiting for transfers between devices, share_grads(): lax.psum(grads[0].astype(jnp.bfloat16), 'lon').astype(jnp.float32)  116 us
    unnamed x11, waiting for transfers between devices  52.7 us
    dot_general x44, matrix products, outer_sum(): lax.dot_general(left, right, (((1,), (1,)), ((), ())), preferred_element_...  36 us
    ppermute x8, starting transfers between devices, extended(): lax.ppermute(lax.slice_in_dim(block, 0, width, axis=dim), axis, backward)  27.4 us
    concatenate x16, other arithmetic, extended(): block = jnp.concatenate([low, block, high], axis=dim)  19 us
  transfers between devices with their start and end apart: 26, of which 18 were waited for; matrix products, arithmetic and copies ran while one was open for 4% of the time, Pallas kernels for 0%

commit v1 on v0

v1 whole, which is shorter than its diff:
```python
import functools

import jax
import jax.numpy as jnp
from jax import lax
from jax.experimental import pallas as pl
from jax.experimental.pallas import tpu as pltpu
from jax.sharding import PartitionSpec as P

BF = jnp.bfloat16
F32 = jnp.float32
SQRT_HALF = 0.7071067811865476
INV_ROOT_TAU = 0.3989422804014327

C = 64
HID = 256
H = 8
WD = 256
HALO = 8
PITCH = WD + 2 * HALO
N = H * PITCH
DEPTH = 4
HALVES = WD // 128
SHARE = 40
CHUNKS = [(s, min(256, N - s)) for s in range(0, N, 256)]
VMEM = 56 * 1024 * 1024

NT = (((1,), (1,)), ((), ()))


def mm(a, b):
    return jnp.dot(a, b, preferred_element_type=F32)


def mm_nt(a, b):
    return lax.dot_general(a, b, NT, preferred_element_type=F32)


def call(body, outs, scratch=(), smem=0, total=0, flops=0, **kw):
    specs = [pl.BlockSpec(memory_space=pltpu.SMEM)] * smem
    specs += [pl.BlockSpec(memory_space=pltpu.VMEM)] * (total - smem)
    return pl.pallas_call(
        body,
        out_shape=outs,
        in_specs=specs,
        out_specs=jax.tree.map(lambda _: pl.BlockSpec(memory_space=pltpu.VMEM), outs),
        scratch_shapes=list(scratch),
        compiler_params=pltpu.CompilerParams(vmem_limit_bytes=VMEM),
        cost_estimate=pl.CostEstimate(flops=flops, bytes_accessed=1 << 20, transcendentals=0),
        **kw,
    )


def shape(*dims, dtype=BF):
    return jax.ShapeDtypeStruct(dims, dtype)


def spread(wide, ref):
    for half in range(HALVES):
        part = ref[:, :, 128 * half : 128 * half + 128]
        wide[half] = part.astype(F32).reshape(C * H, 128)


def edge_kernel(flip_ref, field_ref, slope_ref, low_ref, high_ref, wide_f, wide_g):
    flip = flip_ref[0]
    spread(wide_f, field_ref)
    spread(wide_g, slope_ref)
    lane = lax.broadcasted_iota(jnp.int32, (C, 128), 1)
    low = jnp.zeros((C, 128), F32)
    high = jnp.zeros((C, 128), F32)
    for row in range(H):
        stored = jnp.where(flip == 1, H - 1 - row, row)
        for k, wide in ((0, wide_f), (8, wide_g)):
            at = 16 * row + k
            inside = (lane >= at) & (lane < at + 8)
            first = wide[0, pl.ds(stored, C, stride=H), :]
            last = wide[HALVES - 1, pl.ds(stored, C, stride=H), :]
            low = jnp.where(inside, pltpu.roll(first, at, axis=1), low)
            high = jnp.where(inside, pltpu.roll(last, (at + 8) % 128, axis=1), high)
    low_ref[...] = low.astype(BF)
    high_ref[...] = high.astype(BF)


def flatten(ref, left, right, k, wide, flip):
    spread(wide, ref)
    parts = []
    for row in range(H):
        stored = jnp.where(flip == 1, H - 1 - row, row)
        at = 16 * row + k
        parts.append(left[:, at : at + 8])
        for half in range(HALVES):
            parts.append(wide[half, pl.ds(stored, C, stride=H), :])
        parts.append(right[:, at : at + 8])
    return jnp.concatenate(parts, axis=1)


def unflatten(flat, ref, wide, flip):
    for row in range(H):
        stored = jnp.where(flip == 1, H - 1 - row, row)
        for half in range(HALVES):
            at = row * PITCH + HALO + 128 * half
            wide[half, pl.ds(stored, C, stride=H), :] = flat[:, at : at + 128]
    for half in range(HALVES):
        ref[:, :, 128 * half : 128 * half + 128] = wide[half].reshape(C, H, 128).astype(BF)


def shift(flat, amount):
    return pltpu.roll(flat, amount % N, axis=1)


def rows_stack(dst, value, lane, sign):
    before = jnp.where(lane < PITCH, 0, shift(value, PITCH)).astype(BF)
    after = jnp.where(lane >= N - PITCH, 0, shift(value, -PITCH)).astype(BF)
    first, last = (before, after) if sign > 0 else (after, before)
    dst[0:C, :] = first
    dst[C : 2 * C, :] = value
    dst[2 * C : 3 * C, :] = last


def main_kernel(
    flip_ref,
    field_ref,
    slope_ref,
    left_ref,
    right_ref,
    conv_ref,
    convt_ref,
    expand_ref,
    expandt_ref,
    bias_ref,
    project_ref,
    projectt_ref,
    out_ref,
    grad_ref,
    share_ref,
    wide,
    stack_s,
    hid_s,
    wide_s,
    up_s,
    dh_s,
    rstack_s,
    share_s,
):
    flip = flip_ref[0]
    lane = lax.broadcasted_iota(jnp.int32, (C, N), 1)
    column = lane
    for row in range(1, H):
        column = jnp.where(lane >= row * PITCH, lane - row * PITCH, column)
    inside = (column >= HALO) & (column < HALO + WD)
    mask = jnp.where(inside, 1.0, 0.0).astype(BF)
    left = left_ref[...].astype(F32)
    right = right_ref[...].astype(F32)

    field = flatten(field_ref, left, right, 0, wide, flip).astype(BF)
    for b in range(DEPTH):
        rows_stack(stack_s.at[b], field, lane, 1)
        for start, size in CHUNKS:
            cut = slice(start, start + size)
            wide_s[:, cut] = mm(conv_ref[b], stack_s[b, :, cut])
        hid_s[b] = (
            shift(wide_s[0:C, :], 1) + wide_s[C : 2 * C, :] + shift(wide_s[2 * C : 3 * C, :], -1)
        ).astype(BF)
        parts = []
        for start, size in CHUNKS:
            cut = slice(start, start + size)
            inner = mm(expand_ref[b], hid_s[b, :, cut]) + bias_ref[b]
            active = (0.5 * inner * (1.0 + lax.erf(inner * SQRT_HALF))).astype(BF)
            old = stack_s[b, C : 2 * C, cut].astype(F32)
            parts.append((old + mm(project_ref[b], active)).astype(BF))
        field = jnp.concatenate(parts, axis=1)
    unflatten(field.astype(F32), out_ref, wide, flip)

    up_s[...] = flatten(slope_ref, left, right, 8, wide, flip).astype(BF)
    for b in reversed(range(DEPTH)):
        pg = jnp.zeros((C, HID), F32)
        eg = jnp.zeros((HID, C), F32)
        for start, size in CHUNKS:
            cut = slice(start, start + size)
            up = up_s[:, cut]
            hidden = hid_s[b, :, cut]
            d_active = mm(projectt_ref[b], up)
            inner = mm(expand_ref[b], hidden) + bias_ref[b]
            half = 0.5 * (1.0 + lax.erf(inner * SQRT_HALF))
            active = (inner * half).astype(BF)
            slope = half + inner * (INV_ROOT_TAU * jnp.exp(-0.5 * inner * inner))
            d_inner = (d_active * slope).astype(BF)
            dh_s[:, cut] = mm(expandt_ref[b], d_inner).astype(BF)
            pg = pg + mm_nt(up * mask[:, cut], active)
            eg = eg + mm_nt(d_inner, hidden * mask[:, cut])
        d_hidden = dh_s[...]
        rows_stack(rstack_s, d_hidden, lane, -1)
        for start, size in CHUNKS:
            cut = slice(start, start + size)
            wide_s[:, cut] = mm(convt_ref[b], rstack_s[:, cut])
        up_s[...] = (
            up_s[...].astype(F32)
            + (shift(wide_s[0:C, :], -1) + wide_s[C : 2 * C, :] + shift(wide_s[2 * C : 3 * C, :], 1))
        ).astype(BF)
        own = d_hidden * mask
        rstack_s[0:C, :] = shift(own, -1)
        rstack_s[C : 2 * C, :] = own
        rstack_s[2 * C : 3 * C, :] = shift(own, 1)
        cg = mm_nt(rstack_s[...], stack_s[b])
        for e in range(8):
            low = [cg[c * C + 8 * e : c * C + 8 * e + 8, :] for c in range(3)]
            low.append(jnp.zeros((8, 3 * C), F32))
            share_s[e, 0:32, :] = jnp.concatenate(
                [jnp.concatenate(low, axis=0), eg[32 * e : 32 * e + 32, :]], axis=1
            )
            share_s[e, 32:40, :] = pg[8 * e : 8 * e + 8, :]
        share_ref[b] = share_s[...].reshape(8 * SHARE, 256).astype(BF)
    unflatten(up_s[...].astype(F32), grad_ref, wide, flip)


def sum_kernel(parts, rows, src_ref, dst_ref):
    total = src_ref[0].astype(F32)
    for part in range(1, parts):
        total = total + src_ref[part].astype(F32)
    dst_ref[...] = total.astype(dst_ref.dtype)


def unpack_kernel(src_ref, conv_ref, expand_ref, project_ref):
    for b in range(DEPTH):
        total = src_ref[0, b].astype(F32)
        for part in range(1, src_ref.shape[0]):
            total = total + src_ref[part, b].astype(F32)
        pieces = []
        for r in range(3):
            for c in range(3):
                pieces.append(total[8 * c : 8 * c + 8, C * r : C * r + C])
        conv_ref[b] = jnp.concatenate(pieces, axis=1)
        expand_ref[b] = total[0:32, 3 * C : 4 * C]
        project_ref[b] = total[32:40, :]


def local(members_in, cotangent, conv_weight, expand_weight, expand_bias, project_weight, orient):
    count = lax.axis_size("lon")
    sector = lax.axis_index("lon")
    sectors = jnp.arange(orient.shape[0], dtype=jnp.int32)
    flip = jnp.sum(jnp.where(sectors == sector, orient, 0)).reshape(1)
    field = members_in[0]
    slope = cotangent[0]
    low, high = call(
        edge_kernel,
        [shape(C, 128)] * 2,
        [pltpu.VMEM((HALVES, C * H, 128), F32)] * 2,
        smem=1,
        total=3,
    )(flip, field, slope)
    forward = [(i, (i + 1) % count) for i in range(count)]
    backward = [((i + 1) % count, i) for i in range(count)]
    left = lax.ppermute(high, "lon", forward)
    right = lax.ppermute(low, "lon", backward)

    kernels = conv_weight.reshape(DEPTH, C, 3, 3, C)
    conv = kernels.transpose(0, 3, 1, 2, 4).reshape(DEPTH, 3 * C, 3 * C)
    convt = kernels.transpose(0, 3, 4, 2, 1).reshape(DEPTH, 3 * C, 3 * C)
    section_out, input_grad, shares = call(
        main_kernel,
        [shape(C, H, WD), shape(C, H, WD), shape(DEPTH, 8 * SHARE, 256)],
        [
            pltpu.VMEM((HALVES, C * H, 128), F32),
            pltpu.VMEM((DEPTH, 3 * C, N), BF),
            pltpu.VMEM((DEPTH, C, N), BF),
            pltpu.VMEM((3 * C, N), F32),
            pltpu.VMEM((C, N), BF),
            pltpu.VMEM((C, N), BF),
            pltpu.VMEM((3 * C, N), BF),
            pltpu.VMEM((8, SHARE, 256), F32),
        ],
        smem=1,
        total=12,
    )(
        flip,
        field,
        slope,
        left,
        right,
        conv,
        convt,
        expand_weight,
        expand_weight.transpose(0, 2, 1),
        expand_bias[:, :, None],
        project_weight,
        project_weight.transpose(0, 2, 1),
    )
    parts = shares.reshape(DEPTH, 8, SHARE, 256).transpose(1, 0, 2, 3)
    parts = lax.all_to_all(parts, "ens", 0, 0, tiled=True)
    parts = call(functools.partial(sum_kernel, 8, SHARE), shape(DEPTH, SHARE, 256), total=1)(parts)
    parts = jnp.broadcast_to(parts[None], (count, DEPTH, SHARE, 256))
    parts = lax.all_to_all(parts, "lon", 0, 0, tiled=True)
    conv_grad, expand_grad, project_grad = call(
        unpack_kernel,
        [
            shape(DEPTH, 8, 9 * C, dtype=F32),
            shape(DEPTH, 32, C, dtype=F32),
            shape(DEPTH, 8, HID, dtype=F32),
        ],
        total=1,
    )(parts)
    return section_out[None], input_grad[None], conv_grad, expand_grad, project_grad


def solution(mesh):
    cells = P("ens", None, None, "lon")
    rows = P(None, "ens", None)
    return jax.shard_map(
        local,
        mesh=mesh,
        in_specs=(cells, cells, P(), P(), P(), P(), P()),
        out_specs=(cells, cells, rows, rows, rows),
        check_vma=False,
    )
```

time: 935 us -> 96.5 us (0.10)
  waiting for transfers between devices: 733 us -> 0.01 us
  matrix products: 80.2 us -> 0 us
  blocking collectives: 0 us -> 44.3 us
  Pallas kernels: 0 us -> 35.8 us
  starting transfers between devices: 30.9 us -> 2.6 us
  local copies, waits for them, and re-layouts: 37.5 us -> 11.3 us
  other arithmetic: 26.3 us -> 1.34 us
  between operations: 18.1 us -> 0.71 us
    reduce_scatter x8 -> x0, waiting for transfers between devices: 551 us -> none  [the longest x4 291 us: share_grads(): lax.psum_scatter(summed[1].astype(jnp.bfloat16), 'ens', scatter_dimension...]
    psum x1 -> x0, waiting for transfers between devices: 116 us -> none  [share_grads(): lax.psum(grads[0].astype(jnp.bfloat16), 'lon').astype(jnp.float32)]
    dot_general x132 -> x0, matrix products: 80.2 us -> none  [the longest x44 36 us: outer_sum(): lax.dot_general(left, right, (((1,), (1,)), ((), ())), preferred_element_...]
    unnamed x11 -> x0, waiting for transfers between devices: 52.7 us -> none
    all_to_all x0 -> x2, blocking collectives: none -> 44.3 us  [the longest x1 27.3 us: local(): parts = lax.all_to_all(parts, 'lon', 0, 0, tiled=True)]
    pallas_call x0 -> x4, Pallas kernels: none -> 35.8 us  [the longest x1 29.1 us: local(): call(main_kernel, [shape(C, H, WD), shape(C, H, WD), shape(DEPTH, 8 * SHA...]
    ppermute x16 -> x2, starting transfers between devices: 30.3 us -> 2.6 us  [the longest x1 2.6 us: local(): left = lax.ppermute(high, 'lon', forward)]
    concatenate x16 -> x0, other arithmetic: 19 us -> none  [extended(): block = jnp.concatenate([low, block, high], axis=dim)]
  transfers between devices with their start and end apart: 26 -> 2, of which waited for: 18 -> 0; matrix products, arithmetic and copies ran while one was open for 4% -> 9% of each run, Pallas kernels for 0% -> 0%
where the time goes in v1:
time: 96.5 us; the launch traced here: 96 us
  blocking collectives  44.3 us (46%)
  Pallas kernels  35.8 us (37%)
  local copies, waits for them, and re-layouts  11.3 us (12%)
  starting transfers between devices  2.6 us (3%)
  other arithmetic  1.34 us (1%)
    pallas_call x1, Pallas kernels, local(): call(main_kernel, [shape(C, H, WD), shape(C, H, WD), shape(DEPTH, 8 * SHA...  29.1 us
    all_to_all x1, blocking collectives, local(): parts = lax.all_to_all(parts, 'lon', 0, 0, tiled=True)  27.3 us
    all_to_all x1, blocking collectives, local(): parts = lax.all_to_all(parts, 'ens', 0, 0, tiled=True)  17 us
    unnamed x11, local copies, waits for them, and re-layouts  4.42 us
    pallas_call x1, Pallas kernels, local(): call(edge_kernel, [shape(C, 128)] * 2, [pltpu.VMEM((HALVES, C * H, 128),...  2.7 us
    ppermute x1, starting transfers between devices, local(): left = lax.ppermute(high, 'lon', forward)  2.6 us
    pallas_call x1, Pallas kernels, local(): call(unpack_kernel, [shape(DEPTH, 8, 9 * C, dtype=F32), shape(DEPTH, 32,...  2.14 us
  transfers between devices with their start and end apart: 2, of which 0 were waited for; matrix products, arithmetic and copies ran while one was open for 9% of the time, Pallas kernels for 0%

profile of v1, /device:TPU:1, one launch (start us, length us, event | category | flops | bytes accessed | tf_op | source)
XLA Modules:
  0.0 96.0 jit_solution(17048762023438911711)
XLA Ops:
  0.6 0.0 copy-start.3
  0.6 0.0 copy-start
  0.7 1.3 %fusion = s32[]{:T(128)} fusion(s32[16]{0:T(128)} %param.13, s32[]{:T(128)S(6)} %axis_index.15), kind=kLoop, calls=%fused_computation.2 | loop fusion | flops 47 | bytes 72 | tf_op jit(solution)/shard_map/reduce_sum | solution.py:241
  2.0 2.7 %shard_map.110 = (bf16[64,128]{1,0:T(8,128)(2,1)}, bf16[64,128]{1,0:T(8,128)(2,1)}) custom-call(s32[1]{0:T(128)} %bitcast.flip_ref, bf16[64,8,256]{2,1,0:T(8,128)(2,1)} %bitcast.20, bf16[64,8,256]{2,1,0:T(8,128)(2,1)} %bitcast.22), custom_call_target="tpu_custom_call" | custom-call | bytes 1048576 | tf_op jit(solution)/shard_map/pallas_call | solution.py:244
  4.7 2.6 %collective-permute-start = (bf16[64,128]{1,0:T(8,128)(2,1)}, bf16[64,128]{1,0:T(8,128)(2,1)S(1)}, u32[]{:S(2)}, u32[]{:S(2)}) collective-permute-start(bf16[64,128]{1,0:T(8,128)(2,1)} %get-tuple-element.13), channel_id=1, source_target_pairs={{0,8},{8,16},{16,24},{24,32},{32,40},{40,48},{48,56},{56,64},{64,7... | collective-permute-start | bytes 49160 | tf_op jit(solution)/shard_map/ppermute | solution.py:253
  7.3 0.0 collective-permute-start.1
  7.3 1.8 %copy.20.expand_ref = bf16[4,256,64]{2,1,0:T(8,128)(2,1)} copy(bf16[4,256,64]{1,2,0:T(8,128)(2,1)} %param.10) | data formatting | bytes 262144 | tf_op args[3]
  9.1 1.8 %copy.19 = bf16[4,64,256]{1,2,0:T(8,128)(2,1)} copy(bf16[4,64,256]{2,1,0:T(8,128)(2,1)} %project_ref.1) | data formatting | bytes 262144 | tf_op args[5]
  10.8 0.0 copy-done.3
  10.8 1.0 %copy.21.bias_ref = f32[4,256,1]{2,1,0:T(8,128)} copy(f32[4,256,1]{1,0,2:T(4,128)S(1)} %bitcast.27) | data formatting | bytes 8192 | tf_op jit(solution)/shard_map/broadcast_in_dim | solution.py:284
  11.9 0.0 copy-done
  11.9 0.3 copy.16
  12.2 0.5 copy.18
  12.7 1.2 %reshape.29.convt_ref = bf16[4,192,192]{2,1,0:T(8,128)(2,1)} reshape(bf16[4,3,64,3,64]{4,3,2,1,0:T(4,128)(2,1)S(1)} %copy.18) | data formatting | bytes 589824 | tf_op jit(solution)/shard_map/reshape | solution.py:258
  13.9 0.8 copy.17
  14.7 1.2 %reshape.28.conv_ref = bf16[4,192,192]{2,1,0:T(8,128)(2,1)} reshape(bf16[4,3,64,3,64]{4,3,2,1,0:T(4,128)(2,1)S(1)} %copy.17) | data formatting | bytes 589824 | tf_op jit(solution)/shard_map/reshape | solution.py:257
  15.9 0.0 collective-permute-done.left_ref
  15.9 0.0 copy-start.1
  15.9 0.0 collective-permute-done.1.right_ref
  15.9 0.0 copy-start.2
  15.9 0.6 copy-done.1
  16.5 0.0 copy-done.2
  16.5 29.1 %shard_map.111 = (bf16[64,8,256]{2,1,0:T(8,128)(2,1)}, bf16[64,8,256]{2,1,0:T(8,128)(2,1)}, bf16[4,320,256]{2,1,0:T(8,128)(2,1)}) custom-call(s32[1]{0:T(128)} %bitcast.flip_ref, bf16[64,8,256]{2,1,0:T(8,128)(2,1)} %bitcast.21, bf16[64,8,256]{2,1,0:T(8,128)(2,1)} %bitcast.23, bf16[64,128]{1,0:T(8,128)(2,1)} %copy-done.1, bf16[64,128]{1,0:T(8,128)(2,1)} %copy-done.2, ...), custom_call_target="tpu_custom_call" | custom-call | bytes 1048576 | tf_op jit(solution)/shard_map/pallas_call | solution.py:259
  45.6 1.1 %copy.24 = bf16[4,8,40,256]{3,2,0,1:T(8,128)(2,1)S(1)} copy(bf16[4,8,40,256]{3,2,1,0:T(8,128)(2,1)} %bitcast.25) | data formatting | bytes 1310720 | tf_op jit(solution)/shard_map/reshape | solution.py:288
  46.8 17.0 %all_to_all.10.src_ref = bf16[8,4,40,256]{3,2,1,0:T(8,128)(2,1)} all-to-all(bf16[8,4,40,256]{3,2,1,0:T(8,128)(2,1)S(1)} %bitcast.19), channel_id=1, replica_groups=mesh['lon'=16,'ens'=8] {'ens'}, dimensions={0} | all-to-all | bytes 1310720 | tf_op jit(solution)/shard_map/all_to_all | solution.py:289
  63.7 1.8 %shard_map.112 = bf16[4,40,256]{2,1,0:T(8,128)(2,1)} custom-call(bf16[8,4,40,256]{3,2,1,0:T(8,128)(2,1)} %all_to_all.10.src_ref), custom_call_target="tpu_custom_call" | custom-call | bytes 1048576 | tf_op jit(solution)/shard_map/pallas_call | solution.py:290
  65.5 1.0 %broadcast_in_dim.23 = bf16[16,4,40,256]{3,2,1,0:T(8,128)(2,1)S(1)} broadcast(bf16[4,40,256]{2,1,0:T(8,128)(2,1)} %shard_map.112), dimensions={1,2,3} | broadcast | bytes 1392640 | tf_op jit(solution)/shard_map/broadcast_in_dim | solution.py:291
  66.6 27.3 %all_to_all.11.src_ref = bf16[16,4,40,256]{3,2,1,0:T(8,128)(2,1)} all-to-all(bf16[16,4,40,256]{3,2,1,0:T(8,128)(2,1)S(1)} %broadcast_in_dim.23), channel_id=1, replica_groups=mesh['lon'=16,'ens'=8] {'lon'}, dimensions={0} | all-to-all | bytes 2621440 | tf_op jit(solution)/shard_map/all_to_all | solution.py:292
  93.9 2.1 %shard_map.113 = (f32[4,8,576]{2,1,0:T(8,128)}, f32[4,32,64]{2,1,0:T(8,128)}, f32[4,8,256]{2,1,0:T(8,128)}) custom-call(bf16[16,4,40,256]{3,2,1,0:T(8,128)(2,1)} %all_to_all.11.src_ref), custom_call_target="tpu_custom_call" | custom-call | bytes 1048576 | tf_op jit(solution)/shard_map/pallas_call | solution.py:293
Async XLA Ops:
  0.6 10.2 %copy-start.3 = (f32[4,256]{1,0:T(4,128)S(1)}, f32[4,256]{1,0:T(4,128)}, u32[]{:S(2)}) copy-start(f32[4,256]{1,0:T(4,128)} %param.11) | copy-start | bytes 12292
  0.6 11.2 %copy-start = (bf16[4,64,576]{2,1,0:T(8,128)(2,1)S(1)}, bf16[4,64,576]{2,1,0:T(8,128)(2,1)}, u32[]{:S(2)}) copy-start(bf16[4,64,576]{2,1,0:T(8,128)(2,1)} %param.9) | copy-start | bytes 884740
  4.7 11.2 %collective-permute-start = (bf16[64,128]{1,0:T(8,128)(2,1)}, bf16[64,128]{1,0:T(8,128)(2,1)S(1)}, u32[]{:S(2)}, u32[]{:S(2)}) collective-permute-start(bf16[64,128]{1,0:T(8,128)(2,1)} %get-tuple-element.13), channel_id=1, source_target_pairs={{0,8},{8,16},{16,24},{24,32},{32,40},{40,48},{48,56},{56,64},{64,7... | collective-permute-start | bytes 49160 | tf_op jit(solution)/shard_map/ppermute | solution.py:253
  7.3 8.6 %collective-permute-start.1 = (bf16[64,128]{1,0:T(8,128)(2,1)}, bf16[64,128]{1,0:T(8,128)(2,1)S(1)}, u32[]{:S(2)}, u32[]{:S(2)}) collective-permute-start(bf16[64,128]{1,0:T(8,128)(2,1)} %get-tuple-element.14), channel_id=1, source_target_pairs={{8,0},{16,8},{24,16},{32,24},{40,32},{48,40},{56,48},{64,56},{72,6... | collective-permute-start | bytes 49160 | tf_op jit(solution)/shard_map/ppermute | solution.py:254
  15.9 0.6 copy-start.1
  15.9 0.6 copy-start.2

commit v2 on v1

v2 whole, which is shorter than its diff:
```python
import jax
import jax.numpy as jnp
from jax import lax
from jax.experimental import pallas as pl
from jax.experimental.pallas import tpu as pltpu
from jax.sharding import Mesh
from jax.sharding import PartitionSpec as P

BF = jnp.bfloat16
F32 = jnp.float32
SQRT_HALF = 0.7071067811865476
INV_ROOT_TAU = 0.3989422804014327
HALF_LOG2E = 0.7213475204444817

C = 64
HID = 256
H = 8
WD = 256
HALO = 8
PITCH = WD + 2 * HALO
N = H * PITCH
DEPTH = 4
HALVES = WD // 128
TILES = N // 128
UNITS = 72
CHUNKS = [(s, min(256, N - s)) for s in range(0, N, 256)]
VMEM = 56 * 1024 * 1024
LON = ("y", "xl", "core")

NT = (((1,), (1,)), ((), ()))


def mm(a, b):
    return jnp.dot(a, b, preferred_element_type=F32)


def mm_nt(a, b):
    return lax.dot_general(a, b, NT, preferred_element_type=F32)


def call(body, outs, ins, scratch=(), flops=0):
    specs = [
        pl.BlockSpec(memory_space=pltpu.SMEM if scalar else pltpu.VMEM) for _, scalar in ins
    ]
    return pl.pallas_call(
        body,
        out_shape=outs,
        in_specs=specs,
        out_specs=jax.tree.map(lambda _: pl.BlockSpec(memory_space=pltpu.VMEM), outs),
        scratch_shapes=list(scratch),
        compiler_params=pltpu.CompilerParams(vmem_limit_bytes=VMEM),
        cost_estimate=pl.CostEstimate(flops=flops, bytes_accessed=1 << 20, transcendentals=0),
    )(*[array for array, _ in ins])


def shape(*dims, dtype=BF):
    return jax.ShapeDtypeStruct(dims, dtype)


def spread(wide, ref):
    for half in range(HALVES):
        part = ref[:, :, 128 * half : 128 * half + 128]
        wide[half] = part.astype(F32).reshape(C * H, 128)


def stored_row(flip, row):
    return jnp.where(flip == 1, H - 1 - row, row)


def edge_kernel(place_ref, field_ref, slope_ref, low_ref, high_ref, wide_f, wide_g):
    flip = place_ref[0]
    spread(wide_f, field_ref)
    spread(wide_g, slope_ref)
    lane = lax.broadcasted_iota(jnp.int32, (C, 128), 1)
    low = jnp.zeros((C, 128), F32)
    high = jnp.zeros((C, 128), F32)
    for row in range(H):
        stored = stored_row(flip, row)
        for k, wide in ((0, wide_f), (8, wide_g)):
            at = 16 * row + k
            inside = (lane >= at) & (lane < at + 8)
            first = wide[0, pl.ds(stored, C, stride=H), :]
            last = wide[HALVES - 1, pl.ds(stored, C, stride=H), :]
            low = jnp.where(inside, pltpu.roll(first, at, axis=1), low)
            high = jnp.where(inside, pltpu.roll(last, (at + 8) % 128, axis=1), high)
    low_ref[...] = low.astype(BF)
    high_ref[...] = high.astype(BF)


def flatten(ref, wide, flip):
    spread(wide, ref)
    edge = jnp.zeros((C, HALO), F32)
    parts = []
    for row in range(H):
        stored = stored_row(flip, row)
        parts.append(edge)
        for half in range(HALVES):
            parts.append(wide[half, pl.ds(stored, C, stride=H), :])
        parts.append(edge)
    return jnp.concatenate(parts, axis=1)


def unflatten(flat_ref, ref, wide, flip):
    for row in range(H):
        stored = stored_row(flip, row)
        for half in range(HALVES):
            at = row * PITCH + HALO + 128 * half
            wide[half, pl.ds(stored, C, stride=H), :] = flat_ref[:, at : at + 128].astype(F32)
    for half in range(HALVES):
        ref[:, :, 128 * half : 128 * half + 128] = wide[half].reshape(C, H, 128).astype(BF)


def prep_kernel(
    place_ref,
    field_ref,
    slope_ref,
    kernel_ref,
    expandt_ref,
    bias_ref,
    project_ref,
    field_out,
    slope_out,
    conv_out,
    convt_out,
    expand_out,
    projectt_out,
    bias_out,
    wide,
):
    flip = place_ref[0]
    field_out[...] = flatten(field_ref, wide, flip).astype(BF)
    slope_out[...] = flatten(slope_ref, wide, flip).astype(BF)
    for b in range(DEPTH):
        taps = kernel_ref[b]
        turned = taps.astype(F32).T
        for c in range(3):
            here = slice(c * C, c * C + C)
            at = [(3 * r + c) * C for r in range(3)]
            conv_out[b, here, :] = jnp.concatenate([taps[:, a : a + C] for a in at], axis=1)
            convt_out[b, here, :] = jnp.concatenate(
                [turned[a : a + C, :] for a in at], axis=1
            ).astype(BF)
        expand_out[b] = expandt_ref[b].astype(F32).T.astype(BF)
        projectt_out[b] = project_ref[b].astype(F32).T.astype(BF)
        bias_out[b] = jnp.broadcast_to(bias_ref[b : b + 1, :], (128, HID)).T


def add_halo(flat_ref, left, right):
    lane = lax.broadcasted_iota(jnp.int32, (C, 128), 1)
    for j in range(H + 1):
        cut = slice(256 * j, 256 * j + 128)
        tile = flat_ref[:, cut].astype(F32)
        tile = jnp.where((lane >= 16 * j) & (lane < 16 * j + 8), left, tile)
        tile = jnp.where((lane >= 16 * j - 8) & (lane < 16 * j), right, tile)
        flat_ref[:, cut] = tile.astype(BF)


def shift(flat, amount):
    return pltpu.roll(flat, amount % N, axis=1)


def rows_stack(dst, value, lane, sign):
    before = jnp.where(lane < PITCH, 0, shift(value, PITCH)).astype(BF)
    after = jnp.where(lane >= N - PITCH, 0, shift(value, -PITCH)).astype(BF)
    first, last = (before, after) if sign > 0 else (after, before)
    dst[0:C, :] = first
    dst[C : 2 * C, :] = value
    dst[2 * C : 3 * C, :] = last


def conv_pass(dst, weights, src):
    for start, size in CHUNKS:
        cut = slice(start, start + size)
        dst[:, cut] = mm(weights, src[:, cut])


def pack_share(dst, at, cg, eg, pg):
    blank = jnp.zeros((8, C), F32)
    for e in range(8):
        conv = [cg[c * C + 8 * e : c * C + 8 * e + 8, :] for c in range(3)]
        wide = [eg[32 * e + 8 * i : 32 * e + 8 * i + 8, :] for i in range(4)]
        tail = [conv[i][:, 128:192] for i in range(3)] + wide + [blank]
        units = [conv[i][:, 0:128] for i in range(3)]
        units += [pg[8 * e : 8 * e + 8, 0:128], pg[8 * e : 8 * e + 8, 128:256]]
        units += [jnp.concatenate(tail[2 * i : 2 * i + 2], axis=1) for i in range(4)]
        for i, unit in enumerate(units):
            dst[at, e, 8 * i : 8 * i + 8, :] = unit


def main_kernel(
    place_ref,
    field_ref,
    slope_ref,
    left_ref,
    right_ref,
    conv_ref,
    convt_ref,
    expand_ref,
    expandt_ref,
    bias_ref,
    project_ref,
    projectt_ref,
    out_ref,
    up_ref,
    dh_ref,
    own_ref,
    other_ref,
    stack_s,
    hid_s,
    active_s,
    slope_s,
    wide_s,
    rstack_s,
    share_s,
):
    core = place_ref[1]
    lane = lax.broadcasted_iota(jnp.int32, (C, N), 1)
    column = lane
    for row in range(1, H):
        column = jnp.where(lane >= row * PITCH, lane - row * PITCH, column)
    inside = (column >= HALO) & (column < HALO + WD)
    mask = jnp.where(inside, 1.0, 0.0).astype(BF)

    left = left_ref[...].astype(F32)
    right = right_ref[...].astype(F32)
    out_ref[...] = field_ref[...]
    add_halo(out_ref, left, pltpu.roll(right, 8, axis=1))
    up_ref[...] = slope_ref[...]
    add_halo(up_ref, pltpu.roll(left, 120, axis=1), right)

    for b in range(DEPTH):
        rows_stack(stack_s.at[b], out_ref[...], lane, 1)
        conv_pass(wide_s, conv_ref[b], stack_s.at[b])
        hid_s[b] = (
            shift(wide_s[0:C, :], 1) + wide_s[C : 2 * C, :] + shift(wide_s[2 * C : 3 * C, :], -1)
        ).astype(BF)
        for start, size in CHUNKS:
            cut = slice(start, start + size)
            bias = jnp.concatenate([bias_ref[b]] * (size // 128), axis=1)
            inner = mm(expand_ref[b], hid_s[b, :, cut]) + bias
            half = 0.5 + 0.5 * lax.erf(inner * SQRT_HALF)
            active = (inner * half).astype(BF)
            bell = jnp.exp2((inner * inner) * -HALF_LOG2E)
            slope_s[b, :, cut] = (half + (inner * INV_ROOT_TAU) * bell).astype(BF)
            active_s[b, :, cut] = active
            old = out_ref[:, cut].astype(F32)
            out_ref[:, cut] = (old + mm(project_ref[b], active)).astype(BF)

    for b in reversed(range(DEPTH)):
        pg = jnp.zeros((C, HID), F32)
        eg = jnp.zeros((HID, C), F32)
        for start, size in CHUNKS:
            cut = slice(start, start + size)
            up = up_ref[:, cut]
            d_active = mm(projectt_ref[b], up)
            d_inner = (d_active * slope_s[b, :, cut].astype(F32)).astype(BF)
            dh_ref[:, cut] = mm(expandt_ref[b], d_inner).astype(BF)
            pg = pg + mm_nt(up * mask[:, cut], active_s[b, :, cut])
            eg = eg + mm_nt(d_inner, hid_s[b, :, cut] * mask[:, cut])
        own = dh_ref[...] * mask
        rstack_s[0:C, :] = shift(own, -1)
        rstack_s[C : 2 * C, :] = own
        rstack_s[2 * C : 3 * C, :] = shift(own, 1)
        cg = mm_nt(rstack_s[...], stack_s[b])
        pack_share(share_s, b, cg, eg, pg)
        if b > 0:
            step_back(up_ref, dh_ref, convt_ref[b], rstack_s, wide_s, lane)
    own_ref[...] = share_s[pl.ds(2 * core, 2)].reshape(16 * UNITS, 128).astype(BF)
    other_ref[...] = share_s[pl.ds(2 - 2 * core, 2)].reshape(16 * UNITS, 128).astype(BF)


def step_back(up_ref, dh_ref, weights, rstack_s, wide_s, lane):
    rows_stack(rstack_s, dh_ref[...], lane, -1)
    conv_pass(wide_s, weights, rstack_s)
    up_ref[...] = (
        up_ref[...].astype(F32)
        + (shift(wide_s[0:C, :], -1) + wide_s[C : 2 * C, :] + shift(wide_s[2 * C : 3 * C, :], 1))
    ).astype(BF)


def tail_kernel(
    place_ref, flat_ref, up_in, dh_ref, convt_ref, out_ref, grad_ref, wide, up_s, rstack_s, wide_s
):
    flip = place_ref[0]
    lane = lax.broadcasted_iota(jnp.int32, (C, N), 1)
    up_s[...] = up_in[...]
    step_back(up_s, dh_ref, convt_ref[0], rstack_s, wide_s, lane)
    unflatten(flat_ref, out_ref, wide, flip)
    unflatten(up_s, grad_ref, wide, flip)


def pair_kernel(own_ref, other_ref, dst_ref):
    dst_ref[...] = (own_ref[...].astype(F32) + other_ref[...].astype(F32)).astype(BF)


def sum_kernel(src_ref, dst_ref):
    total = src_ref[0].astype(F32)
    for part in range(1, src_ref.shape[0]):
        total = total + src_ref[part].astype(F32)
    total = total.astype(BF)
    for part in range(dst_ref.shape[0]):
        dst_ref[part] = total


def unpack_kernel(src_ref, conv_ref, expand_ref, project_ref):
    for b in range(DEPTH):
        core, xl = b // 2, b % 2
        total = 0.0
        for y in range(4):
            total = total + src_ref[4 * y + 2 * xl + core].astype(F32)
        unit = [total[8 * i : 8 * i + 8, :] for i in range(9)]
        tail = []
        for i in range(5, 9):
            tail += [unit[i][:, 0:C], unit[i][:, C : 2 * C]]
        pieces = []
        for r in range(3):
            for c in range(3):
                pieces.append(tail[c] if r == 2 else unit[c][:, C * r : C * r + C])
        conv_ref[b] = jnp.concatenate(pieces, axis=1)
        for i in range(4):
            expand_ref[b, 8 * i : 8 * i + 8, :] = tail[3 + i]
        project_ref[b] = jnp.concatenate([unit[3], unit[4]], axis=1)


def local(members_in, cotangent, conv_weight, expand_weight, expand_bias, project_weight, orient):
    core = lax.axis_index("core")
    sector = lax.axis_index(LON)
    flip = lax.dynamic_index_in_dim(orient, sector, 0, keepdims=False)
    place = jnp.stack([flip, core])
    field = members_in[0]
    slope = cotangent[0]
    wide = pltpu.VMEM((HALVES, C * H, 128), F32)
    low, high = call(
        edge_kernel,
        [shape(C, 128)] * 2,
        [(place, True), (field, False), (slope, False)],
        [wide, wide],
    )
    count = lax.axis_size(LON)
    left = lax.ppermute(high, LON, [(i, (i + 1) % count) for i in range(count)])
    right = lax.ppermute(low, LON, [((i + 1) % count, i) for i in range(count)])

    expandt = expand_weight.transpose(0, 2, 1)
    flat_f, flat_g, conv, convt, expand, projectt, bias = call(
        prep_kernel,
        [
            shape(C, N),
            shape(C, N),
            shape(DEPTH, 3 * C, 3 * C),
            shape(DEPTH, 3 * C, 3 * C),
            shape(DEPTH, HID, C),
            shape(DEPTH, HID, C),
            shape(DEPTH, HID, 128, dtype=F32),
        ],
        [
            (place, True),
            (field, False),
            (slope, False),
            (conv_weight, False),
            (expandt, False),
            (expand_bias, False),
            (project_weight, False),
        ],
        [wide],
        flops=1 << 27,
    )
    flat_out, up, d_hidden, own, other = call(
        main_kernel,
        [
            shape(C, N),
            shape(C, N),
            shape(C, N),
            shape(16 * UNITS, 128),
            shape(16 * UNITS, 128),
        ],
        [
            (place, True),
            (flat_f, False),
            (flat_g, False),
            (left, False),
            (right, False),
            (conv, False),
            (convt, False),
            (expand, False),
            (expandt, False),
            (bias, False),
            (project_weight, False),
            (projectt, False),
        ],
        [
            pltpu.VMEM((DEPTH, 3 * C, N), BF),
            pltpu.VMEM((DEPTH, C, N), BF),
            pltpu.VMEM((DEPTH, HID, N), BF),
            pltpu.VMEM((DEPTH, HID, N), BF),
            pltpu.VMEM((3 * C, N), F32),
            pltpu.VMEM((3 * C, N), BF),
            pltpu.VMEM((DEPTH, 8, UNITS, 128), F32),
        ],
        flops=1 << 33,
    )
    came = lax.ppermute(other, "core", [(0, 1), (1, 0)])
    share = call(pair_kernel, shape(16 * UNITS, 128), [(own, False), (came, False)])
    parts = lax.all_to_all(share.reshape(16, UNITS, 128), ("xl", "ens"), 0, 0, tiled=True)
    section_out, input_grad = call(
        tail_kernel,
        [shape(C, H, WD)] * 2,
        [(place, True), (flat_out, False), (up, False), (d_hidden, False), (convt, False)],
        [wide, pltpu.VMEM((C, N), BF), pltpu.VMEM((3 * C, N), BF), pltpu.VMEM((3 * C, N), F32)],
        flops=1 << 30,
    )
    parts = call(sum_kernel, shape(count, UNITS, 128), [(parts, False)])
    parts = lax.all_to_all(parts, LON, 0, 0, tiled=True)
    conv_grad, expand_grad, project_grad = call(
        unpack_kernel,
        [
            shape(DEPTH, 8, 9 * C, dtype=F32),
            shape(DEPTH, 32, C, dtype=F32),
            shape(DEPTH, 8, HID, dtype=F32),
        ],
        [(parts, False)],
    )
    return section_out[None], input_grad[None], conv_grad, expand_grad, project_grad


def solution(mesh):
    split = Mesh(mesh.devices.reshape(4, 2, 2, 8), LON + ("ens",))
    cells = P("ens", None, None, LON)
    rows = P(None, "ens", None)
    return jax.shard_map(
        local,
        mesh=split,
        in_specs=(cells, cells, P(), P(), P(), P(), P()),
        out_specs=(cells, cells, rows, rows, rows),
        check_vma=False,
    )
```

time: 96.5 us -> 73.7 us (0.76)
  blocking collectives: 44.3 us -> 15.7 us
  local copies, waits for them, and re-layouts: 11.3 us -> 3.24 us
  starting transfers between devices: 2.6 us -> 10.4 us
  waiting for transfers between devices: 0.01 us -> 5.89 us
    all_to_all x2 -> x1, blocking collectives: 44.3 us -> 15.7 us  [local(): lax.all_to_all(share.reshape(16, UNITS, 128), ('xl', 'ens'), 0, 0, tiled=...]
    all_to_all x0 -> x1, starting transfers between devices: none -> 5.23 us  [local(): parts = lax.all_to_all(parts, LON, 0, 0, tiled=True)]
    all_to_all x0 -> x1, waiting for transfers between devices: none -> 4.37 us  [local(): parts = lax.all_to_all(parts, LON, 0, 0, tiled=True)]
    reshape x3 -> x0, local copies, waits for them, and re-layouts: 3.54 us -> none  [the longest x1 1.21 us: local(): convt = kernels.transpose(0, 3, 4, 2, 1).reshape(DEPTH, 3 * C, 3 * C)]
    ppermute x2 -> x3, starting transfers between devices: 2.6 us -> 5.19 us  [the longest x1 2.6 us: local(): left = lax.ppermute(high, LON, [(i, (i + 1) % count) for i in range(count)])]
    broadcast_in_dim x2 -> x0, local copies, waits for them, and re-layouts: 2.04 us -> none  [the longest x1 1.04 us: local(): expand_bias[:, :, None]]
    unnamed x11 -> x10, local copies, waits for them, and re-layouts: 4.42 us -> 2.66 us
    ppermute x2 -> x3, waiting for transfers between devices: 0.01 us -> 1.52 us  [the longest x1 1.42 us: local(): came = lax.ppermute(other, 'core', [(0, 1), (1, 0)])]
  transfers between devices with their start and end apart: 2 -> 4, of which waited for: 0 -> 3; matrix products, arithmetic and copies ran while one was open for 9% -> 0% of each run, Pallas kernels for 0% -> 9%
where the time goes in v2:
time: 73.7 us; the launch traced here: 73.2 us
  Pallas kernels  36.1 us (49%)
  blocking collectives  15.7 us (21%)
  starting transfers between devices  10.4 us (14%)
  waiting for transfers between devices  5.89 us (8%)
  local copies, waits for them, and re-layouts  3.24 us (4%)
  other arithmetic  1.23 us (2%)
    pallas_call x7, Pallas kernels, call(): pl.pallas_call(body, out_shape=outs, in_specs=specs, out_specs=jax.tree.m...  36.1 us
    all_to_all x1, blocking collectives, local(): lax.all_to_all(share.reshape(16, UNITS, 128), ('xl', 'ens'), 0, 0, tiled=...  15.7 us
    all_to_all x1, starting transfers between devices, local(): parts = lax.all_to_all(parts, LON, 0, 0, tiled=True)  5.23 us
    all_to_all x1, waiting for transfers between devices, local(): parts = lax.all_to_all(parts, LON, 0, 0, tiled=True)  4.37 us
    unnamed x10, local copies, waits for them, and re-layouts  2.66 us
    ppermute x1, starting transfers between devices, local(): left = lax.ppermute(high, LON, [(i, (i + 1) % count) for i in range(count)])  2.6 us
    ppermute x1, starting transfers between devices, local(): came = lax.ppermute(other, 'core', [(0, 1), (1, 0)])  2.59 us
  transfers between devices with their start and end apart: 4, of which 3 were waited for; matrix products, arithmetic and copies ran while one was open for 0% of the time, Pallas kernels for 9%

profile of v2, /device:TPU:1, one launch (start us, length us, event | category | flops | bytes accessed | tf_op | source)
XLA Modules:
  0.0 73.2 jit_solution(18149799042245192304)
XLA Ops:
  0.6 0.0 copy-start.4
  0.6 0.6 copy-done.4
  1.3 0.6 dynamic_slice.4
  1.9 1.2 %pad_add_fusion.place_ref = s32[2]{0:T(128)} fusion(s32[1]{0:T(128)} %bitcast, s32[1]{0:T(128)} %dynamic_slice.4), kind=kLoop, calls=%fused_computation | loop fusion | flops 2 | bytes 16 | tf_op jit(solution)/shard_map/stack | solution.py:329
  3.1 2.1 %shard_map.111 = (bf16[64,128]{1,0:T(8,128)(2,1)}, bf16[64,128]{1,0:T(8,128)(2,1)}) custom-call(s32[2]{0:T(128)} %pad_add_fusion.place_ref, bf16[64,8,256]{2,1,0:T(8,128)(2,1)} %bitcast.8, bf16[64,8,256]{2,1,0:T(8,128)(2,1)} %bitcast.10), custom_call_target="tpu_custom_call" | custom-call | bytes 1048576 | tf_op jit(solution)/shard_map/pallas_call | solution.py:45
  5.2 2.6 %collective-permute-start = (bf16[64,128]{1,0:T(8,128)(2,1)}, bf16[64,128]{1,0:T(8,128)(2,1)S(1)}, u32[]{:S(2)}, u32[]{:S(2)}) collective-permute-start(bf16[64,128]{1,0:T(8,128)(2,1)} %get-tuple-element.26), channel_id=1, source_target_pairs={{0,8},{8,16},{16,24},{24,32},{32,40},{40,48},{48,56},{56,64},{64,7... | collective-permute-start | bytes 49160 | tf_op jit(solution)/shard_map/ppermute | solution.py:340
  7.8 0.0 collective-permute-start.1
  7.8 3.6 %shard_map.110 = (bf16[64,2176]{1,0:T(8,128)(2,1)}, bf16[64,2176]{1,0:T(8,128)(2,1)}, bf16[4,192,192]{2,1,0:T(8,128)(2,1)}, bf16[4,192,192]{2,1,0:T(8,128)(2,1)}...) custom-call(s32[2]{0:T(128)} %pad_add_fusion.place_ref, ...), custom_call_target="tpu_custom_call" | custom-call | flops 134217728 | bytes 1048576 | tf_op jit(solution)/shard_map/pallas_call | solution.py:45
  11.3 0.0 collective-permute-done.left_ref
  11.3 0.0 copy-start.2
  11.3 0.1 collective-permute-done.1.right_ref
  11.5 0.0 copy-start.3
  11.5 0.5 copy-done.2
  11.9 0.1 copy-done.3
  12.1 22.1 %shard_map.112 = (bf16[64,2176]{1,0:T(8,128)(2,1)}, bf16[64,2176]{1,0:T(8,128)(2,1)}, bf16[64,2176]{1,0:T(8,128)(2,1)}, bf16[1152,128]{1,0:T(8,128)(2,1)}, bf16[1152,128]{1,0:T(8,128)(2,1)}) custom-call(s32[2]{0:T(128)} %pad_add_fusion.place_ref, bf16[64,2176]{1,0:T(8,128)(2,1)} %get-tuple-element.24.field_ref, ...), custom_call_target="tpu_custom_call" | custom-call | flops 8589934592 | bytes 1048576 | tf_op jit(solution)/shard_map/pallas_call | solution.py:45
  34.1 2.6 %collective-permute-start.2 = (bf16[1152,128]{1,0:T(8,128)(2,1)}, bf16[1152,128]{1,0:T(8,128)(2,1)S(1)}, u32[]{:S(2)}, u32[]{:S(2)}) collective-permute-start(bf16[1152,128]{1,0:T(8,128)(2,1)} %get-tuple-element.39), channel_id=1, source_target_pairs={{0,8},{8,0},{1,9},{9,1},{2,10},{10,2},{3,11},{11,3},{4,12},{12,4},... | collective-permute-start | bytes 884744 | tf_op jit(solution)/shard_map/ppermute | solution.py:401
  36.7 1.4 %collective-permute-done.2.other_ref = bf16[1152,128]{1,0:T(8,128)(2,1)S(1)} collective-permute-done((bf16[1152,128]{1,0:T(8,128)(2,1)}, bf16[1152,128]{1,0:T(8,128)(2,1)S(1)}, u32[]{:S(2)}, u32[]{:S(2)}) %collective-permute-start.2) | collective-permute-done | bytes 294944 | tf_op jit(solution)/shard_map/ppermute | solution.py:401
  38.1 0.0 copy-start.1
  38.1 0.7 copy-done.1
  38.8 1.8 %shard_map.114 = bf16[1152,128]{1,0:T(8,128)(2,1)} custom-call(bf16[1152,128]{1,0:T(8,128)(2,1)} %get-tuple-element.38.own_ref, bf16[1152,128]{1,0:T(8,128)(2,1)} %copy-done.1), custom_call_target="tpu_custom_call" | custom-call | bytes 1048576 | tf_op jit(solution)/shard_map/pallas_call | solution.py:45
  40.7 15.7 %all_to_all.10.src_ref = bf16[16,72,128]{2,1,0:T(8,128)(2,1)} all-to-all(bf16[16,72,128]{2,1,0:T(8,128)(2,1)} %bitcast.7), channel_id=1, replica_groups=mesh['y'=4,'xl'=2,'core'=2,'ens'=8] {'xl','ens'}, dimensions={0} | all-to-all | bytes 589824 | tf_op jit(solution)/shard_map/all_to_all | solution.py:403
  56.4 1.7 %shard_map.115 = bf16[16,72,128]{2,1,0:T(8,128)(2,1)} custom-call(bf16[16,72,128]{2,1,0:T(8,128)(2,1)} %all_to_all.10.src_ref), custom_call_target="tpu_custom_call" | custom-call | bytes 1048576 | tf_op jit(solution)/shard_map/pallas_call | solution.py:45
  58.1 5.2 %all-to-all-start.1 = ((bf16[16,72,128]{2,1,0:T(8,128)(2,1)}), bf16[16,72,128]{2,1,0:T(8,128)(2,1)S(1)}, u32[]{:S(2)}, u32[]{:S(2)}) async-start(bf16[16,72,128]{2,1,0:T(8,128)(2,1)} %shard_map.115), calls=%async_computation.1 | async-start | bytes 589824 | tf_op jit(solution)/shard_map/all_to_all | solution.py:412
  63.3 3.1 %shard_map.113 = (bf16[64,8,256]{2,1,0:T(8,128)(2,1)}, bf16[64,8,256]{2,1,0:T(8,128)(2,1)}) custom-call(s32[2]{0:T(128)} %pad_add_fusion.place_ref, bf16[64,2176]{1,0:T(8,128)(2,1)} %get-tuple-element.33.flat_ref, bf16[64,2176]{1,0:T(8,128)(2,1)} %get-tuple-element.34.up_in, bf16[64,2176]{1,0:T(8,128)(2,1)} %get-tuple-element.35.dh_ref, ...), custom_call_target="tpu_custom_call" | custom-call | flops 1073741824 | bytes 1048576 | tf_op jit(solution)/shard_map/pallas_call | solution.py:45
  66.4 4.4 %all-to-all-done.1.src_ref = bf16[16,72,128]{2,1,0:T(8,128)(2,1)S(1)} async-done(((bf16[16,72,128]{2,1,0:T(8,128)(2,1)}), bf16[16,72,128]{2,1,0:T(8,128)(2,1)S(1)}, u32[]{:S(2)}, u32[]{:S(2)}) %all-to-all-start.1) | async-done | bytes 294944 | tf_op jit(solution)/shard_map/all_to_all | solution.py:412
  70.8 0.0 copy-start
  70.8 0.7 copy-done
  71.5 1.7 %shard_map.116 = (f32[4,8,576]{2,1,0:T(8,128)}, f32[4,32,64]{2,1,0:T(8,128)}, f32[4,8,256]{2,1,0:T(8,128)}) custom-call(bf16[16,72,128]{2,1,0:T(8,128)(2,1)} %copy-done), custom_call_target="tpu_custom_call" | custom-call | bytes 1048576 | tf_op jit(solution)/shard_map/pallas_call | solution.py:45
Async XLA Ops:
  0.6 0.7 copy-start.4
  5.2 6.2 %collective-permute-start = (bf16[64,128]{1,0:T(8,128)(2,1)}, bf16[64,128]{1,0:T(8,128)(2,1)S(1)}, u32[]{:S(2)}, u32[]{:S(2)}) collective-permute-start(bf16[64,128]{1,0:T(8,128)(2,1)} %get-tuple-element.26), channel_id=1, source_target_pairs={{0,8},{8,16},{16,24},{24,32},{32,40},{40,48},{48,56},{56,64},{64,7... | collective-permute-start | bytes 49160 | tf_op jit(solution)/shard_map/ppermute | solution.py:340
  7.8 3.7 %collective-permute-start.1 = (bf16[64,128]{1,0:T(8,128)(2,1)}, bf16[64,128]{1,0:T(8,128)(2,1)S(1)}, u32[]{:S(2)}, u32[]{:S(2)}) collective-permute-start(bf16[64,128]{1,0:T(8,128)(2,1)} %get-tuple-element.27), channel_id=1, source_target_pairs={{8,0},{16,8},{24,16},{32,24},{40,32},{48,40},{56,48},{64,56},{72,6... | collective-permute-start | bytes 49160 | tf_op jit(solution)/shard_map/ppermute | solution.py:341
  11.3 0.6 copy-start.2
  11.5 0.6 copy-start.3
  34.1 4.0 %collective-permute-start.2 = (bf16[1152,128]{1,0:T(8,128)(2,1)}, bf16[1152,128]{1,0:T(8,128)(2,1)S(1)}, u32[]{:S(2)}, u32[]{:S(2)}) collective-permute-start(bf16[1152,128]{1,0:T(8,128)(2,1)} %get-tuple-element.39), channel_id=1, source_target_pairs={{0,8},{8,0},{1,9},{9,1},{2,10},{10,2},{3,11},{11,3},{4,12},{12,4},... | collective-permute-start | bytes 884744 | tf_op jit(solution)/shard_map/ppermute | solution.py:401
  38.1 0.7 copy-start.1
  58.1 12.7 %all-to-all-start.1 = ((bf16[16,72,128]{2,1,0:T(8,128)(2,1)}), bf16[16,72,128]{2,1,0:T(8,128)(2,1)S(1)}, u32[]{:S(2)}, u32[]{:S(2)}) async-start(bf16[16,72,128]{2,1,0:T(8,128)(2,1)} %shard_map.115), calls=%async_computation.1 | async-start | bytes 589824 | tf_op jit(solution)/shard_map/all_to_all | solution.py:412
  70.8 0.7 copy-start

commit v3 on v2

--- a/solution.py
+++ b/solution.py
@@ -24,7 +24,9 @@
 TILES = N // 128
 UNITS = 72
 CHUNKS = [(s, min(256, N - s)) for s in range(0, N, 256)]
-VMEM = 56 * 1024 * 1024
+FORWARD_LAG = 7
+BACKWARD_LAG = 8
+TURN = 6
 LON = ("y", "xl", "core")
 
 NT = (((1,), (1,)), ((), ()))
@@ -38,7 +40,7 @@
     return lax.dot_general(a, b, NT, preferred_element_type=F32)
 
 
-def call(body, outs, ins, scratch=(), flops=0):
+def call(body, outs, ins, scratch=(), flops=0, mib=8):
     specs = [
         pl.BlockSpec(memory_space=pltpu.SMEM if scalar else pltpu.VMEM) for _, scalar in ins
     ]
@@ -48,7 +50,7 @@
         in_specs=specs,
         out_specs=jax.tree.map(lambda _: pl.BlockSpec(memory_space=pltpu.VMEM), outs),
         scratch_shapes=list(scratch),
-        compiler_params=pltpu.CompilerParams(vmem_limit_bytes=VMEM),
+        compiler_params=pltpu.CompilerParams(vmem_limit_bytes=mib << 20),
         cost_estimate=pl.CostEstimate(flops=flops, bytes_accessed=1 << 20, transcendentals=0),
     )(*[array for array, _ in ins])
 
@@ -63,12 +65,17 @@
         wide[half] = part.astype(F32).reshape(C * H, 128)
 
 
+def own_flip(orient_ref):
+    sector = (lax.axis_index("y") * 2 + lax.axis_index("xl")) * 2 + lax.axis_index("core")
+    return orient_ref[sector]
+
+
 def stored_row(flip, row):
     return jnp.where(flip == 1, H - 1 - row, row)
 
 
-def edge_kernel(place_ref, field_ref, slope_ref, low_ref, high_ref, wide_f, wide_g):
-    flip = place_ref[0]
+def edge_kernel(orient_ref, field_ref, slope_ref, low_ref, high_ref, wide_f, wide_g):
+    flip = own_flip(orient_ref)
     spread(wide_f, field_ref)
     spread(wide_g, slope_ref)
     lane = lax.broadcasted_iota(jnp.int32, (C, 128), 1)
@@ -111,7 +118,7 @@
 
 
 def prep_kernel(
-    place_ref,
+    orient_ref,
     field_ref,
     slope_ref,
     kernel_ref,
@@ -127,7 +134,7 @@
     bias_out,
     wide,
 ):
-    flip = place_ref[0]
+    flip = own_flip(orient_ref)
     field_out[...] = flatten(field_ref, wide, flip).astype(BF)
     slope_out[...] = flatten(slope_ref, wide, flip).astype(BF)
     for b in range(DEPTH):
@@ -187,8 +194,176 @@
             dst[at, e, 8 * i : 8 * i + 8, :] = unit
 
 
+def tile(ref, t, rows=slice(None)):
+    return ref[rows, 128 * t : 128 * t + 128]
+
+
+def span(t):
+    return slice(128 * t, 128 * t + 128)
+
+
+TILE_SETS = [[t for t in range(s // 128, (s + z) // 128)] for s, z in CHUNKS]
+CUTS = [slice(s, s + z) for s, z in CHUNKS]
+COUNT = len(CHUNKS)
+
+
+def make_row_stack(src_ref, dst_ref, sign):
+    lane = lax.broadcasted_iota(jnp.int32, (C, 128), 1)
+    rolled = {}
+
+    def roll16(t, way):
+        if (t, way) not in rolled:
+            rolled[t, way] = pltpu.roll(tile(src_ref, t), 16 * way % 128, axis=1)
+        return rolled[t, way]
+
+    def stack(t):
+        if t < 2:
+            before = jnp.zeros((C, 128), BF)
+        elif t == 2:
+            before = jnp.where(lane < 16, 0, roll16(0, 1)).astype(BF)
+        else:
+            before = jnp.where(lane < 16, roll16(t - 3, 1), roll16(t - 2, 1))
+        if t > TILES - 3:
+            after = jnp.zeros((C, 128), BF)
+        elif t == TILES - 3:
+            after = jnp.where(lane < 112, roll16(TILES - 1, -1), 0).astype(BF)
+        else:
+            after = jnp.where(lane < 112, roll16(t + 2, -1), roll16(t + 3, -1))
+        first, last = (before, after) if sign > 0 else (after, before)
+        dst_ref[0:C, span(t)] = first
+        dst_ref[C : 2 * C, span(t)] = tile(src_ref, t)
+        dst_ref[2 * C : 3 * C, span(t)] = last
+
+    return stack
+
+
+def make_neighbours(read_right, read_left):
+    lane = lax.broadcasted_iota(jnp.int32, (C, 128), 1)
+    right = {}
+    left = {}
+
+    def get(t):
+        for k in (t - 1, t):
+            if k not in right:
+                right[k] = pltpu.roll(read_right(k % TILES), 1, axis=1)
+        for k in (t, t + 1):
+            if k not in left:
+                left[k] = pltpu.roll(read_left(k % TILES), 127, axis=1)
+        return jnp.where(lane < 1, right[t - 1], right[t]), jnp.where(lane < 127, left[t], left[t + 1])
+
+    return get
+
+
+def forward_stages(
+    b, out_ref, stack_s, wide_s, hid_s, active_s, slope_s, conv_ref, expand_ref, bias_ref, project_ref
+):
+    stack = make_row_stack(out_ref, stack_s.at[b], 1)
+    moved = make_neighbours(
+        lambda t: tile(wide_s, t, slice(0, C)), lambda t: tile(wide_s, t, slice(2 * C, 3 * C))
+    )
+
+    def stacks(i):
+        for t in TILE_SETS[i]:
+            stack(t)
+
+    def conv(i):
+        wide_s[:, CUTS[i]] = mm(conv_ref[b], stack_s[b, :, CUTS[i]])
+
+    def hidden(i):
+        for t in TILE_SETS[i]:
+            low, high = moved(t)
+            hid_s[b, :, span(t)] = (low + tile(wide_s, t, slice(C, 2 * C)) + high).astype(BF)
+
+    def expand(i):
+        cut = CUTS[i]
+        bias = jnp.concatenate([bias_ref[b]] * len(TILE_SETS[i]), axis=1)
+        inner = mm(expand_ref[b], hid_s[b, :, cut]) + bias
+        half = 0.5 + 0.5 * lax.erf(inner * SQRT_HALF)
+        bell = jnp.exp2((inner * inner) * -HALF_LOG2E)
+        slope_s[b, :, cut] = (half + (inner * INV_ROOT_TAU) * bell).astype(BF)
+        active_s[b, :, cut] = (inner * half).astype(BF)
+
+    def project(i):
+        cut = CUTS[i]
+        old = stack_s[b, C : 2 * C, cut].astype(F32)
+        out_ref[:, cut] = (old + mm(project_ref[b], active_s[b, :, cut])).astype(BF)
+
+    return [(stacks, 0), (conv, 1), (hidden, 2), (expand, 3), (project, 4)]
+
+
+def backward_stages(
+    b, up_ref, dh_ref, stack_s, rstack_s, own_s, wide_s, hid_s, active_s, slope_s, din_s, mask_s,
+    convt_ref, expandt_ref, projectt_ref, sums,
+):
+    stack = make_row_stack(dh_ref, rstack_s, -1)
+    moved = make_neighbours(
+        lambda t: tile(wide_s, t, slice(2 * C, 3 * C)), lambda t: tile(wide_s, t, slice(0, C))
+    )
+    own_moved = make_neighbours(
+        lambda t: tile(own_s, t, slice(C, 2 * C)), lambda t: tile(own_s, t, slice(C, 2 * C))
+    )
+    pg = []
+    eg = []
+    cg = []
+
+    def inner(i):
+        cut = CUTS[i]
+        up = up_ref[:, cut]
+        d_active = mm(projectt_ref[b], up)
+        d_inner = (d_active * slope_s[b, :, cut].astype(F32)).astype(BF)
+        din_s[:, cut] = d_inner
+        pg.append(mm_nt(up * mask_s[:, cut], active_s[b, :, cut]))
+
+    def hidden(i):
+        cut = CUTS[i]
+        d_inner = din_s[:, cut]
+        d_hidden = mm(expandt_ref[b], d_inner).astype(BF)
+        dh_ref[:, cut] = d_hidden
+        own_s[C : 2 * C, cut] = d_hidden * mask_s[:, cut]
+        eg.append(mm_nt(d_inner, hid_s[b, :, cut] * mask_s[:, cut]))
+
+    def shares(i):
+        for t in TILE_SETS[i]:
+            right, left = own_moved(t)
+            own_s[0:C, span(t)] = left
+            own_s[2 * C : 3 * C, span(t)] = right
+        cg.append(mm_nt(own_s[:, CUTS[i]], stack_s[b, :, CUTS[i]]))
+
+    def stacks(i):
+        for t in TILE_SETS[i]:
+            stack(t)
+
+    def conv(i):
+        wide_s[:, CUTS[i]] = mm(convt_ref[b], rstack_s[:, CUTS[i]])
+
+    def update(i):
+        for t in TILE_SETS[i]:
+            right, left = moved(t)
+            total = tile(up_ref, t).astype(F32) + (left + tile(wide_s, t, slice(C, 2 * C)) + right)
+            up_ref[:, span(t)] = total.astype(BF)
+
+    def finish():
+        sums[b] = (sum(cg[1:], cg[0]), sum(eg[1:], eg[0]), sum(pg[1:], pg[0]))
+
+    stages = [(inner, 0), (hidden, 1), (shares, 3)]
+    if b > 0:
+        stages += [(stacks, 4), (conv, 5), (update, 7)]
+    return stages, finish
+
+
+def emit(jobs):
+    last = max(first + max(lag for _, lag in stages) + COUNT for first, stages, _ in jobs)
+    for step in range(last + 1):
+        for first, stages, finish in jobs:
+            for stage, lag in stages:
+                i = step - first - lag
+                if 0 <= i < COUNT:
+                    stage(i)
+            if finish is not None and step == first + max(lag for _, lag in stages) + COUNT:
+                finish()
+
+
 def main_kernel(
-    place_ref,
     field_ref,
     slope_ref,
     left_ref,
@@ -212,8 +387,11 @@
     wide_s,
     rstack_s,
     share_s,
+    own_s,
+    din_s,
+    mask_s,
 ):
-    core = place_ref[1]
+    core = lax.axis_index("core")
     lane = lax.broadcasted_iota(jnp.int32, (C, N), 1)
     column = lane
     for row in range(1, H):
@@ -228,43 +406,36 @@
     up_ref[...] = slope_ref[...]
     add_halo(up_ref, pltpu.roll(left, 120, axis=1), right)
 
+    mask_s[...] = mask
+    wide_s[:, N - 128 : N] = jnp.zeros((3 * C, 128), F32)
+    own_s[C : 2 * C, N - 128 : N] = jnp.zeros((C, 128), BF)
+    jobs = []
+    first = 0
     for b in range(DEPTH):
-        rows_stack(stack_s.at[b], out_ref[...], lane, 1)
-        conv_pass(wide_s, conv_ref[b], stack_s.at[b])
-        hid_s[b] = (
-            shift(wide_s[0:C, :], 1) + wide_s[C : 2 * C, :] + shift(wide_s[2 * C : 3 * C, :], -1)
-        ).astype(BF)
-        for start, size in CHUNKS:
-            cut = slice(start, start + size)
-            bias = jnp.concatenate([bias_ref[b]] * (size // 128), axis=1)
-            inner = mm(expand_ref[b], hid_s[b, :, cut]) + bias
-            half = 0.5 + 0.5 * lax.erf(inner * SQRT_HALF)
-            active = (inner * half).astype(BF)
-            bell = jnp.exp2((inner * inner) * -HALF_LOG2E)
-            slope_s[b, :, cut] = (half + (inner * INV_ROOT_TAU) * bell).astype(BF)
-            active_s[b, :, cut] = active
-            old = out_ref[:, cut].astype(F32)
-            out_ref[:, cut] = (old + mm(project_ref[b], active)).astype(BF)
+        stages = forward_stages(
+            b, out_ref, stack_s, wide_s, hid_s, active_s, slope_s,
+            conv_ref, expand_ref, bias_ref, project_ref,
+        )
+        jobs.append((first, stages, None))
+        first += FORWARD_LAG
+    first = first - FORWARD_LAG + TURN
+    sums = {}
+
+    def closing(b, finish):
+        def run():
+            finish()
+            pack_share(share_s, b, *sums[b])
+
+        return run
 
     for b in reversed(range(DEPTH)):
-        pg = jnp.zeros((C, HID), F32)
-        eg = jnp.zeros((HID, C), F32)
-        for start, size in CHUNKS:
-            cut = slice(start, start + size)
-            up = up_ref[:, cut]
-            d_active = mm(projectt_ref[b], up)
-            d_inner = (d_active * slope_s[b, :, cut].astype(F32)).astype(BF)
-            dh_ref[:, cut] = mm(expandt_ref[b], d_inner).astype(BF)
-            pg = pg + mm_nt(up * mask[:, cut], active_s[b, :, cut])
-            eg = eg + mm_nt(d_inner, hid_s[b, :, cut] * mask[:, cut])
-        own = dh_ref[...] * mask
-        rstack_s[0:C, :] = shift(own, -1)
-        rstack_s[C : 2 * C, :] = own
-        rstack_s[2 * C : 3 * C, :] = shift(own, 1)
-        cg = mm_nt(rstack_s[...], stack_s[b])
-        pack_share(share_s, b, cg, eg, pg)
-        if b > 0:
-            step_back(up_ref, dh_ref, convt_ref[b], rstack_s, wide_s, lane)
+        stages, finish = backward_stages(
+            b, up_ref, dh_ref, stack_s, rstack_s, own_s, wide_s, hid_s, active_s, slope_s, din_s,
+            mask_s, convt_ref, expandt_ref, projectt_ref, sums,
+        )
+        jobs.append((first, stages, closing(b, finish)))
+        first += BACKWARD_LAG
+    emit(jobs)
     own_ref[...] = share_s[pl.ds(2 * core, 2)].reshape(16 * UNITS, 128).astype(BF)
     other_ref[...] = share_s[pl.ds(2 - 2 * core, 2)].reshape(16 * UNITS, 128).astype(BF)
 
@@ -279,27 +450,14 @@
 
 
 def tail_kernel(
-    place_ref, flat_ref, up_in, dh_ref, convt_ref, out_ref, grad_ref, wide, up_s, rstack_s, wide_s
+    orient_ref, flat_ref, up_in, dh_ref, convt_ref, out_ref, grad_ref, wide, up_s, rstack_s, wide_s
 ):
-    flip = place_ref[0]
+    flip = own_flip(orient_ref)
     lane = lax.broadcasted_iota(jnp.int32, (C, N), 1)
     up_s[...] = up_in[...]
     step_back(up_s, dh_ref, convt_ref[0], rstack_s, wide_s, lane)
     unflatten(flat_ref, out_ref, wide, flip)
     unflatten(up_s, grad_ref, wide, flip)
-
-
-def pair_kernel(own_ref, other_ref, dst_ref):
-    dst_ref[...] = (own_ref[...].astype(F32) + other_ref[...].astype(F32)).astype(BF)
-
-
-def sum_kernel(src_ref, dst_ref):
-    total = src_ref[0].astype(F32)
-    for part in range(1, src_ref.shape[0]):
-        total = total + src_ref[part].astype(F32)
-    total = total.astype(BF)
-    for part in range(dst_ref.shape[0]):
-        dst_ref[part] = total
 
 
 def unpack_kernel(src_ref, conv_ref, expand_ref, project_ref):
@@ -322,19 +480,31 @@
         project_ref[b] = jnp.concatenate([unit[3], unit[4]], axis=1)
 
 
+def main_scratch():
+    return [
+        pltpu.VMEM((DEPTH, 3 * C, N), BF),
+        pltpu.VMEM((DEPTH, C, N), BF),
+        pltpu.VMEM((DEPTH, HID, N), BF),
+        pltpu.VMEM((DEPTH, HID, N), BF),
+        pltpu.VMEM((3 * C, N), F32),
+        pltpu.VMEM((3 * C, N), BF),
+        pltpu.VMEM((DEPTH, 8, UNITS, 128), F32),
+        pltpu.VMEM((3 * C, N), BF),
+        pltpu.VMEM((HID, N), BF),
+        pltpu.VMEM((C, N), BF),
+    ]
+
+
 def local(members_in, cotangent, conv_weight, expand_weight, expand_bias, project_weight, orient):
-    core = lax.axis_index("core")
-    sector = lax.axis_index(LON)
-    flip = lax.dynamic_index_in_dim(orient, sector, 0, keepdims=False)
-    place = jnp.stack([flip, core])
     field = members_in[0]
     slope = cotangent[0]
     wide = pltpu.VMEM((HALVES, C * H, 128), F32)
     low, high = call(
         edge_kernel,
         [shape(C, 128)] * 2,
-        [(place, True), (field, False), (slope, False)],
+        [(orient, True), (field, False), (slope, False)],
         [wide, wide],
+        mib=12,
     )
     count = lax.axis_size(LON)
     left = lax.ppermute(high, LON, [(i, (i + 1) % count) for i in range(count)])
@@ -353,7 +523,7 @@
             shape(DEPTH, HID, 128, dtype=F32),
         ],
         [
-            (place, True),
+            (orient, True),
             (field, False),
             (slope, False),
             (conv_weight, False),
@@ -363,6 +533,7 @@
         ],
         [wide],
         flops=1 << 27,
+        mib=16,
     )
     flat_out, up, d_hidden, own, other = call(
         main_kernel,
@@ -374,7 +545,6 @@
             shape(16 * UNITS, 128),
         ],
         [
-            (place, True),
             (flat_f, False),
             (flat_g, False),
             (left, False),
@@ -387,28 +557,23 @@
             (project_weight, False),
             (projectt, False),
         ],
-        [
-            pltpu.VMEM((DEPTH, 3 * C, N), BF),
-            pltpu.VMEM((DEPTH, C, N), BF),
-            pltpu.VMEM((DEPTH, HID, N), BF),
-            pltpu.VMEM((DEPTH, HID, N), BF),
-            pltpu.VMEM((3 * C, N), F32),
-            pltpu.VMEM((3 * C, N), BF),
-            pltpu.VMEM((DEPTH, 8, UNITS, 128), F32),
-        ],
+        main_scratch(),
         flops=1 << 33,
+        mib=40,
     )
     came = lax.ppermute(other, "core", [(0, 1), (1, 0)])
-    share = call(pair_kernel, shape(16 * UNITS, 128), [(own, False), (came, False)])
+    share = (own.astype(F32) + came.astype(F32)).astype(BF)
     parts = lax.all_to_all(share.reshape(16, UNITS, 128), ("xl", "ens"), 0, 0, tiled=True)
     section_out, input_grad = call(
         tail_kernel,
         [shape(C, H, WD)] * 2,
-        [(place, True), (flat_out, False), (up, False), (d_hidden, False), (convt, False)],
+        [(orient, True), (flat_out, False), (up, False), (d_hidden, False), (convt, False)],
         [wide, pltpu.VMEM((C, N), BF), pltpu.VMEM((3 * C, N), BF), pltpu.VMEM((3 * C, N), F32)],
         flops=1 << 30,
-    )
-    parts = call(sum_kernel, shape(count, UNITS, 128), [(parts, False)])
+        mib=16,
+    )
+    total = jnp.sum(parts.astype(F32), axis=0).astype(BF)
+    parts = jnp.broadcast_to(total[None], (count, UNITS, 128))
     parts = lax.all_to_all(parts, LON, 0, 0, tiled=True)
     conv_grad, expand_grad, project_grad = call(
         unpack_kernel,

time: 73.7 us -> 59 us (0.80)
  Pallas kernels: 36.1 us -> 19.4 us
  local copies, waits for them, and re-layouts: 3.24 us -> 6.09 us
  other arithmetic: 1.23 us -> 0.13 us
    pallas_call x7 -> x5, Pallas kernels: 36.1 us -> 19.4 us  [call(): pl.pallas_call(body, out_shape=outs, in_specs=specs, out_specs=jax.tree.m...]
    unnamed x10 -> x22, local copies, waits for them, and re-layouts: 2.66 us -> 5.34 us
    another operation x1 -> x0, other arithmetic: 1.23 us -> none  [local(): place = jnp.stack([flip, core])]
    broadcast_in_dim x0 -> x1, local copies, waits for them, and re-layouts: none -> 0.75 us  [local(): parts = jnp.broadcast_to(total[None], (count, UNITS, 128))]
  transfers between devices with their start and end apart: 4 -> 4, of which waited for: 3 -> 2; matrix products, arithmetic and copies ran while one was open for 0% -> 0% of each run, Pallas kernels for 9% -> 7%
where the time goes in v3:
time: 59 us; the launch traced here: 58.6 us
  Pallas kernels  19.4 us (33%)
  blocking collectives  15.4 us (26%)
  starting transfers between devices  10.6 us (18%)
  waiting for transfers between devices  6.29 us (11%)
  local copies, waits for them, and re-layouts  6.09 us (10%)
  between operations  0.73 us (1%)
    pallas_call x5, Pallas kernels, call(): pl.pallas_call(body, out_shape=outs, in_specs=specs, out_specs=jax.tree.m...  19.4 us
    all_to_all x1, blocking collectives, local(): lax.all_to_all(share.reshape(16, UNITS, 128), ('xl', 'ens'), 0, 0, tiled=...  15.4 us
    unnamed x22, local copies, waits for them, and re-layouts  5.34 us
    all_to_all x1, starting transfers between devices, local(): parts = lax.all_to_all(parts, LON, 0, 0, tiled=True)  5.23 us
    all_to_all x1, waiting for transfers between devices, local(): parts = lax.all_to_all(parts, LON, 0, 0, tiled=True)  5.08 us
    ppermute x1, starting transfers between devices, local(): came = lax.ppermute(other, 'core', [(0, 1), (1, 0)])  2.75 us
    ppermute x1, starting transfers between devices, local(): left = lax.ppermute(high, LON, [(i, (i + 1) % count) for i in range(count)])  2.67 us
    ppermute x1, waiting for transfers between devices, local(): came = lax.ppermute(other, 'core', [(0, 1), (1, 0)])  1.21 us
  transfers between devices with their start and end apart: 4, of which 2 were waited for; matrix products, arithmetic and copies ran while one was open for 0% of the time, Pallas kernels for 7%

profile of v3, /device:TPU:1, one launch (start us, length us, event | category | flops | bytes accessed | tf_op | source)
XLA Modules:
  0.0 58.6 jit_solution(4862494010114880418)
XLA Ops:
  0.6 0.0 copy-start.10
  0.6 0.6 %copy-done.10 = s32[16]{0:T(128)S(1)} copy-done((s32[16]{0:T(128)S(1)}, s32[16]{0:T(128)}, u32[]{:S(2)}) %copy-start.10) | copy-done | bytes 88
  1.3 0.0 copy-start
  1.3 0.9 %copy-done = bf16[1,64,8,256]{3,2,1,0:T(8,128)(2,1)S(1)} copy-done((bf16[1,64,8,256]{3,2,1,0:T(8,128)(2,1)S(1)}, bf16[1,64,8,256]{3,2,1,0:T(8,128)(2,1)}, u32[]{:S(2)}) %copy-start) | copy-done | bytes 262168
  2.2 0.0 copy-start.2
  2.2 0.9 %copy-done.2 = bf16[1,64,8,256]{3,2,1,0:T(8,128)(2,1)S(1)} copy-done((bf16[1,64,8,256]{3,2,1,0:T(8,128)(2,1)S(1)}, bf16[1,64,8,256]{3,2,1,0:T(8,128)(2,1)}, u32[]{:S(2)}) %copy-start.2) | copy-done | bytes 262168
  3.2 0.0 copy-start.1
  3.2 0.0 copy-start.3
  3.2 0.9 %shard_map.111 = (bf16[64,128]{1,0:T(8,128)(2,1)S(1)}, bf16[64,128]{1,0:T(8,128)(2,1)S(1)}) custom-call(s32[16]{0:T(128)S(1)} %copy-done.10, bf16[64,8,256]{2,1,0:T(8,128)(2,1)S(1)} %bitcast.6, bf16[64,8,256]{2,1,0:T(8,128)(2,1)S(1)} %bitcast.8), custom_call_target="tpu_custom_call" | custom-call | bytes 1048576 | tf_op jit(solution)/shard_map/pallas_call | solution.py:47
  4.1 0.0 copy-start.9
  4.1 2.7 %collective-permute-start = (bf16[64,128]{1,0:T(8,128)(2,1)S(1)}, bf16[64,128]{1,0:T(8,128)(2,1)S(1)}, u32[]{:S(2)}, u32[]{:S(2)}) collective-permute-start(bf16[64,128]{1,0:T(8,128)(2,1)S(1)} %get-tuple-element.26), channel_id=1, source_target_pairs={{0,8},{8,16},{16,24},{24,32},{32,40},{40,48},{48,56},{56,64},{64,7... | collective-permute-start | bytes 49160 | tf_op jit(solution)/shard_map/ppermute | solution.py:510
  6.8 0.0 collective-permute-start.1
  6.8 0.0 copy-done.1
  6.8 0.0 copy-done.3
  6.8 0.0 copy-done.9
  6.8 0.0 copy-start.4
  6.8 1.0 %copy-done.4 = bf16[4,64,576]{2,1,0:T(8,128)(2,1)S(1)} copy-done((bf16[4,64,576]{2,1,0:T(8,128)(2,1)S(1)}, bf16[4,64,576]{2,1,0:T(8,128)(2,1)}, u32[]{:S(2)}) %copy-start.4) | copy-done | bytes 294936
  7.8 0.0 copy-start.5
  7.8 0.9 %copy-done.5 = bf16[4,256,64]{1,2,0:T(8,128)(2,1)S(1)} copy-done((bf16[4,256,64]{1,2,0:T(8,128)(2,1)S(1)}, bf16[4,256,64]{1,2,0:T(8,128)(2,1)}, u32[]{:S(2)}) %copy-start.5) | copy-done | bytes 131096
  8.7 0.0 copy-start.7
  8.7 0.9 %copy-done.7 = bf16[4,64,256]{2,1,0:T(8,128)(2,1)S(1)} copy-done((bf16[4,64,256]{2,1,0:T(8,128)(2,1)S(1)}, bf16[4,64,256]{2,1,0:T(8,128)(2,1)}, u32[]{:S(2)}) %copy-start.7) | copy-done | bytes 131096
  9.6 0.0 copy-start.6
  9.6 0.0 copy-start.8
  9.6 1.6 %shard_map.110 = (bf16[64,2176]{1,0:T(8,128)(2,1)S(1)}, bf16[64,2176]{1,0:T(8,128)(2,1)S(1)}, bf16[4,192,192]{2,1,0:T(8,128)(2,1)S(1)}, bf16[4,192,192]{2,1,0:T(...) custom-call(s32[16]{0:T(128)S(1)} %copy-done.10, ...), custom_call_target="tpu_custom_call" | custom-call | flops 134217728 | bytes 1048576 | tf_op jit(solution)/shard_map/pallas_call | solution.py:47
  11.2 0.0 collective-permute-done.left_ref
  11.3 0.0 collective-permute-done.1.right_ref
  11.3 0.0 copy-done.6
  11.3 0.0 copy-done.8
  11.3 13.7 %shard_map.112 = (bf16[64,2176]{1,0:T(8,128)(2,1)S(1)}, bf16[64,2176]{1,0:T(8,128)(2,1)S(1)}, bf16[64,2176]{1,0:T(8,128)(2,1)S(1)}, bf16[1152,128]{1,0:T(8,128)(2,1)S(1)}, bf16[1152,128]{1,0:T(8,128)(2,1)S(1)}) custom-call(bf16[64,2176]{1,0:T(8,128)(2,1)S(1)} %get-tuple-element.24.field_ref, bf16[64,2176]{1,0:T(8,128)(2,1)S(1)} %get-tuple-element.25.slope_ref, ...), custom_call_target="tpu_custom_call" | custom-call | flops 8589934592 | bytes 1048576 | tf_op jit(solution)/shard_map/pallas_call | solution.py:47
  25.0 2.7 %collective-permute-start.2 = (bf16[1152,128]{1,0:T(8,128)(2,1)S(1)}, bf16[1152,128]{1,0:T(8,128)(2,1)S(1)}, u32[]{:S(2)}, u32[]{:S(2)}) collective-permute-start(bf16[1152,128]{1,0:T(8,128)(2,1)S(1)} %get-tuple-element.39), channel_id=1, source_target_pairs={{0,8},{8,0},{1,9},{9,1},{2,10},{10,2},{3,11},{11,3},{4,12},{12,4},... | collective-permute-start | bytes 884744 | tf_op jit(solution)/shard_map/ppermute | solution.py:564
  27.7 1.2 %collective-permute-done.2 = bf16[1152,128]{1,0:T(8,128)(2,1)S(1)} collective-permute-done((bf16[1152,128]{1,0:T(8,128)(2,1)S(1)}, bf16[1152,128]{1,0:T(8,128)(2,1)S(1)}, u32[]{:S(2)}, u32[]{:S(2)}) %collective-permute-start.2) | collective-permute-done | bytes 294944 | tf_op jit(solution)/shard_map/ppermute | solution.py:564
  29.0 0.1 add_convert_fusion
  29.0 15.4 %all_to_all.10 = bf16[16,72,128]{2,1,0:T(8,128)(2,1)S(1)} all-to-all(bf16[16,72,128]{2,1,0:T(8,128)(2,1)S(1)} %bitcast.12), channel_id=1, replica_groups=mesh['y'=4,'xl'=2,'core'=2,'ens'=8] {'xl','ens'}, dimensions={0} | all-to-all | bytes 589824 | tf_op jit(solution)/shard_map/all_to_all | solution.py:566
  44.5 0.7 %broadcast_in_dim.14 = bf16[16,72,128]{2,1,0:T(8,128)(2,1)} broadcast(bf16[72,128]{1,0:T(8,128)(2,1)S(1)} %reduce_sum.12), dimensions={1,2} | broadcast | bytes 313344 | tf_op jit(solution)/shard_map/broadcast_in_dim | solution.py:576
  45.2 5.2 %all-to-all-start.1 = ((bf16[16,72,128]{2,1,0:T(8,128)(2,1)}), bf16[16,72,128]{2,1,0:T(8,128)(2,1)S(1)}, u32[]{:S(2)}, u32[]{:S(2)}) async-start(bf16[16,72,128]{2,1,0:T(8,128)(2,1)} %broadcast_in_dim.14), calls=%async_computation.1 | async-start | bytes 589824 | tf_op jit(solution)/shard_map/all_to_all | solution.py:577
  50.4 2.4 %shard_map.113 = (bf16[64,8,256]{2,1,0:T(8,128)(2,1)}, bf16[64,8,256]{2,1,0:T(8,128)(2,1)}) custom-call(s32[16]{0:T(128)S(1)} %copy-done.10, bf16[64,2176]{1,0:T(8,128)(2,1)S(1)} %get-tuple-element.33.flat_ref, bf16[64,2176]{1,0:T(8,128)(2,1)S(1)} %get-tuple-element.34.up_in, bf16[64,2176]{1,0:T(8,128)(2,1)S(1)} %get-tuple-element.35.dh_ref, ...), custom_call_target="tpu_custom_call" | custom-call | flops 1073741824 | bytes 1048576 | tf_op jit(solution)/shard_map/pallas_call | solution.py:47
  52.8 5.1 %all-to-all-done.1.src_ref = bf16[16,72,128]{2,1,0:T(8,128)(2,1)S(1)} async-done(((bf16[16,72,128]{2,1,0:T(8,128)(2,1)}), bf16[16,72,128]{2,1,0:T(8,128)(2,1)S(1)}, u32[]{:S(2)}, u32[]{:S(2)}) %all-to-all-start.1) | async-done | bytes 294944 | tf_op jit(solution)/shard_map/all_to_all | solution.py:577
  57.9 0.7 %shard_map.114 = (f32[4,8,576]{2,1,0:T(8,128)}, f32[4,32,64]{2,1,0:T(8,128)}, f32[4,8,256]{2,1,0:T(8,128)}) custom-call(bf16[16,72,128]{2,1,0:T(8,128)(2,1)S(1)} %all-to-all-done.1.src_ref), custom_call_target="tpu_custom_call" | custom-call | bytes 1048576 | tf_op jit(solution)/shard_map/pallas_call | solution.py:47
  (1 shorter events, 0.0 us)
Async XLA Ops:
  0.6 0.7 %copy-start.10 = (s32[16]{0:T(128)S(1)}, s32[16]{0:T(128)}, u32[]{:S(2)}) copy-start(s32[16]{0:T(128)} %orient_ref.5) | copy-start | bytes 196
  1.3 0.9 %copy-start = (bf16[1,64,8,256]{3,2,1,0:T(8,128)(2,1)S(1)}, bf16[1,64,8,256]{3,2,1,0:T(8,128)(2,1)}, u32[]{:S(2)}) copy-start(bf16[1,64,8,256]{3,2,1,0:T(8,128)(2,1)} %param.7) | copy-start | bytes 786436
  2.2 0.9 %copy-start.2 = (bf16[1,64,8,256]{3,2,1,0:T(8,128)(2,1)S(1)}, bf16[1,64,8,256]{3,2,1,0:T(8,128)(2,1)}, u32[]{:S(2)}) copy-start(bf16[1,64,8,256]{3,2,1,0:T(8,128)(2,1)} %param.8) | copy-start | bytes 786436
  3.2 3.6 %copy-start.1 = (bf16[1,64,8,256]{3,2,1,0:T(8,128)(2,1)S(1)}, bf16[1,64,8,256]{3,2,1,0:T(8,128)(2,1)}, u32[]{:S(2)}) copy-start(bf16[1,64,8,256]{3,2,1,0:T(8,128)(2,1)} %param.7) | copy-start | bytes 786436
  3.2 3.6 %copy-start.3 = (bf16[1,64,8,256]{3,2,1,0:T(8,128)(2,1)S(1)}, bf16[1,64,8,256]{3,2,1,0:T(8,128)(2,1)}, u32[]{:S(2)}) copy-start(bf16[1,64,8,256]{3,2,1,0:T(8,128)(2,1)} %param.8) | copy-start | bytes 786436
  4.1 2.7 %copy-start.9 = (f32[4,256]{1,0:T(4,128)S(1)}, f32[4,256]{1,0:T(4,128)}, u32[]{:S(2)}) copy-start(f32[4,256]{1,0:T(4,128)} %bias_ref.1) | copy-start | bytes 12292
  4.1 7.1 %collective-permute-start = (bf16[64,128]{1,0:T(8,128)(2,1)S(1)}, bf16[64,128]{1,0:T(8,128)(2,1)S(1)}, u32[]{:S(2)}, u32[]{:S(2)}) collective-permute-start(bf16[64,128]{1,0:T(8,128)(2,1)S(1)} %get-tuple-element.26), channel_id=1, source_target_pairs={{0,8},{8,16},{16,24},{24,32},{32,40},{40,48},{48,56},{56,64},{64,7... | collective-permute-start | bytes 49160 | tf_op jit(solution)/shard_map/ppermute | solution.py:510
  6.8 4.5 %collective-permute-start.1 = (bf16[64,128]{1,0:T(8,128)(2,1)S(1)}, bf16[64,128]{1,0:T(8,128)(2,1)S(1)}, u32[]{:S(2)}, u32[]{:S(2)}) collective-permute-start(bf16[64,128]{1,0:T(8,128)(2,1)S(1)} %get-tuple-element.27), channel_id=1, source_target_pairs={{8,0},{16,8},{24,16},{32,24},{40,32},{48,40},{56,48},{64,56},{72,6... | collective-permute-start | bytes 49160 | tf_op jit(solution)/shard_map/ppermute | solution.py:511
  6.8 1.0 %copy-start.4 = (bf16[4,64,576]{2,1,0:T(8,128)(2,1)S(1)}, bf16[4,64,576]{2,1,0:T(8,128)(2,1)}, u32[]{:S(2)}) copy-start(bf16[4,64,576]{2,1,0:T(8,128)(2,1)} %kernel_ref.1) | copy-start | bytes 884740
  7.8 0.9 %copy-start.5 = (bf16[4,256,64]{1,2,0:T(8,128)(2,1)S(1)}, bf16[4,256,64]{1,2,0:T(8,128)(2,1)}, u32[]{:S(2)}) copy-start(bf16[4,256,64]{1,2,0:T(8,128)(2,1)} %param.10) | copy-start | bytes 393220
  8.7 0.9 %copy-start.7 = (bf16[4,64,256]{2,1,0:T(8,128)(2,1)S(1)}, bf16[4,64,256]{2,1,0:T(8,128)(2,1)}, u32[]{:S(2)}) copy-start(bf16[4,64,256]{2,1,0:T(8,128)(2,1)} %project_ref.3) | copy-start | bytes 393220
  9.6 1.7 %copy-start.6 = (bf16[4,256,64]{1,2,0:T(8,128)(2,1)S(1)}, bf16[4,256,64]{1,2,0:T(8,128)(2,1)}, u32[]{:S(2)}) copy-start(bf16[4,256,64]{1,2,0:T(8,128)(2,1)} %param.10) | copy-start | bytes 393220
  9.6 1.7 %copy-start.8 = (bf16[4,64,256]{2,1,0:T(8,128)(2,1)S(1)}, bf16[4,64,256]{2,1,0:T(8,128)(2,1)}, u32[]{:S(2)}) copy-start(bf16[4,64,256]{2,1,0:T(8,128)(2,1)} %project_ref.3) | copy-start | bytes 393220
  25.0 4.0 %collective-permute-start.2 = (bf16[1152,128]{1,0:T(8,128)(2,1)S(1)}, bf16[1152,128]{1,0:T(8,128)(2,1)S(1)}, u32[]{:S(2)}, u32[]{:S(2)}) collective-permute-start(bf16[1152,128]{1,0:T(8,128)(2,1)S(1)} %get-tuple-element.39), channel_id=1, source_target_pairs={{0,8},{8,0},{1,9},{9,1},{2,10},{10,2},{3,11},{11,3},{4,12},{12,4},... | collective-permute-start | bytes 884744 | tf_op jit(solution)/shard_map/ppermute | solution.py:564
  45.2 12.7 %all-to-all-start.1 = ((bf16[16,72,128]{2,1,0:T(8,128)(2,1)}), bf16[16,72,128]{2,1,0:T(8,128)(2,1)S(1)}, u32[]{:S(2)}, u32[]{:S(2)}) async-start(bf16[16,72,128]{2,1,0:T(8,128)(2,1)} %broadcast_in_dim.14), calls=%async_computation.1 | async-start | bytes 589824 | tf_op jit(solution)/shard_map/all_to_all | solution.py:577

commit v4 on v3

--- a/solution.py
+++ b/solution.py
@@ -7,6 +7,7 @@
 from jax.sharding import PartitionSpec as P
 
 BF = jnp.bfloat16
+VM = pltpu.VMEM
 F32 = jnp.float32
 SQRT_HALF = 0.7071067811865476
 INV_ROOT_TAU = 0.3989422804014327
@@ -23,10 +24,13 @@
 HALVES = WD // 128
 TILES = N // 128
 UNITS = 72
+BIAS_ROWS = 16
 CHUNKS = [(s, min(256, N - s)) for s in range(0, N, 256)]
-FORWARD_LAG = 7
+FORWARD_LAG = 8
 BACKWARD_LAG = 8
-TURN = 6
+TURN = 7
+
+
 LON = ("y", "xl", "core")
 
 NT = (((1,), (1,)), ((), ()))
@@ -41,9 +45,7 @@
 
 
 def call(body, outs, ins, scratch=(), flops=0, mib=8):
-    specs = [
-        pl.BlockSpec(memory_space=pltpu.SMEM if scalar else pltpu.VMEM) for _, scalar in ins
-    ]
+    specs = [pl.BlockSpec(memory_space=space) for _, space in ins]
     return pl.pallas_call(
         body,
         out_shape=outs,
@@ -65,19 +67,26 @@
         wide[half] = part.astype(F32).reshape(C * H, 128)
 
 
-def own_flip(orient_ref):
-    sector = (lax.axis_index("y") * 2 + lax.axis_index("xl")) * 2 + lax.axis_index("core")
-    return orient_ref[sector]
-
-
 def stored_row(flip, row):
     return jnp.where(flip == 1, H - 1 - row, row)
 
 
-def edge_kernel(orient_ref, field_ref, slope_ref, low_ref, high_ref, wide_f, wide_g):
-    flip = own_flip(orient_ref)
-    spread(wide_f, field_ref)
-    spread(wide_g, slope_ref)
+def edge_kernel(*refs):
+    orient_in, *sources = refs[0:7]
+    low_ref, high_ref, flag_ref, *targets = refs[7:16]
+    wide_f, wide_g, orient_s, sems = refs[16:20]
+    copies = [pltpu.make_async_copy(orient_in, orient_s, sems.at[0])]
+    for i, (source, target) in enumerate(zip(sources, targets)):
+        copies.append(pltpu.make_async_copy(source, target, sems.at[i + 1]))
+    for copy in copies:
+        copy.start()
+    for copy in copies[0:3]:
+        copy.wait()
+    sector = (lax.axis_index("y") * 2 + lax.axis_index("xl")) * 2 + lax.axis_index("core")
+    flip = orient_s[sector]
+    flag_ref[...] = jnp.full((8, 128), flip, jnp.int32)
+    spread(wide_f, targets[0])
+    spread(wide_g, targets[1])
     lane = lax.broadcasted_iota(jnp.int32, (C, 128), 1)
     low = jnp.zeros((C, 128), F32)
     high = jnp.zeros((C, 128), F32)
@@ -92,6 +101,8 @@
             high = jnp.where(inside, pltpu.roll(last, (at + 8) % 128, axis=1), high)
     low_ref[...] = low.astype(BF)
     high_ref[...] = high.astype(BF)
+    for copy in copies[3:]:
+        copy.wait()
 
 
 def flatten(ref, wide, flip):
@@ -118,7 +129,7 @@
 
 
 def prep_kernel(
-    orient_ref,
+    flag_ref,
     field_ref,
     slope_ref,
     kernel_ref,
@@ -130,13 +141,14 @@
     conv_out,
     convt_out,
     expand_out,
+    project_out,
     projectt_out,
-    bias_out,
     wide,
 ):
-    flip = own_flip(orient_ref)
+    flip = flag_ref[0, 0]
     field_out[...] = flatten(field_ref, wide, flip).astype(BF)
     slope_out[...] = flatten(slope_ref, wide, flip).astype(BF)
+    lane = lax.broadcasted_iota(jnp.int32, (HID, 128), 1)
     for b in range(DEPTH):
         taps = kernel_ref[b]
         turned = taps.astype(F32).T
@@ -147,9 +159,16 @@
             convt_out[b, here, :] = jnp.concatenate(
                 [turned[a : a + C, :] for a in at], axis=1
             ).astype(BF)
-        expand_out[b] = expandt_ref[b].astype(F32).T.astype(BF)
-        projectt_out[b] = project_ref[b].astype(F32).T.astype(BF)
-        bias_out[b] = jnp.broadcast_to(bias_ref[b : b + 1, :], (128, HID)).T
+        bias = jnp.broadcast_to(bias_ref[b : b + 1, :], (128, HID)).T
+        high = bias.astype(BF).astype(F32)
+        middle = (bias - high).astype(BF).astype(F32)
+        low = bias - high - middle
+        parts = jnp.where(lane == 0, high, jnp.where(lane == 1, middle, jnp.where(lane == 2, low, 0.0)))
+        weight = jnp.concatenate([expandt_ref[b].astype(F32).T, parts[:, 0:BIAS_ROWS]], axis=1)
+        expand_out[b] = weight.astype(BF)
+        half = 0.5 * project_ref[b].astype(F32)
+        project_out[b] = half.astype(BF)
+        projectt_out[b] = half.T.astype(BF)
 
 
 def add_halo(flat_ref, left, right):
@@ -255,7 +274,7 @@
 
 
 def forward_stages(
-    b, out_ref, stack_s, wide_s, hid_s, active_s, slope_s, conv_ref, expand_ref, bias_ref, project_ref
+    b, out_ref, stack_s, wide_s, hid_s, active_s, slope_s, conv_ref, expand_ref, project_ref, inner_s
 ):
     stack = make_row_stack(out_ref, stack_s.at[b], 1)
     moved = make_neighbours(
@@ -272,23 +291,26 @@
     def hidden(i):
         for t in TILE_SETS[i]:
             low, high = moved(t)
-            hid_s[b, :, span(t)] = (low + tile(wide_s, t, slice(C, 2 * C)) + high).astype(BF)
+            hid_s[b, 0:C, span(t)] = (low + tile(wide_s, t, slice(C, 2 * C)) + high).astype(BF)
 
     def expand(i):
         cut = CUTS[i]
-        bias = jnp.concatenate([bias_ref[b]] * len(TILE_SETS[i]), axis=1)
-        inner = mm(expand_ref[b], hid_s[b, :, cut]) + bias
-        half = 0.5 + 0.5 * lax.erf(inner * SQRT_HALF)
+        inner_s[:, cut] = mm(expand_ref[b], hid_s[b, :, cut])
+
+    def gelu(i):
+        cut = CUTS[i]
+        inner = inner_s[:, cut]
+        twice = 1.0 + lax.erf(inner * SQRT_HALF)
         bell = jnp.exp2((inner * inner) * -HALF_LOG2E)
-        slope_s[b, :, cut] = (half + (inner * INV_ROOT_TAU) * bell).astype(BF)
-        active_s[b, :, cut] = (inner * half).astype(BF)
+        slope_s[b, :, cut] = (twice + (inner * (2.0 * INV_ROOT_TAU)) * bell).astype(BF)
+        active_s[b, :, cut] = (inner * twice).astype(BF)
 
     def project(i):
         cut = CUTS[i]
         old = stack_s[b, C : 2 * C, cut].astype(F32)
         out_ref[:, cut] = (old + mm(project_ref[b], active_s[b, :, cut])).astype(BF)
 
-    return [(stacks, 0), (conv, 1), (hidden, 2), (expand, 3), (project, 4)]
+    return [(gelu, 4), (hidden, 3), (stacks, 0), (conv, 1), (expand, 3), (project, 5)]
 
 
 def backward_stages(
@@ -310,8 +332,7 @@
         cut = CUTS[i]
         up = up_ref[:, cut]
         d_active = mm(projectt_ref[b], up)
-        d_inner = (d_active * slope_s[b, :, cut].astype(F32)).astype(BF)
-        din_s[:, cut] = d_inner
+        din_s[:, cut] = (d_active * slope_s[b, :, cut].astype(F32)).astype(BF)
         pg.append(mm_nt(up * mask_s[:, cut], active_s[b, :, cut]))
 
     def hidden(i):
@@ -320,7 +341,7 @@
         d_hidden = mm(expandt_ref[b], d_inner).astype(BF)
         dh_ref[:, cut] = d_hidden
         own_s[C : 2 * C, cut] = d_hidden * mask_s[:, cut]
-        eg.append(mm_nt(d_inner, hid_s[b, :, cut] * mask_s[:, cut]))
+        eg.append(mm_nt(d_inner, hid_s[b, 0:C, cut] * mask_s[:, cut]))
 
     def shares(i):
         for t in TILE_SETS[i]:
@@ -343,7 +364,7 @@
             up_ref[:, span(t)] = total.astype(BF)
 
     def finish():
-        sums[b] = (sum(cg[1:], cg[0]), sum(eg[1:], eg[0]), sum(pg[1:], pg[0]))
+        sums[b] = (sum(cg[1:], cg[0]), sum(eg[1:], eg[0]), 0.5 * sum(pg[1:], pg[0]))
 
     stages = [(inner, 0), (hidden, 1), (shares, 3)]
     if b > 0:
@@ -372,7 +393,6 @@
     convt_ref,
     expand_ref,
     expandt_ref,
-    bias_ref,
     project_ref,
     projectt_ref,
     out_ref,
@@ -390,6 +410,7 @@
     own_s,
     din_s,
     mask_s,
+    inner_s,
 ):
     core = lax.axis_index("core")
     lane = lax.broadcasted_iota(jnp.int32, (C, N), 1)
@@ -407,6 +428,9 @@
     add_halo(up_ref, pltpu.roll(left, 120, axis=1), right)
 
     mask_s[...] = mask
+    bias_row = lax.broadcasted_iota(jnp.int32, (BIAS_ROWS, N), 0)
+    for b in range(DEPTH):
+        hid_s[b, C : C + BIAS_ROWS, :] = jnp.where(bias_row < 3, 1.0, 0.0).astype(BF)
     wide_s[:, N - 128 : N] = jnp.zeros((3 * C, 128), F32)
     own_s[C : 2 * C, N - 128 : N] = jnp.zeros((C, 128), BF)
     jobs = []
@@ -414,7 +438,7 @@
     for b in range(DEPTH):
         stages = forward_stages(
             b, out_ref, stack_s, wide_s, hid_s, active_s, slope_s,
-            conv_ref, expand_ref, bias_ref, project_ref,
+            conv_ref, expand_ref, project_ref, inner_s,
         )
         jobs.append((first, stages, None))
         first += FORWARD_LAG
@@ -450,9 +474,9 @@
 
 
 def tail_kernel(
-    orient_ref, flat_ref, up_in, dh_ref, convt_ref, out_ref, grad_ref, wide, up_s, rstack_s, wide_s
+    flag_ref, flat_ref, up_in, dh_ref, convt_ref, out_ref, grad_ref, wide, up_s, rstack_s, wide_s
 ):
-    flip = own_flip(orient_ref)
+    flip = flag_ref[0, 0]
     lane = lax.broadcasted_iota(jnp.int32, (C, N), 1)
     up_s[...] = up_in[...]
     step_back(up_s, dh_ref, convt_ref[0], rstack_s, wide_s, lane)
@@ -483,7 +507,7 @@
 def main_scratch():
     return [
         pltpu.VMEM((DEPTH, 3 * C, N), BF),
-        pltpu.VMEM((DEPTH, C, N), BF),
+        pltpu.VMEM((DEPTH, C + BIAS_ROWS, N), BF),
         pltpu.VMEM((DEPTH, HID, N), BF),
         pltpu.VMEM((DEPTH, HID, N), BF),
         pltpu.VMEM((3 * C, N), F32),
@@ -492,6 +516,7 @@
         pltpu.VMEM((3 * C, N), BF),
         pltpu.VMEM((HID, N), BF),
         pltpu.VMEM((C, N), BF),
+        pltpu.VMEM((HID, N), F32),
     ]
 
 
@@ -499,37 +524,38 @@
     field = members_in[0]
     slope = cotangent[0]
     wide = pltpu.VMEM((HALVES, C * H, 128), F32)
-    low, high = call(
+    sources = [field, slope, conv_weight, expand_weight.transpose(0, 2, 1), expand_bias, project_weight]
+    low, high, flag, field, slope, taps, expandt, bias, weight = call(
         edge_kernel,
-        [shape(C, 128)] * 2,
-        [(orient, True), (field, False), (slope, False)],
-        [wide, wide],
-        mib=12,
+        [shape(C, 128), shape(C, 128), shape(8, 128, dtype=jnp.int32)]
+        + [shape(*array.shape, dtype=array.dtype) for array in sources],
+        [(pltpu.with_memory_space_constraint(array, pltpu.HBM), pl.ANY) for array in [orient] + sources],
+        [wide, wide, pltpu.SMEM((16,), jnp.int32), pltpu.SemaphoreType.DMA((7,))],
+        mib=8,
     )
     count = lax.axis_size(LON)
     left = lax.ppermute(high, LON, [(i, (i + 1) % count) for i in range(count)])
     right = lax.ppermute(low, LON, [((i + 1) % count, i) for i in range(count)])
 
-    expandt = expand_weight.transpose(0, 2, 1)
-    flat_f, flat_g, conv, convt, expand, projectt, bias = call(
+    flat_f, flat_g, conv, convt, expand, project, projectt = call(
         prep_kernel,
         [
             shape(C, N),
             shape(C, N),
             shape(DEPTH, 3 * C, 3 * C),
             shape(DEPTH, 3 * C, 3 * C),
+            shape(DEPTH, HID, C + BIAS_ROWS),
+            shape(DEPTH, C, HID),
             shape(DEPTH, HID, C),
-            shape(DEPTH, HID, C),
-            shape(DEPTH, HID, 128, dtype=F32),
         ],
         [
-            (orient, True),
-            (field, False),
-            (slope, False),
-            (conv_weight, False),
-            (expandt, False),
-            (expand_bias, False),
-            (project_weight, False),
+            (flag, VM),
+            (field, VM),
+            (slope, VM),
+            (taps, VM),
+            (expandt, VM),
+            (bias, VM),
+            (weight, VM),
         ],
         [wide],
         flops=1 << 27,
@@ -545,17 +571,16 @@
             shape(16 * UNITS, 128),
         ],
         [
-            (flat_f, False),
-            (flat_g, False),
-            (left, False),
-            (right, False),
-            (conv, False),
-            (convt, False),
-            (expand, False),
-            (expandt, False),
-            (bias, False),
-            (project_weight, False),
-            (projectt, False),
+            (flat_f, VM),
+            (flat_g, VM),
+            (left, VM),
+            (right, VM),
+            (conv, VM),
+            (convt, VM),
+            (expand, VM),
+            (expandt, VM),
+            (project, VM),
+            (projectt, VM),
         ],
         main_scratch(),
         flops=1 << 33,
@@ -567,7 +592,7 @@
     section_out, input_grad = call(
         tail_kernel,
         [shape(C, H, WD)] * 2,
-        [(orient, True), (flat_out, False), (up, False), (d_hidden, False), (convt, False)],
+        [(flag, VM), (flat_out, VM), (up, VM), (d_hidden, VM), (convt, VM)],
         [wide, pltpu.VMEM((C, N), BF), pltpu.VMEM((3 * C, N), BF), pltpu.VMEM((3 * C, N), F32)],
         flops=1 << 30,
         mib=16,
@@ -582,7 +607,7 @@
             shape(DEPTH, 32, C, dtype=F32),
             shape(DEPTH, 8, HID, dtype=F32),
         ],
-        [(parts, False)],
+        [(parts, VM)],
     )
     return section_out[None], input_grad[None], conv_grad, expand_grad, project_grad
 

time: 59 us -> 54.3 us (0.920)
  local copies, waits for them, and re-layouts: 6.09 us -> 0.75 us
  waiting for transfers between devices: 6.29 us -> 9.06 us
  starting transfers between devices: 10.6 us -> 9.07 us
  Pallas kernels: 19.4 us -> 18.3 us
  blocking collectives: 15.4 us -> 16.1 us
    unnamed x22 -> x0, local copies, waits for them, and re-layouts: 5.34 us -> none
    ppermute x1, waiting for transfers between devices: 0.01 us -> 2.29 us  [local(): right = lax.ppermute(low, LON, [((i + 1) % count, i) for i in range(count)])]
    ppermute x1, starting transfers between devices: 2.75 us -> 0.73 us  [local(): came = lax.ppermute(other, 'core', [(0, 1), (1, 0)])]
    pallas_call x5, Pallas kernels: 19.4 us -> 18.3 us  [call(): pl.pallas_call(body, out_shape=outs, in_specs=specs, out_specs=jax.tree.m...]
    all_to_all x1, blocking collectives: 15.4 us -> 16.1 us  [local(): lax.all_to_all(share.reshape(16, UNITS, 128), ('xl', 'ens'), 0, 0, tiled=...]
  transfers between devices with their start and end apart: 4 -> 4, of which waited for: 2 -> 3; matrix products, arithmetic and copies ran while one was open for 0% -> 0% of each run, Pallas kernels for 7% -> 6%
where the time goes in v4:
time: 54.3 us; the launch traced here: 54.1 us
  Pallas kernels  18.3 us (34%)
  blocking collectives  16.1 us (30%)
  starting transfers between devices  9.07 us (17%)
  waiting for transfers between devices  9.06 us (17%)
  local copies, waits for them, and re-layouts  0.75 us (1%)
  between operations  0.67 us (1%)
    pallas_call x5, Pallas kernels, call(): pl.pallas_call(body, out_shape=outs, in_specs=specs, out_specs=jax.tree.m...  18.3 us
    all_to_all x1, blocking collectives, local(): lax.all_to_all(share.reshape(16, UNITS, 128), ('xl', 'ens'), 0, 0, tiled=...  16.1 us
    all_to_all x1, starting transfers between devices, local(): parts = lax.all_to_all(parts, LON, 0, 0, tiled=True)  5.66 us
    all_to_all x1, waiting for transfers between devices, local(): parts = lax.all_to_all(parts, LON, 0, 0, tiled=True)  5.55 us
    ppermute x1, starting transfers between devices, local(): left = lax.ppermute(high, LON, [(i, (i + 1) % count) for i in range(count)])  2.67 us
    ppermute x1, waiting for transfers between devices, local(): right = lax.ppermute(low, LON, [((i + 1) % count, i) for i in range(count)])  2.29 us
    ppermute x1, waiting for transfers between devices, local(): came = lax.ppermute(other, 'core', [(0, 1), (1, 0)])  1.21 us
  transfers between devices with their start and end apart: 4, of which 3 were waited for; matrix products, arithmetic and copies ran while one was open for 0% of the time, Pallas kernels for 6%

profile of v4, /device:TPU:1, one launch (start us, length us, event | category | flops | bytes accessed | tf_op | source)
XLA Modules:
  0.0 54.1 jit_solution(12542284394355022795)
XLA Ops:
  0.6 1.5 %shard_map.110 = (bf16[64,128]{1,0:T(8,128)(2,1)S(1)}, bf16[64,128]{1,0:T(8,128)(2,1)S(1)}, s32[8,128]{1,0:T(8,128)S(1)}, bf16[64,8,256]{2,1,0:T(8,128)(2,1)S(1)...) custom-call(s32[16]{0:T(128)} %refs_0_.1, ...), custom_call_target="tpu_custom_call" | custom-call | bytes 1048576 | tf_op jit(solution)/shard_map/pallas_call | solution.py:49
  2.1 2.7 %collective-permute-start = (bf16[64,128]{1,0:T(8,128)(2,1)S(1)}, bf16[64,128]{1,0:T(8,128)(2,1)S(1)}, u32[]{:S(2)}, u32[]{:S(2)}) collective-permute-start(bf16[64,128]{1,0:T(8,128)(2,1)S(1)} %get-tuple-element.40), channel_id=1, source_target_pairs={{0,8},{8,16},{16,24},{24,32},{32,40},{40,48},{48,56},{56,64},{64,7... | collective-permute-start | bytes 49160 | tf_op jit(solution)/shard_map/ppermute | solution.py:537
  4.8 0.0 collective-permute-start.1
  4.8 1.1 %shard_map.111 = (bf16[64,2176]{1,0:T(8,128)(2,1)S(1)}, bf16[64,2176]{1,0:T(8,128)(2,1)S(1)}, bf16[4,192,192]{2,1,0:T(8,128)(2,1)S(1)}, bf16[4,192,192]{2,1,0:T(...) custom-call(s32[8,128]{1,0:T(8,128)S(1)} %get-tuple-element.31.flag_, ...), custom_call_target="tpu_custom_call" | custom-call | flops 134217728 | bytes 1048576 | tf_op jit(solution)/shard_map/pallas_call | solution.py:49
  6.0 0.0 collective-permute-done.left_ref
  6.0 2.3 %collective-permute-done.1.right_ref = bf16[64,128]{1,0:T(8,128)(2,1)S(1)} collective-permute-done((bf16[64,128]{1,0:T(8,128)(2,1)S(1)}, bf16[64,128]{1,0:T(8,128)(2,1)S(1)}, u32[]{:S(2)}, u32[]{:S(2)}) %collective-permute-start.1) | collective-permute-done | bytes 16416 | tf_op jit(solution)/shard_map/ppermute | solution.py:538
  8.3 13.0 %shard_map.112 = (bf16[64,2176]{1,0:T(8,128)(2,1)S(1)}, bf16[64,2176]{1,0:T(8,128)(2,1)S(1)}, bf16[64,2176]{1,0:T(8,128)(2,1)S(1)}, bf16[1152,128]{1,0:T(8,128)(2,1)S(1)}, bf16[1152,128]{1,0:T(8,128)(2,1)S(1)}) custom-call(bf16[64,2176]{1,0:T(8,128)(2,1)S(1)} %get-tuple-element.38.field_ref, bf16[64,2176]{1,0:T(8,128)(2,1)S(1)} %get-tuple-element.39.slope_ref, ...), custom_call_target="tpu_custom_call" | custom-call | flops 8589934592 | bytes 1048576 | tf_op jit(solution)/shard_map/pallas_call | solution.py:49
  21.3 0.7 %collective-permute-start.2 = (bf16[1152,128]{1,0:T(8,128)(2,1)S(1)}, bf16[1152,128]{1,0:T(8,128)(2,1)S(1)}, u32[]{:S(2)}, u32[]{:S(2)}) collective-permute-start(bf16[1152,128]{1,0:T(8,128)(2,1)S(1)} %get-tuple-element.53), channel_id=1, source_target_pairs={{0,8},{8,0},{1,9},{9,1},{2,10},{10,2},{3,11},{11,3},{4,12},{12,4},... | collective-permute-start | bytes 884744 | tf_op jit(solution)/shard_map/ppermute | solution.py:589
  22.1 1.2 %collective-permute-done.2 = bf16[1152,128]{1,0:T(8,128)(2,1)S(1)} collective-permute-done((bf16[1152,128]{1,0:T(8,128)(2,1)S(1)}, bf16[1152,128]{1,0:T(8,128)(2,1)S(1)}, u32[]{:S(2)}, u32[]{:S(2)}) %collective-permute-start.2) | collective-permute-done | bytes 294944 | tf_op jit(solution)/shard_map/ppermute | solution.py:589
  23.3 0.1 add_convert_fusion
  23.4 16.1 %all_to_all.10 = bf16[16,72,128]{2,1,0:T(8,128)(2,1)S(1)} all-to-all(bf16[16,72,128]{2,1,0:T(8,128)(2,1)S(1)} %bitcast.6), channel_id=1, replica_groups=mesh['y'=4,'xl'=2,'core'=2,'ens'=8] {'xl','ens'}, dimensions={0} | all-to-all | bytes 589824 | tf_op jit(solution)/shard_map/all_to_all | solution.py:591
  39.5 0.7 %broadcast_in_dim.14 = bf16[16,72,128]{2,1,0:T(8,128)(2,1)} broadcast(bf16[72,128]{1,0:T(8,128)(2,1)S(1)} %reduce_sum.12), dimensions={1,2} | broadcast | bytes 313344 | tf_op jit(solution)/shard_map/broadcast_in_dim | solution.py:601
  40.3 5.7 %all-to-all-start.1 = ((bf16[16,72,128]{2,1,0:T(8,128)(2,1)}), bf16[16,72,128]{2,1,0:T(8,128)(2,1)S(1)}, u32[]{:S(2)}, u32[]{:S(2)}) async-start(bf16[16,72,128]{2,1,0:T(8,128)(2,1)} %broadcast_in_dim.14), calls=%async_computation.1 | async-start | bytes 589824 | tf_op jit(solution)/shard_map/all_to_all | solution.py:602
  45.9 1.8 %shard_map.113 = (bf16[64,8,256]{2,1,0:T(8,128)(2,1)}, bf16[64,8,256]{2,1,0:T(8,128)(2,1)}) custom-call(s32[8,128]{1,0:T(8,128)S(1)} %get-tuple-element.31.flag_ref, bf16[64,2176]{1,0:T(8,128)(2,1)S(1)} %get-tuple-element.47.flat_ref, bf16[64,2176]{1,0:T(8,128)(2,1)S(1)} %get-tuple-element.48.up_in, bf16[64,2176]{1,0:T(8,128)(2,1)S(1)} %get-tuple-element.49.dh_ref, ...), custom_call_target="tpu_custom_call" | custom-call | flops 1073741824 | bytes 1048576 | tf_op jit(solution)/shard_map/pallas_call | solution.py:49
  47.8 5.6 %all-to-all-done.1.src_ref = bf16[16,72,128]{2,1,0:T(8,128)(2,1)S(1)} async-done(((bf16[16,72,128]{2,1,0:T(8,128)(2,1)}), bf16[16,72,128]{2,1,0:T(8,128)(2,1)S(1)}, u32[]{:S(2)}, u32[]{:S(2)}) %all-to-all-start.1) | async-done | bytes 294944 | tf_op jit(solution)/shard_map/all_to_all | solution.py:602
  53.3 0.7 %shard_map.114 = (f32[4,8,576]{2,1,0:T(8,128)}, f32[4,32,64]{2,1,0:T(8,128)}, f32[4,8,256]{2,1,0:T(8,128)}) custom-call(bf16[16,72,128]{2,1,0:T(8,128)(2,1)S(1)} %all-to-all-done.1.src_ref), custom_call_target="tpu_custom_call" | custom-call | bytes 1048576 | tf_op jit(solution)/shard_map/pallas_call | solution.py:49
  (1 shorter events, 0.0 us)
Async XLA Ops:
  2.1 3.8 %collective-permute-start = (bf16[64,128]{1,0:T(8,128)(2,1)S(1)}, bf16[64,128]{1,0:T(8,128)(2,1)S(1)}, u32[]{:S(2)}, u32[]{:S(2)}) collective-permute-start(bf16[64,128]{1,0:T(8,128)(2,1)S(1)} %get-tuple-element.40), channel_id=1, source_target_pairs={{0,8},{8,16},{16,24},{24,32},{32,40},{40,48},{48,56},{56,64},{64,7... | collective-permute-start | bytes 49160 | tf_op jit(solution)/shard_map/ppermute | solution.py:537
  4.8 3.5 %collective-permute-start.1 = (bf16[64,128]{1,0:T(8,128)(2,1)S(1)}, bf16[64,128]{1,0:T(8,128)(2,1)S(1)}, u32[]{:S(2)}, u32[]{:S(2)}) collective-permute-start(bf16[64,128]{1,0:T(8,128)(2,1)S(1)} %get-tuple-element.41), channel_id=1, source_target_pairs={{8,0},{16,8},{24,16},{32,24},{40,32},{48,40},{56,48},{64,56},{72,6... | collective-permute-start | bytes 49160 | tf_op jit(solution)/shard_map/ppermute | solution.py:538
  21.3 1.9 %collective-permute-start.2 = (bf16[1152,128]{1,0:T(8,128)(2,1)S(1)}, bf16[1152,128]{1,0:T(8,128)(2,1)S(1)}, u32[]{:S(2)}, u32[]{:S(2)}) collective-permute-start(bf16[1152,128]{1,0:T(8,128)(2,1)S(1)} %get-tuple-element.53), channel_id=1, source_target_pairs={{0,8},{8,0},{1,9},{9,1},{2,10},{10,2},{3,11},{11,3},{4,12},{12,4},... | collective-permute-start | bytes 884744 | tf_op jit(solution)/shard_map/ppermute | solution.py:589
  40.3 13.1 %all-to-all-start.1 = ((bf16[16,72,128]{2,1,0:T(8,128)(2,1)}), bf16[16,72,128]{2,1,0:T(8,128)(2,1)S(1)}, u32[]{:S(2)}, u32[]{:S(2)}) async-start(bf16[16,72,128]{2,1,0:T(8,128)(2,1)} %broadcast_in_dim.14), calls=%async_computation.1 | async-start | bytes 589824 | tf_op jit(solution)/shard_map/all_to_all | solution.py:602

commit v5 on v4

--- a/solution.py
+++ b/solution.py
@@ -26,9 +26,9 @@
 UNITS = 72
 BIAS_ROWS = 16
 CHUNKS = [(s, min(256, N - s)) for s in range(0, N, 256)]
-FORWARD_LAG = 8
+FORWARD_LAG = 9
 BACKWARD_LAG = 8
-TURN = 7
+TURN = 8
 
 
 LON = ("y", "xl", "core")
@@ -73,7 +73,7 @@
 
 def edge_kernel(*refs):
     orient_in, *sources = refs[0:7]
-    low_ref, high_ref, flag_ref, *targets = refs[7:16]
+    inner_ref, outer_ref, flag_ref, *targets = refs[7:16]
     wide_f, wide_g, orient_s, sems = refs[16:20]
     copies = [pltpu.make_async_copy(orient_in, orient_s, sems.at[0])]
     for i, (source, target) in enumerate(zip(sources, targets)):
@@ -99,8 +99,9 @@
             last = wide[HALVES - 1, pl.ds(stored, C, stride=H), :]
             low = jnp.where(inside, pltpu.roll(first, at, axis=1), low)
             high = jnp.where(inside, pltpu.roll(last, (at + 8) % 128, axis=1), high)
-    low_ref[...] = low.astype(BF)
-    high_ref[...] = high.astype(BF)
+    first = lax.axis_index("core") == 0
+    inner_ref[...] = jnp.where(first, high, low).astype(BF)
+    outer_ref[...] = jnp.where(first, low, high).astype(BF)
     for copy in copies[3:]:
         copy.wait()
 
@@ -143,11 +144,19 @@
     expand_out,
     project_out,
     projectt_out,
+    mask_out,
     wide,
 ):
     flip = flag_ref[0, 0]
     field_out[...] = flatten(field_ref, wide, flip).astype(BF)
     slope_out[...] = flatten(slope_ref, wide, flip).astype(BF)
+    lane = lax.broadcasted_iota(jnp.int32, (16, N), 1)
+    column = lane
+    for row in range(1, H):
+        column = jnp.where(lane >= row * PITCH, lane - row * PITCH, column)
+    mask = jnp.where((column >= HALO) & (column < HALO + WD), 1.0, 0.0).astype(BF)
+    for k in range(0, C, 16):
+        mask_out[k : k + 16, :] = mask
     lane = lax.broadcasted_iota(jnp.int32, (HID, 128), 1)
     for b in range(DEPTH):
         taps = kernel_ref[b]
@@ -310,7 +319,7 @@
         old = stack_s[b, C : 2 * C, cut].astype(F32)
         out_ref[:, cut] = (old + mm(project_ref[b], active_s[b, :, cut])).astype(BF)
 
-    return [(gelu, 4), (hidden, 3), (stacks, 0), (conv, 1), (expand, 3), (project, 5)]
+    return [(conv, 1), (gelu, 5), (expand, 4), (hidden, 3), (project, 6), (stacks, 0)]
 
 
 def backward_stages(
@@ -387,14 +396,15 @@
 def main_kernel(
     field_ref,
     slope_ref,
-    left_ref,
-    right_ref,
+    inner_ref,
+    outer_ref,
     conv_ref,
     convt_ref,
     expand_ref,
     expandt_ref,
     project_ref,
     projectt_ref,
+    mask_s,
     out_ref,
     up_ref,
     dh_ref,
@@ -409,25 +419,19 @@
     share_s,
     own_s,
     din_s,
-    mask_s,
     inner_s,
 ):
     core = lax.axis_index("core")
-    lane = lax.broadcasted_iota(jnp.int32, (C, N), 1)
-    column = lane
-    for row in range(1, H):
-        column = jnp.where(lane >= row * PITCH, lane - row * PITCH, column)
-    inside = (column >= HALO) & (column < HALO + WD)
-    mask = jnp.where(inside, 1.0, 0.0).astype(BF)
-
-    left = left_ref[...].astype(F32)
-    right = right_ref[...].astype(F32)
+    first = core == 0
+    inner = inner_ref[...].astype(F32)
+    outer = outer_ref[...].astype(F32)
+    left = jnp.where(first, outer, inner)
+    right = jnp.where(first, inner, outer)
     out_ref[...] = field_ref[...]
     add_halo(out_ref, left, pltpu.roll(right, 8, axis=1))
     up_ref[...] = slope_ref[...]
     add_halo(up_ref, pltpu.roll(left, 120, axis=1), right)
 
-    mask_s[...] = mask
     bias_row = lax.broadcasted_iota(jnp.int32, (BIAS_ROWS, N), 0)
     for b in range(DEPTH):
         hid_s[b, C : C + BIAS_ROWS, :] = jnp.where(bias_row < 3, 1.0, 0.0).astype(BF)
@@ -474,34 +478,37 @@
 
 
 def tail_kernel(
-    flag_ref, flat_ref, up_in, dh_ref, convt_ref, out_ref, grad_ref, wide, up_s, rstack_s, wide_s
+    flag_ref, flat_ref, up_in, dh_ref, convt_ref, out_ref, grad_ref, blank_ref, wide, up_s, rstack_s, wide_s
 ):
     flip = flag_ref[0, 0]
     lane = lax.broadcasted_iota(jnp.int32, (C, N), 1)
     up_s[...] = up_in[...]
     step_back(up_s, dh_ref, convt_ref[0], rstack_s, wide_s, lane)
+    blank_ref[...] = jnp.zeros((UNITS, 128), F32)
     unflatten(flat_ref, out_ref, wide, flip)
     unflatten(up_s, grad_ref, wide, flip)
 
 
-def unpack_kernel(src_ref, conv_ref, expand_ref, project_ref):
-    for b in range(DEPTH):
-        core, xl = b // 2, b % 2
-        total = 0.0
-        for y in range(4):
-            total = total + src_ref[4 * y + 2 * xl + core].astype(F32)
-        unit = [total[8 * i : 8 * i + 8, :] for i in range(9)]
-        tail = []
-        for i in range(5, 9):
-            tail += [unit[i][:, 0:C], unit[i][:, C : 2 * C]]
-        pieces = []
-        for r in range(3):
-            for c in range(3):
-                pieces.append(tail[c] if r == 2 else unit[c][:, C * r : C * r + C])
-        conv_ref[b] = jnp.concatenate(pieces, axis=1)
-        for i in range(4):
-            expand_ref[b, 8 * i : 8 * i + 8, :] = tail[3 + i]
-        project_ref[b] = jnp.concatenate([unit[3], unit[4]], axis=1)
+def unpack_kernel(mine_ref, theirs_ref, conv_ref, expand_ref, project_ref):
+    core = lax.axis_index("core")
+    for source, pair in ((mine_ref, core), (theirs_ref, 1 - core)):
+        for xl in range(2):
+            unpack_block(source[xl].astype(F32), 2 * pair + xl, conv_ref, expand_ref, project_ref)
+
+
+def unpack_block(total, b, conv_ref, expand_ref, project_ref):
+    unit = [total[8 * i : 8 * i + 8, :] for i in range(9)]
+    tail = []
+    for i in range(5, 9):
+        tail += [unit[i][:, 0:C], unit[i][:, C : 2 * C]]
+    pieces = []
+    for r in range(3):
+        for c in range(3):
+            pieces.append(tail[c] if r == 2 else unit[c][:, C * r : C * r + C])
+    conv_ref[b] = jnp.concatenate(pieces, axis=1)
+    for i in range(4):
+        expand_ref[b, 8 * i : 8 * i + 8, :] = tail[3 + i]
+    project_ref[b] = jnp.concatenate([unit[3], unit[4]], axis=1)
 
 
 def main_scratch():
@@ -515,7 +522,6 @@
         pltpu.VMEM((DEPTH, 8, UNITS, 128), F32),
         pltpu.VMEM((3 * C, N), BF),
         pltpu.VMEM((HID, N), BF),
-        pltpu.VMEM((C, N), BF),
         pltpu.VMEM((HID, N), F32),
     ]
 
@@ -525,7 +531,7 @@
     slope = cotangent[0]
     wide = pltpu.VMEM((HALVES, C * H, 128), F32)
     sources = [field, slope, conv_weight, expand_weight.transpose(0, 2, 1), expand_bias, project_weight]
-    low, high, flag, field, slope, taps, expandt, bias, weight = call(
+    inner, outer, flag, field, slope, taps, expandt, bias, weight = call(
         edge_kernel,
         [shape(C, 128), shape(C, 128), shape(8, 128, dtype=jnp.int32)]
         + [shape(*array.shape, dtype=array.dtype) for array in sources],
@@ -534,10 +540,11 @@
         mib=8,
     )
     count = lax.axis_size(LON)
-    left = lax.ppermute(high, LON, [(i, (i + 1) % count) for i in range(count)])
-    right = lax.ppermute(low, LON, [((i + 1) % count, i) for i in range(count)])
-
-    flat_f, flat_g, conv, convt, expand, project, projectt = call(
+    inner = lax.ppermute(inner, "core", [(0, 1), (1, 0)])
+    across = [(i, (i + 1) % count) for i in range(1, count, 2)]
+    outer = lax.ppermute(outer, LON, across + [(target, source) for source, target in across])
+
+    flat_f, flat_g, conv, convt, expand, project, projectt, mask = call(
         prep_kernel,
         [
             shape(C, N),
@@ -547,6 +554,7 @@
             shape(DEPTH, HID, C + BIAS_ROWS),
             shape(DEPTH, C, HID),
             shape(DEPTH, HID, C),
+            shape(C, N),
         ],
         [
             (flag, VM),
@@ -573,14 +581,15 @@
         [
             (flat_f, VM),
             (flat_g, VM),
-            (left, VM),
-            (right, VM),
+            (inner, VM),
+            (outer, VM),
             (conv, VM),
             (convt, VM),
             (expand, VM),
             (expandt, VM),
             (project, VM),
             (projectt, VM),
+            (mask, VM),
         ],
         main_scratch(),
         flops=1 << 33,
@@ -589,17 +598,20 @@
     came = lax.ppermute(other, "core", [(0, 1), (1, 0)])
     share = (own.astype(F32) + came.astype(F32)).astype(BF)
     parts = lax.all_to_all(share.reshape(16, UNITS, 128), ("xl", "ens"), 0, 0, tiled=True)
-    section_out, input_grad = call(
+    section_out, input_grad, blank = call(
         tail_kernel,
-        [shape(C, H, WD)] * 2,
+        [shape(C, H, WD)] * 2 + [shape(UNITS, 128, dtype=F32)],
         [(flag, VM), (flat_out, VM), (up, VM), (d_hidden, VM), (convt, VM)],
         [wide, pltpu.VMEM((C, N), BF), pltpu.VMEM((3 * C, N), BF), pltpu.VMEM((3 * C, N), F32)],
         flops=1 << 30,
         mib=16,
     )
-    total = jnp.sum(parts.astype(F32), axis=0).astype(BF)
-    parts = jnp.broadcast_to(total[None], (count, UNITS, 128))
-    parts = lax.all_to_all(parts, LON, 0, 0, tiled=True)
+    total = (jnp.sum(parts.astype(F32), axis=0) + blank).astype(BF)
+    chips = lax.axis_size(("y", "xl"))
+    parts = jnp.broadcast_to(total[None], (chips, UNITS, 128))
+    parts = lax.all_to_all(parts, ("y", "xl"), 0, 0, tiled=True)
+    mine = jnp.sum(parts.reshape(chips // 2, 2, UNITS, 128).astype(F32), axis=0).astype(BF)
+    theirs = lax.ppermute(mine, "core", [(0, 1), (1, 0)])
     conv_grad, expand_grad, project_grad = call(
         unpack_kernel,
         [
@@ -607,7 +619,7 @@
             shape(DEPTH, 32, C, dtype=F32),
             shape(DEPTH, 8, HID, dtype=F32),
         ],
-        [(parts, VM)],
+        [(mine, VM), (theirs, VM)],
     )
     return section_out[None], input_grad[None], conv_grad, expand_grad, project_grad
 

time: 54.3 us -> 53.9 us (level)
  starting transfers between devices: 9.07 us -> 15.7 us
  blocking collectives: 16.1 us -> 9.85 us
  other arithmetic: 0.13 us -> 0.86 us
  local copies, waits for them, and re-layouts: 0.75 us -> 0.02 us
  Pallas kernels: 18.3 us -> 17.7 us
    all_to_all x1, blocking collectives: 16.1 us -> 9.85 us  [local(): parts = lax.all_to_all(parts, ('y', 'xl'), 0, 0, tiled=True)]
    ppermute x2 -> x3, starting transfers between devices: 2.67 us -> 5.76 us  [the longest x1 2.98 us: local(): theirs = lax.ppermute(mine, 'core', [(0, 1), (1, 0)])]
    all_to_all x1, starting transfers between devices: 5.66 us -> 7.47 us  [local(): lax.all_to_all(share.reshape(16, UNITS, 128), ('xl', 'ens'), 0, 0, tiled=...]
    ppermute x1, starting transfers between devices: 0.73 us -> 2.5 us  [local(): came = lax.ppermute(other, 'core', [(0, 1), (1, 0)])]
    broadcast_in_dim x1, local copies, waits for them, and re-layouts: 0.75 us -> 0.02 us  [local(): parts = jnp.broadcast_to(total[None], (chips, UNITS, 128))]
    ppermute x2 -> x3, waiting for transfers between devices: 2.29 us -> 1.57 us  [the longest x1 0.87 us: local(): theirs = lax.ppermute(mine, 'core', [(0, 1), (1, 0)])]
    convert_element_type x1, other arithmetic: 0.08 us -> 0.79 us  [local(): share = (own.astype(F32) + came.astype(F32)).astype(BF)]
    pallas_call x5, Pallas kernels: 18.3 us -> 17.7 us  [call(): pl.pallas_call(body, out_shape=outs, in_specs=specs, out_specs=jax.tree.m...]
  transfers between devices with their start and end apart: 4 -> 5, of which waited for: 3 -> 4; matrix products, arithmetic and copies ran while one was open for 0% -> 0% of each run, Pallas kernels for 6% -> 6%
where the time goes in v5:
time: 53.9 us; the launch traced here: 53.7 us
  Pallas kernels  17.7 us (33%)
  starting transfers between devices  15.7 us (29%)
  blocking collectives  9.85 us (18%)
  waiting for transfers between devices  8.82 us (16%)
  other arithmetic  0.86 us (2%)
  between operations  0.69 us (1%)
    pallas_call x5, Pallas kernels, call(): pl.pallas_call(body, out_shape=outs, in_specs=specs, out_specs=jax.tree.m...  17.7 us
    all_to_all x1, blocking collectives, local(): parts = lax.all_to_all(parts, ('y', 'xl'), 0, 0, tiled=True)  9.85 us
    all_to_all x1, starting transfers between devices, local(): lax.all_to_all(share.reshape(16, UNITS, 128), ('xl', 'ens'), 0, 0, tiled=...  7.47 us
    all_to_all x1, waiting for transfers between devices, local(): lax.all_to_all(share.reshape(16, UNITS, 128), ('xl', 'ens'), 0, 0, tiled=...  6.04 us
    ppermute x1, starting transfers between devices, local(): theirs = lax.ppermute(mine, 'core', [(0, 1), (1, 0)])  2.98 us
    ppermute x1, starting transfers between devices, local(): came = lax.ppermute(other, 'core', [(0, 1), (1, 0)])  2.5 us
    ppermute x1, starting transfers between devices, local(): inner = lax.ppermute(inner, 'core', [(0, 1), (1, 0)])  1.5 us
    ppermute x1, starting transfers between devices, local(): lax.ppermute(outer, LON, across + [(target, source) for source, target in...  1.27 us
  transfers between devices with their start and end apart: 5, of which 4 were waited for; matrix products, arithmetic and copies ran while one was open for 0% of the time, Pallas kernels for 6%

profile of v5, /device:TPU:1, one launch (start us, length us, event | category | flops | bytes accessed | tf_op | source)
XLA Modules:
  0.0 53.7 jit_solution(2970183307253275130)
XLA Ops:
  0.6 1.5 %shard_map.110 = (bf16[64,128]{1,0:T(8,128)(2,1)S(1)}, bf16[64,128]{1,0:T(8,128)(2,1)S(1)}, s32[8,128]{1,0:T(8,128)S(1)}, bf16[64,8,256]{2,1,0:T(8,128)(2,1)S(1)...) custom-call(s32[16]{0:T(128)} %refs_0_.1, ...), custom_call_target="tpu_custom_call" | custom-call | bytes 1048576 | tf_op jit(solution)/shard_map/pallas_call | solution.py:49
  2.1 1.5 %collective-permute-start = (bf16[64,128]{1,0:T(8,128)(2,1)S(1)}, bf16[64,128]{1,0:T(8,128)(2,1)S(1)}, u32[]{:S(2)}, u32[]{:S(2)}) collective-permute-start(bf16[64,128]{1,0:T(8,128)(2,1)S(1)} %get-tuple-element.42), channel_id=1, source_target_pairs={{0,8},{8,0},{1,9},{9,1},{2,10},{10,2},{3,11},{11,3},{4,12},{12,4},... | collective-permute-start | bytes 49160 | tf_op jit(solution)/shard_map/ppermute | solution.py:543
  3.6 1.3 %collective-permute-start.1 = (bf16[64,128]{1,0:T(8,128)(2,1)S(1)}, bf16[64,128]{1,0:T(8,128)(2,1)S(1)}, u32[]{:S(2)}, u32[]{:S(2)}) collective-permute-start(bf16[64,128]{1,0:T(8,128)(2,1)S(1)} %get-tuple-element.43), channel_id=1, source_target_pairs={{8,16},{24,32},{40,48},{56,64},{72,80},{88,96},{104,112},{120,0},{... | collective-permute-start | bytes 49160 | tf_op jit(solution)/shard_map/ppermute | solution.py:545
  4.9 1.2 %shard_map.111 = (bf16[64,2176]{1,0:T(8,128)(2,1)S(1)}, bf16[64,2176]{1,0:T(8,128)(2,1)S(1)}, bf16[4,192,192]{2,1,0:T(8,128)(2,1)S(1)}, bf16[4,192,192]{2,1,0:T(...) custom-call(s32[8,128]{1,0:T(8,128)S(1)} %get-tuple-element.33.flag_, ...), custom_call_target="tpu_custom_call" | custom-call | flops 134217728 | bytes 1048576 | tf_op jit(solution)/shard_map/pallas_call | solution.py:49
  6.1 0.0 collective-permute-done.inner_ref
  6.1 0.7 %collective-permute-done.1.outer_ref = bf16[64,128]{1,0:T(8,128)(2,1)S(1)} collective-permute-done((bf16[64,128]{1,0:T(8,128)(2,1)S(1)}, bf16[64,128]{1,0:T(8,128)(2,1)S(1)}, u32[]{:S(2)}, u32[]{:S(2)}) %collective-permute-start.1) | collective-permute-done | bytes 16416 | tf_op jit(solution)/shard_map/ppermute | solution.py:545
  6.8 12.4 %shard_map.112 = (bf16[64,2176]{1,0:T(8,128)(2,1)S(1)}, bf16[64,2176]{1,0:T(8,128)(2,1)S(1)}, bf16[64,2176]{1,0:T(8,128)(2,1)S(1)}, bf16[1152,128]{1,0:T(8,128)(2,1)S(1)}, bf16[1152,128]{1,0:T(8,128)(2,1)S(1)}) custom-call(bf16[64,2176]{1,0:T(8,128)(2,1)S(1)} %get-tuple-element.40.field_ref, bf16[64,2176]{1,0:T(8,128)(2,1)S(1)} %get-tuple-element.41.slope_ref, ...), custom_call_target="tpu_custom_call" | custom-call | flops 8589934592 | bytes 1048576 | tf_op jit(solution)/shard_map/pallas_call | solution.py:49
  19.3 2.5 %collective-permute-start.2 = (bf16[1152,128]{1,0:T(8,128)(2,1)S(1)}, bf16[1152,128]{1,0:T(8,128)(2,1)S(1)}, u32[]{:S(2)}, u32[]{:S(2)}) collective-permute-start(bf16[1152,128]{1,0:T(8,128)(2,1)S(1)} %get-tuple-element.56), channel_id=1, source_target_pairs={{0,8},{8,0},{1,9},{9,1},{2,10},{10,2},{3,11},{11,3},{4,12},{12,4},... | collective-permute-start | bytes 884744 | tf_op jit(solution)/shard_map/ppermute | solution.py:598
  21.8 1.2 %collective-permute-done.2 = bf16[1152,128]{1,0:T(8,128)(2,1)S(1)} collective-permute-done((bf16[1152,128]{1,0:T(8,128)(2,1)S(1)}, bf16[1152,128]{1,0:T(8,128)(2,1)S(1)}, u32[]{:S(2)}, u32[]{:S(2)}) %collective-permute-start.2) | collective-permute-done | bytes 294944 | tf_op jit(solution)/shard_map/ppermute | solution.py:598
  23.0 0.8 %add_convert_fusion = bf16[1152,128]{1,0:T(8,128)(2,1)} fusion(bf16[1152,128]{1,0:T(8,128)(2,1)S(1)} %collective-permute-done.2, bf16[1152,128]{1,0:T(8,128)(2,1)S(1)} %get-tuple-element.55), kind=kLoop, calls=%fused_computation.1 | loop fusion | flops 589824 | bytes 884736 | tf_op jit(solution)/shard_map/convert_element_type | solution.py:599
  23.8 7.5 %all-to-all-start = ((bf16[16,72,128]{2,1,0:T(8,128)(2,1)}), bf16[16,72,128]{2,1,0:T(8,128)(2,1)S(1)}, u32[]{:S(2)}, u32[]{:S(2)}) async-start(bf16[16,72,128]{2,1,0:T(8,128)(2,1)} %bitcast.5), calls=%async_computation | async-start | bytes 589824 | tf_op jit(solution)/shard_map/all_to_all | solution.py:600
  31.2 1.8 %shard_map.113 = (bf16[64,8,256]{2,1,0:T(8,128)(2,1)}, bf16[64,8,256]{2,1,0:T(8,128)(2,1)}, f32[72,128]{1,0:T(8,128)S(1)}) custom-call(s32[8,128]{1,0:T(8,128)S(1)} %get-tuple-element.33.flag_ref, bf16[64,2176]{1,0:T(8,128)(2,1)S(1)} %get-tuple-element.50.flat_ref, bf16[64,2176]{1,0:T(8,128)(2,1)S(1)} %get-tuple-element.51.up_in, ...), custom_call_target="tpu_custom_call" | custom-call | flops 1073741824 | bytes 1048576 | tf_op jit(solution)/shard_map/pallas_call | solution.py:49
  33.1 6.0 %all-to-all-done = bf16[16,72,128]{2,1,0:T(8,128)(2,1)S(1)} async-done(((bf16[16,72,128]{2,1,0:T(8,128)(2,1)}), bf16[16,72,128]{2,1,0:T(8,128)(2,1)S(1)}, u32[]{:S(2)}, u32[]{:S(2)}) %all-to-all-start) | async-done | bytes 294944 | tf_op jit(solution)/shard_map/all_to_all | solution.py:600
  39.2 9.9 %all_to_all.10 = bf16[8,72,128]{2,1,0:T(8,128)(2,1)S(1)} all-to-all(bf16[8,72,128]{2,1,0:T(8,128)(2,1)S(1)} %broadcast_in_dim.14), channel_id=1, replica_groups=mesh['y'=4,'xl'=2,'core'=2,'ens'=8] {'y','xl'}, dimensions={0} | all-to-all | bytes 294912 | tf_op jit(solution)/shard_map/all_to_all | solution.py:612
  49.1 3.0 %collective-permute-start.3 = (bf16[2,72,128]{2,1,0:T(8,128)(2,1)S(1)}, bf16[2,72,128]{2,1,0:T(8,128)(2,1)S(1)}, u32[]{:S(2)}, u32[]{:S(2)}) collective-permute-start(bf16[2,72,128]{2,1,0:T(8,128)(2,1)S(1)} %reduce_sum.22.mine_ref), channel_id=1, source_target_pairs={{0,8},{8,0},{1,9},{9,1},{2,10},{10,2},{3,11},{11,3},{4,12},{12,4},... | collective-permute-start | bytes 110600 | tf_op jit(solution)/shard_map/ppermute | solution.py:614
  52.1 0.9 %collective-permute-done.3.theirs_ref = bf16[2,72,128]{2,1,0:T(8,128)(2,1)S(1)} collective-permute-done((bf16[2,72,128]{2,1,0:T(8,128)(2,1)S(1)}, bf16[2,72,128]{2,1,0:T(8,128)(2,1)S(1)}, u32[]{:S(2)}, u32[]{:S(2)}) %collective-permute-start.3) | collective-permute-done | bytes 36896 | tf_op jit(solution)/shard_map/ppermute | solution.py:614
  53.0 0.7 %shard_map.114 = (f32[4,8,576]{2,1,0:T(8,128)}, f32[4,32,64]{2,1,0:T(8,128)}, f32[4,8,256]{2,1,0:T(8,128)}) custom-call(bf16[2,72,128]{2,1,0:T(8,128)(2,1)S(1)} %reduce_sum.22.mine_ref, bf16[2,72,128]{2,1,0:T(8,128)(2,1)S(1)} %collective-permute-done.3.theirs_ref), custom_call_target="tpu_custom_call" | custom-call | bytes 1048576 | tf_op jit(solution)/shard_map/pallas_call | solution.py:49
  (4 shorter events, 0.1 us)
Async XLA Ops:
  2.1 4.0 %collective-permute-start = (bf16[64,128]{1,0:T(8,128)(2,1)S(1)}, bf16[64,128]{1,0:T(8,128)(2,1)S(1)}, u32[]{:S(2)}, u32[]{:S(2)}) collective-permute-start(bf16[64,128]{1,0:T(8,128)(2,1)S(1)} %get-tuple-element.42), channel_id=1, source_target_pairs={{0,8},{8,0},{1,9},{9,1},{2,10},{10,2},{3,11},{11,3},{4,12},{12,4},... | collective-permute-start | bytes 49160 | tf_op jit(solution)/shard_map/ppermute | solution.py:543
  3.6 3.2 %collective-permute-start.1 = (bf16[64,128]{1,0:T(8,128)(2,1)S(1)}, bf16[64,128]{1,0:T(8,128)(2,1)S(1)}, u32[]{:S(2)}, u32[]{:S(2)}) collective-permute-start(bf16[64,128]{1,0:T(8,128)(2,1)S(1)} %get-tuple-element.43), channel_id=1, source_target_pairs={{8,16},{24,32},{40,48},{56,64},{72,80},{88,96},{104,112},{120,0},{... | collective-permute-start | bytes 49160 | tf_op jit(solution)/shard_map/ppermute | solution.py:545
  19.3 3.7 %collective-permute-start.2 = (bf16[1152,128]{1,0:T(8,128)(2,1)S(1)}, bf16[1152,128]{1,0:T(8,128)(2,1)S(1)}, u32[]{:S(2)}, u32[]{:S(2)}) collective-permute-start(bf16[1152,128]{1,0:T(8,128)(2,1)S(1)} %get-tuple-element.56), channel_id=1, source_target_pairs={{0,8},{8,0},{1,9},{9,1},{2,10},{10,2},{3,11},{11,3},{4,12},{12,4},... | collective-permute-start | bytes 884744 | tf_op jit(solution)/shard_map/ppermute | solution.py:598
  23.8 15.4 %all-to-all-start = ((bf16[16,72,128]{2,1,0:T(8,128)(2,1)}), bf16[16,72,128]{2,1,0:T(8,128)(2,1)S(1)}, u32[]{:S(2)}, u32[]{:S(2)}) async-start(bf16[16,72,128]{2,1,0:T(8,128)(2,1)} %bitcast.5), calls=%async_computation | async-start | bytes 589824 | tf_op jit(solution)/shard_map/all_to_all | solution.py:600
  49.1 3.8 %collective-permute-start.3 = (bf16[2,72,128]{2,1,0:T(8,128)(2,1)S(1)}, bf16[2,72,128]{2,1,0:T(8,128)(2,1)S(1)}, u32[]{:S(2)}, u32[]{:S(2)}) collective-permute-start(bf16[2,72,128]{2,1,0:T(8,128)(2,1)S(1)} %reduce_sum.22.mine_ref), channel_id=1, source_target_pairs={{0,8},{8,0},{1,9},{9,1},{2,10},{10,2},{3,11},{11,3},{4,12},{12,4},... | collective-permute-start | bytes 110600 | tf_op jit(solution)/shard_map/ppermute | solution.py:614

commit v6 on v5

--- a/solution.py
+++ b/solution.py
@@ -27,6 +27,8 @@
 BIAS_ROWS = 16
 CHUNKS = [(s, min(256, N - s)) for s in range(0, N, 256)]
 FORWARD_LAG = 9
+GELU_PARTS = 4
+GROUP = 3
 BACKWARD_LAG = 8
 TURN = 8
 
@@ -308,11 +310,13 @@
 
     def gelu(i):
         cut = CUTS[i]
-        inner = inner_s[:, cut]
-        twice = 1.0 + lax.erf(inner * SQRT_HALF)
-        bell = jnp.exp2((inner * inner) * -HALF_LOG2E)
-        slope_s[b, :, cut] = (twice + (inner * (2.0 * INV_ROOT_TAU)) * bell).astype(BF)
-        active_s[b, :, cut] = (inner * twice).astype(BF)
+        for part in range(GELU_PARTS):
+            rows = slice(part * HID // GELU_PARTS, (part + 1) * HID // GELU_PARTS)
+            inner = inner_s[rows, cut]
+            twice = 1.0 + lax.erf(inner * SQRT_HALF)
+            bell = jnp.exp2((inner * inner) * -HALF_LOG2E)
+            slope_s[b, rows, cut] = (twice + (inner * (2.0 * INV_ROOT_TAU)) * bell).astype(BF)
+            active_s[b, rows, cut] = (inner * twice).astype(BF)
 
     def project(i):
         cut = CUTS[i]
@@ -320,6 +324,10 @@
         out_ref[:, cut] = (old + mm(project_ref[b], active_s[b, :, cut])).astype(BF)
 
     return [(conv, 1), (gelu, 5), (expand, 4), (hidden, 3), (project, 6), (stacks, 0)]
+
+
+def add_to(total, term):
+    total[:] = [total[0] + term] if total else [term]
 
 
 def backward_stages(
@@ -342,7 +350,7 @@
         up = up_ref[:, cut]
         d_active = mm(projectt_ref[b], up)
         din_s[:, cut] = (d_active * slope_s[b, :, cut].astype(F32)).astype(BF)
-        pg.append(mm_nt(up * mask_s[:, cut], active_s[b, :, cut]))
+        add_to(pg, mm_nt(up * mask_s[:, cut], active_s[b, :, cut]))
 
     def hidden(i):
         cut = CUTS[i]
@@ -350,14 +358,16 @@
         d_hidden = mm(expandt_ref[b], d_inner).astype(BF)
         dh_ref[:, cut] = d_hidden
         own_s[C : 2 * C, cut] = d_hidden * mask_s[:, cut]
-        eg.append(mm_nt(d_inner, hid_s[b, 0:C, cut] * mask_s[:, cut]))
+        add_to(eg, mm_nt(d_inner, hid_s[b, 0:C, cut] * mask_s[:, cut]))
 
     def shares(i):
         for t in TILE_SETS[i]:
             right, left = own_moved(t)
             own_s[0:C, span(t)] = left
             own_s[2 * C : 3 * C, span(t)] = right
-        cg.append(mm_nt(own_s[:, CUTS[i]], stack_s[b, :, CUTS[i]]))
+        if i % GROUP == GROUP - 1:
+            cut = slice(CUTS[i + 1 - GROUP].start, CUTS[i].stop)
+            add_to(cg, mm_nt(own_s[:, cut], stack_s[b, :, cut]))
 
     def stacks(i):
         for t in TILE_SETS[i]:
@@ -373,7 +383,7 @@
             up_ref[:, span(t)] = total.astype(BF)
 
     def finish():
-        sums[b] = (sum(cg[1:], cg[0]), sum(eg[1:], eg[0]), 0.5 * sum(pg[1:], pg[0]))
+        sums[b] = (cg[0], eg[0], 0.5 * pg[0])
 
     stages = [(inner, 0), (hidden, 1), (shares, 3)]
     if b > 0:

time: 53.9 us -> 53.4 us (level)
  Pallas kernels: 17.7 us -> 17.1 us
    pallas_call x5, Pallas kernels: 17.7 us -> 17.1 us  [call(): pl.pallas_call(body, out_shape=outs, in_specs=specs, out_specs=jax.tree.m...]
where the time goes in v6:
time: 53.4 us; the launch traced here: 53.1 us
  Pallas kernels  17.1 us (32%)
  starting transfers between devices  15.7 us (29%)
  blocking collectives  9.86 us (18%)
  waiting for transfers between devices  8.82 us (17%)
  other arithmetic  0.86 us (2%)
  between operations  0.69 us (1%)
    pallas_call x5, Pallas kernels, call(): pl.pallas_call(body, out_shape=outs, in_specs=specs, out_specs=jax.tree.m...  17.1 us
    all_to_all x1, blocking collectives, local(): parts = lax.all_to_all(parts, ('y', 'xl'), 0, 0, tiled=True)  9.86 us
    all_to_all x1, starting transfers between devices, local(): lax.all_to_all(share.reshape(16, UNITS, 128), ('xl', 'ens'), 0, 0, tiled=...  7.47 us
    all_to_all x1, waiting for transfers between devices, local(): lax.all_to_all(share.reshape(16, UNITS, 128), ('xl', 'ens'), 0, 0, tiled=...  6.04 us
    ppermute x1, starting transfers between devices, local(): theirs = lax.ppermute(mine, 'core', [(0, 1), (1, 0)])  2.98 us
    ppermute x1, starting transfers between devices, local(): came = lax.ppermute(other, 'core', [(0, 1), (1, 0)])  2.5 us
    ppermute x1, starting transfers between devices, local(): inner = lax.ppermute(inner, 'core', [(0, 1), (1, 0)])  1.5 us
    ppermute x1, starting transfers between devices, local(): lax.ppermute(outer, LON, across + [(target, source) for source, target in...  1.27 us
  transfers between devices with their start and end apart: 5, of which 4 were waited for; matrix products, arithmetic and copies ran while one was open for 0% of the time, Pallas kernels for 6%

profile of v6, /device:TPU:1, one launch (start us, length us, event | category | flops | bytes accessed | tf_op | source)
XLA Modules:
  0.0 53.1 jit_solution(2558338180560747426)
XLA Ops:
  0.6 1.5 %shard_map.110 = (bf16[64,128]{1,0:T(8,128)(2,1)S(1)}, bf16[64,128]{1,0:T(8,128)(2,1)S(1)}, s32[8,128]{1,0:T(8,128)S(1)}, bf16[64,8,256]{2,1,0:T(8,128)(2,1)S(1)...) custom-call(s32[16]{0:T(128)} %refs_0_.1, ...), custom_call_target="tpu_custom_call" | custom-call | bytes 1048576 | tf_op jit(solution)/shard_map/pallas_call | solution.py:51
  2.1 1.5 %collective-permute-start = (bf16[64,128]{1,0:T(8,128)(2,1)S(1)}, bf16[64,128]{1,0:T(8,128)(2,1)S(1)}, u32[]{:S(2)}, u32[]{:S(2)}) collective-permute-start(bf16[64,128]{1,0:T(8,128)(2,1)S(1)} %get-tuple-element.42), channel_id=1, source_target_pairs={{0,8},{8,0},{1,9},{9,1},{2,10},{10,2},{3,11},{11,3},{4,12},{12,4},... | collective-permute-start | bytes 49160 | tf_op jit(solution)/shard_map/ppermute | solution.py:553
  3.6 1.3 %collective-permute-start.1 = (bf16[64,128]{1,0:T(8,128)(2,1)S(1)}, bf16[64,128]{1,0:T(8,128)(2,1)S(1)}, u32[]{:S(2)}, u32[]{:S(2)}) collective-permute-start(bf16[64,128]{1,0:T(8,128)(2,1)S(1)} %get-tuple-element.43), channel_id=1, source_target_pairs={{8,16},{24,32},{40,48},{56,64},{72,80},{88,96},{104,112},{120,0},{... | collective-permute-start | bytes 49160 | tf_op jit(solution)/shard_map/ppermute | solution.py:555
  4.9 1.2 %shard_map.111 = (bf16[64,2176]{1,0:T(8,128)(2,1)S(1)}, bf16[64,2176]{1,0:T(8,128)(2,1)S(1)}, bf16[4,192,192]{2,1,0:T(8,128)(2,1)S(1)}, bf16[4,192,192]{2,1,0:T(...) custom-call(s32[8,128]{1,0:T(8,128)S(1)} %get-tuple-element.33.flag_, ...), custom_call_target="tpu_custom_call" | custom-call | flops 134217728 | bytes 1048576 | tf_op jit(solution)/shard_map/pallas_call | solution.py:51
  6.1 0.0 collective-permute-done.inner_ref
  6.1 0.7 %collective-permute-done.1.outer_ref = bf16[64,128]{1,0:T(8,128)(2,1)S(1)} collective-permute-done((bf16[64,128]{1,0:T(8,128)(2,1)S(1)}, bf16[64,128]{1,0:T(8,128)(2,1)S(1)}, u32[]{:S(2)}, u32[]{:S(2)}) %collective-permute-start.1) | collective-permute-done | bytes 16416 | tf_op jit(solution)/shard_map/ppermute | solution.py:555
  6.8 11.9 %shard_map.112 = (bf16[64,2176]{1,0:T(8,128)(2,1)S(1)}, bf16[64,2176]{1,0:T(8,128)(2,1)S(1)}, bf16[64,2176]{1,0:T(8,128)(2,1)S(1)}, bf16[1152,128]{1,0:T(8,128)(2,1)S(1)}, bf16[1152,128]{1,0:T(8,128)(2,1)S(1)}) custom-call(bf16[64,2176]{1,0:T(8,128)(2,1)S(1)} %get-tuple-element.40.field_ref, bf16[64,2176]{1,0:T(8,128)(2,1)S(1)} %get-tuple-element.41.slope_ref, ...), custom_call_target="tpu_custom_call" | custom-call | flops 8589934592 | bytes 1048576 | tf_op jit(solution)/shard_map/pallas_call | solution.py:51
  18.7 2.5 %collective-permute-start.2 = (bf16[1152,128]{1,0:T(8,128)(2,1)S(1)}, bf16[1152,128]{1,0:T(8,128)(2,1)S(1)}, u32[]{:S(2)}, u32[]{:S(2)}) collective-permute-start(bf16[1152,128]{1,0:T(8,128)(2,1)S(1)} %get-tuple-element.56), channel_id=1, source_target_pairs={{0,8},{8,0},{1,9},{9,1},{2,10},{10,2},{3,11},{11,3},{4,12},{12,4},... | collective-permute-start | bytes 884744 | tf_op jit(solution)/shard_map/ppermute | solution.py:608
  21.2 1.2 %collective-permute-done.2 = bf16[1152,128]{1,0:T(8,128)(2,1)S(1)} collective-permute-done((bf16[1152,128]{1,0:T(8,128)(2,1)S(1)}, bf16[1152,128]{1,0:T(8,128)(2,1)S(1)}, u32[]{:S(2)}, u32[]{:S(2)}) %collective-permute-start.2) | collective-permute-done | bytes 294944 | tf_op jit(solution)/shard_map/ppermute | solution.py:608
  22.4 0.8 %add_convert_fusion = bf16[1152,128]{1,0:T(8,128)(2,1)} fusion(bf16[1152,128]{1,0:T(8,128)(2,1)S(1)} %collective-permute-done.2, bf16[1152,128]{1,0:T(8,128)(2,1)S(1)} %get-tuple-element.55), kind=kLoop, calls=%fused_computation.1 | loop fusion | flops 589824 | bytes 884736 | tf_op jit(solution)/shard_map/convert_element_type | solution.py:609
  23.2 7.5 %all-to-all-start = ((bf16[16,72,128]{2,1,0:T(8,128)(2,1)}), bf16[16,72,128]{2,1,0:T(8,128)(2,1)S(1)}, u32[]{:S(2)}, u32[]{:S(2)}) async-start(bf16[16,72,128]{2,1,0:T(8,128)(2,1)} %bitcast.5), calls=%async_computation | async-start | bytes 589824 | tf_op jit(solution)/shard_map/all_to_all | solution.py:610
  30.6 1.8 %shard_map.113 = (bf16[64,8,256]{2,1,0:T(8,128)(2,1)}, bf16[64,8,256]{2,1,0:T(8,128)(2,1)}, f32[72,128]{1,0:T(8,128)S(1)}) custom-call(s32[8,128]{1,0:T(8,128)S(1)} %get-tuple-element.33.flag_ref, bf16[64,2176]{1,0:T(8,128)(2,1)S(1)} %get-tuple-element.50.flat_ref, bf16[64,2176]{1,0:T(8,128)(2,1)S(1)} %get-tuple-element.51.up_in, ...), custom_call_target="tpu_custom_call" | custom-call | flops 1073741824 | bytes 1048576 | tf_op jit(solution)/shard_map/pallas_call | solution.py:51
  32.5 6.0 %all-to-all-done = bf16[16,72,128]{2,1,0:T(8,128)(2,1)S(1)} async-done(((bf16[16,72,128]{2,1,0:T(8,128)(2,1)}), bf16[16,72,128]{2,1,0:T(8,128)(2,1)S(1)}, u32[]{:S(2)}, u32[]{:S(2)}) %all-to-all-start) | async-done | bytes 294944 | tf_op jit(solution)/shard_map/all_to_all | solution.py:610
  38.6 9.9 %all_to_all.10 = bf16[8,72,128]{2,1,0:T(8,128)(2,1)S(1)} all-to-all(bf16[8,72,128]{2,1,0:T(8,128)(2,1)S(1)} %broadcast_in_dim.14), channel_id=1, replica_groups=mesh['y'=4,'xl'=2,'core'=2,'ens'=8] {'y','xl'}, dimensions={0} | all-to-all | bytes 294912 | tf_op jit(solution)/shard_map/all_to_all | solution.py:622
  48.5 3.0 %collective-permute-start.3 = (bf16[2,72,128]{2,1,0:T(8,128)(2,1)S(1)}, bf16[2,72,128]{2,1,0:T(8,128)(2,1)S(1)}, u32[]{:S(2)}, u32[]{:S(2)}) collective-permute-start(bf16[2,72,128]{2,1,0:T(8,128)(2,1)S(1)} %reduce_sum.22.mine_ref), channel_id=1, source_target_pairs={{0,8},{8,0},{1,9},{9,1},{2,10},{10,2},{3,11},{11,3},{4,12},{12,4},... | collective-permute-start | bytes 110600 | tf_op jit(solution)/shard_map/ppermute | solution.py:624
  51.5 0.9 %collective-permute-done.3.theirs_ref = bf16[2,72,128]{2,1,0:T(8,128)(2,1)S(1)} collective-permute-done((bf16[2,72,128]{2,1,0:T(8,128)(2,1)S(1)}, bf16[2,72,128]{2,1,0:T(8,128)(2,1)S(1)}, u32[]{:S(2)}, u32[]{:S(2)}) %collective-permute-start.3) | collective-permute-done | bytes 36896 | tf_op jit(solution)/shard_map/ppermute | solution.py:624
  52.4 0.7 %shard_map.114 = (f32[4,8,576]{2,1,0:T(8,128)}, f32[4,32,64]{2,1,0:T(8,128)}, f32[4,8,256]{2,1,0:T(8,128)}) custom-call(bf16[2,72,128]{2,1,0:T(8,128)(2,1)S(1)} %reduce_sum.22.mine_ref, bf16[2,72,128]{2,1,0:T(8,128)(2,1)S(1)} %collective-permute-done.3.theirs_ref), custom_call_target="tpu_custom_call" | custom-call | bytes 1048576 | tf_op jit(solution)/shard_map/pallas_call | solution.py:51
  (4 shorter events, 0.1 us)
Async XLA Ops:
  2.1 4.0 %collective-permute-start = (bf16[64,128]{1,0:T(8,128)(2,1)S(1)}, bf16[64,128]{1,0:T(8,128)(2,1)S(1)}, u32[]{:S(2)}, u32[]{:S(2)}) collective-permute-start(bf16[64,128]{1,0:T(8,128)(2,1)S(1)} %get-tuple-element.42), channel_id=1, source_target_pairs={{0,8},{8,0},{1,9},{9,1},{2,10},{10,2},{3,11},{11,3},{4,12},{12,4},... | collective-permute-start | bytes 49160 | tf_op jit(solution)/shard_map/ppermute | solution.py:553
  3.6 3.2 %collective-permute-start.1 = (bf16[64,128]{1,0:T(8,128)(2,1)S(1)}, bf16[64,128]{1,0:T(8,128)(2,1)S(1)}, u32[]{:S(2)}, u32[]{:S(2)}) collective-permute-start(bf16[64,128]{1,0:T(8,128)(2,1)S(1)} %get-tuple-element.43), channel_id=1, source_target_pairs={{8,16},{24,32},{40,48},{56,64},{72,80},{88,96},{104,112},{120,0},{... | collective-permute-start | bytes 49160 | tf_op jit(solution)/shard_map/ppermute | solution.py:555
  18.7 3.7 %collective-permute-start.2 = (bf16[1152,128]{1,0:T(8,128)(2,1)S(1)}, bf16[1152,128]{1,0:T(8,128)(2,1)S(1)}, u32[]{:S(2)}, u32[]{:S(2)}) collective-permute-start(bf16[1152,128]{1,0:T(8,128)(2,1)S(1)} %get-tuple-element.56), channel_id=1, source_target_pairs={{0,8},{8,0},{1,9},{9,1},{2,10},{10,2},{3,11},{11,3},{4,12},{12,4},... | collective-permute-start | bytes 884744 | tf_op jit(solution)/shard_map/ppermute | solution.py:608
  23.2 15.4 %all-to-all-start = ((bf16[16,72,128]{2,1,0:T(8,128)(2,1)}), bf16[16,72,128]{2,1,0:T(8,128)(2,1)S(1)}, u32[]{:S(2)}, u32[]{:S(2)}) async-start(bf16[16,72,128]{2,1,0:T(8,128)(2,1)} %bitcast.5), calls=%async_computation | async-start | bytes 589824 | tf_op jit(solution)/shard_map/all_to_all | solution.py:610
  48.5 3.8 %collective-permute-start.3 = (bf16[2,72,128]{2,1,0:T(8,128)(2,1)S(1)}, bf16[2,72,128]{2,1,0:T(8,128)(2,1)S(1)}, u32[]{:S(2)}, u32[]{:S(2)}) collective-permute-start(bf16[2,72,128]{2,1,0:T(8,128)(2,1)S(1)} %reduce_sum.22.mine_ref), channel_id=1, source_target_pairs={{0,8},{8,0},{1,9},{9,1},{2,10},{10,2},{3,11},{11,3},{4,12},{12,4},... | collective-permute-start | bytes 110600 | tf_op jit(solution)/shard_map/ppermute | solution.py:624

commit v7 on v6

--- a/solution.py
+++ b/solution.py
@@ -606,8 +606,6 @@
         mib=40,
     )
     came = lax.ppermute(other, "core", [(0, 1), (1, 0)])
-    share = (own.astype(F32) + came.astype(F32)).astype(BF)
-    parts = lax.all_to_all(share.reshape(16, UNITS, 128), ("xl", "ens"), 0, 0, tiled=True)
     section_out, input_grad, blank = call(
         tail_kernel,
         [shape(C, H, WD)] * 2 + [shape(UNITS, 128, dtype=F32)],
@@ -616,7 +614,9 @@
         flops=1 << 30,
         mib=16,
     )
-    total = (jnp.sum(parts.astype(F32), axis=0) + blank).astype(BF)
+    share = own.reshape(16, UNITS, 128).astype(F32) + came.reshape(16, UNITS, 128).astype(F32)
+    parts = lax.all_to_all((share + blank).astype(BF), ("xl", "ens"), 0, 0, tiled=True)
+    total = jnp.sum(parts.astype(F32), axis=0).astype(BF)
     chips = lax.axis_size(("y", "xl"))
     parts = jnp.broadcast_to(total[None], (chips, UNITS, 128))
     parts = lax.all_to_all(parts, ("y", "xl"), 0, 0, tiled=True)

time: 53.4 us -> 52.5 us (0.983)
  blocking collectives: 9.86 us -> 24.2 us
  waiting for transfers between devices: 8.82 us -> 1.58 us
  starting transfers between devices: 15.7 us -> 8.73 us
  other arithmetic: 0.86 us -> 0.18 us
    all_to_all x0 -> x1, blocking collectives: none -> 15.7 us  [local(): lax.all_to_all((share + blank).astype(BF), ('xl', 'ens'), 0, 0, tiled=True)]
    all_to_all x1 -> x0, starting transfers between devices: 7.47 us -> none  [local(): lax.all_to_all(share.reshape(16, UNITS, 128), ('xl', 'ens'), 0, 0, tiled=...]
    all_to_all x1 -> x0, waiting for transfers between devices: 6.04 us -> none  [local(): lax.all_to_all(share.reshape(16, UNITS, 128), ('xl', 'ens'), 0, 0, tiled=...]
    all_to_all x1, blocking collectives: 9.86 us -> 8.49 us  [local(): parts = lax.all_to_all(parts, ('y', 'xl'), 0, 0, tiled=True)]
    ppermute x1, waiting for transfers between devices: 1.21 us -> 0.01 us  [local(): came = lax.ppermute(other, 'core', [(0, 1), (1, 0)])]
    convert_element_type x2 -> x1, other arithmetic: 0.79 us -> 0.05 us  [local(): (share + blank).astype(BF)]
  transfers between devices with their start and end apart: 5 -> 4, of which waited for: 4 -> 2; matrix products, arithmetic and copies ran while one was open for 0% -> 0% of each run, Pallas kernels for 6% -> 6%
where the time goes in v7:
time: 52.5 us; the launch traced here: 52.3 us
  blocking collectives  24.2 us (46%)
  Pallas kernels  16.9 us (32%)
  starting transfers between devices  8.73 us (17%)
  waiting for transfers between devices  1.58 us (3%)
  between operations  0.69 us (1%)
    pallas_call x5, Pallas kernels, call(): pl.pallas_call(body, out_shape=outs, in_specs=specs, out_specs=jax.tree.m...  16.9 us
    all_to_all x1, blocking collectives, local(): lax.all_to_all((share + blank).astype(BF), ('xl', 'ens'), 0, 0, tiled=True)  15.7 us
    all_to_all x1, blocking collectives, local(): parts = lax.all_to_all(parts, ('y', 'xl'), 0, 0, tiled=True)  8.49 us
    ppermute x1, starting transfers between devices, local(): theirs = lax.ppermute(mine, 'core', [(0, 1), (1, 0)])  3.46 us
    ppermute x1, starting transfers between devices, local(): came = lax.ppermute(other, 'core', [(0, 1), (1, 0)])  2.5 us
    ppermute x1, starting transfers between devices, local(): inner = lax.ppermute(inner, 'core', [(0, 1), (1, 0)])  1.5 us
    ppermute x1, starting transfers between devices, local(): lax.ppermute(outer, LON, across + [(target, source) for source, target in...  1.27 us
  transfers between devices with their start and end apart: 4, of which 2 were waited for; matrix products, arithmetic and copies ran while one was open for 0% of the time, Pallas kernels for 6%

profile of v7, /device:TPU:1, one launch (start us, length us, event | category | flops | bytes accessed | tf_op | source)
XLA Modules:
  0.0 52.3 jit_solution(17794847641989873123)
XLA Ops:
  0.6 1.5 %shard_map.110 = (bf16[64,128]{1,0:T(8,128)(2,1)S(1)}, bf16[64,128]{1,0:T(8,128)(2,1)S(1)}, s32[8,128]{1,0:T(8,128)S(1)}, bf16[64,8,256]{2,1,0:T(8,128)(2,1)S(1)...) custom-call(s32[16]{0:T(128)} %refs_0_.1, ...), custom_call_target="tpu_custom_call" | custom-call | bytes 1048576 | tf_op jit(solution)/shard_map/pallas_call | solution.py:51
  2.1 1.5 %collective-permute-start = (bf16[64,128]{1,0:T(8,128)(2,1)S(1)}, bf16[64,128]{1,0:T(8,128)(2,1)S(1)}, u32[]{:S(2)}, u32[]{:S(2)}) collective-permute-start(bf16[64,128]{1,0:T(8,128)(2,1)S(1)} %get-tuple-element.42), channel_id=1, source_target_pairs={{0,8},{8,0},{1,9},{9,1},{2,10},{10,2},{3,11},{11,3},{4,12},{12,4},... | collective-permute-start | bytes 49160 | tf_op jit(solution)/shard_map/ppermute | solution.py:553
  3.6 1.3 %collective-permute-start.1 = (bf16[64,128]{1,0:T(8,128)(2,1)S(1)}, bf16[64,128]{1,0:T(8,128)(2,1)S(1)}, u32[]{:S(2)}, u32[]{:S(2)}) collective-permute-start(bf16[64,128]{1,0:T(8,128)(2,1)S(1)} %get-tuple-element.43), channel_id=1, source_target_pairs={{8,16},{24,32},{40,48},{56,64},{72,80},{88,96},{104,112},{120,0},{... | collective-permute-start | bytes 49160 | tf_op jit(solution)/shard_map/ppermute | solution.py:555
  4.9 1.2 %shard_map.111 = (bf16[64,2176]{1,0:T(8,128)(2,1)S(1)}, bf16[64,2176]{1,0:T(8,128)(2,1)S(1)}, bf16[4,192,192]{2,1,0:T(8,128)(2,1)S(1)}, bf16[4,192,192]{2,1,0:T(...) custom-call(s32[8,128]{1,0:T(8,128)S(1)} %get-tuple-element.33.flag_, ...), custom_call_target="tpu_custom_call" | custom-call | flops 134217728 | bytes 1048576 | tf_op jit(solution)/shard_map/pallas_call | solution.py:51
  6.1 0.0 collective-permute-done.inner_ref
  6.1 0.7 %collective-permute-done.1.outer_ref = bf16[64,128]{1,0:T(8,128)(2,1)S(1)} collective-permute-done((bf16[64,128]{1,0:T(8,128)(2,1)S(1)}, bf16[64,128]{1,0:T(8,128)(2,1)S(1)}, u32[]{:S(2)}, u32[]{:S(2)}) %collective-permute-start.1) | collective-permute-done | bytes 16416 | tf_op jit(solution)/shard_map/ppermute | solution.py:555
  6.8 11.7 %shard_map.112 = (bf16[64,2176]{1,0:T(8,128)(2,1)S(1)}, bf16[64,2176]{1,0:T(8,128)(2,1)S(1)}, bf16[64,2176]{1,0:T(8,128)(2,1)S(1)}, bf16[1152,128]{1,0:T(8,128)(2,1)S(1)}, bf16[1152,128]{1,0:T(8,128)(2,1)S(1)}) custom-call(bf16[64,2176]{1,0:T(8,128)(2,1)S(1)} %get-tuple-element.40.field_ref, bf16[64,2176]{1,0:T(8,128)(2,1)S(1)} %get-tuple-element.41.slope_ref, ...), custom_call_target="tpu_custom_call" | custom-call | flops 8589934592 | bytes 1048576 | tf_op jit(solution)/shard_map/pallas_call | solution.py:51
  18.5 2.5 %collective-permute-start.2 = (bf16[1152,128]{1,0:T(8,128)(2,1)S(1)}, bf16[1152,128]{1,0:T(8,128)(2,1)S(1)}, u32[]{:S(2)}, u32[]{:S(2)}) collective-permute-start(bf16[1152,128]{1,0:T(8,128)(2,1)S(1)} %get-tuple-element.56), channel_id=1, source_target_pairs={{0,8},{8,0},{1,9},{9,1},{2,10},{10,2},{3,11},{11,3},{4,12},{12,4},... | collective-permute-start | bytes 884744 | tf_op jit(solution)/shard_map/ppermute | solution.py:608
  21.0 1.8 %shard_map.113 = (bf16[64,8,256]{2,1,0:T(8,128)(2,1)}, bf16[64,8,256]{2,1,0:T(8,128)(2,1)}, f32[72,128]{1,0:T(8,128)S(1)}) custom-call(s32[8,128]{1,0:T(8,128)S(1)} %get-tuple-element.33.flag_ref, bf16[64,2176]{1,0:T(8,128)(2,1)S(1)} %get-tuple-element.50.flat_ref, bf16[64,2176]{1,0:T(8,128)(2,1)S(1)} %get-tuple-element.51.up_in, ...), custom_call_target="tpu_custom_call" | custom-call | flops 1073741824 | bytes 1048576 | tf_op jit(solution)/shard_map/pallas_call | solution.py:51
  22.8 0.0 collective-permute-done.2
  22.8 0.1 convert_add_fusion
  22.9 0.1 add_convert_fusion
  22.9 15.7 %all_to_all.10 = bf16[16,72,128]{2,1,0:T(8,128)(2,1)S(1)} all-to-all(bf16[16,72,128]{2,1,0:T(8,128)(2,1)S(1)} %add_convert_fusion), channel_id=1, replica_groups=mesh['y'=4,'xl'=2,'core'=2,'ens'=8] {'xl','ens'}, dimensions={0} | all-to-all | bytes 589824 | tf_op jit(solution)/shard_map/all_to_all | solution.py:618
  38.7 8.5 %all_to_all.11 = bf16[8,72,128]{2,1,0:T(8,128)(2,1)S(1)} all-to-all(bf16[8,72,128]{2,1,0:T(8,128)(2,1)S(1)} %broadcast_in_dim.15), channel_id=1, replica_groups=mesh['y'=4,'xl'=2,'core'=2,'ens'=8] {'y','xl'}, dimensions={0} | all-to-all | bytes 294912 | tf_op jit(solution)/shard_map/all_to_all | solution.py:622
  47.2 3.5 %collective-permute-start.3 = (bf16[2,72,128]{2,1,0:T(8,128)(2,1)S(1)}, bf16[2,72,128]{2,1,0:T(8,128)(2,1)S(1)}, u32[]{:S(2)}, u32[]{:S(2)}) collective-permute-start(bf16[2,72,128]{2,1,0:T(8,128)(2,1)S(1)} %reduce_sum.25.mine_ref), channel_id=1, source_target_pairs={{0,8},{8,0},{1,9},{9,1},{2,10},{10,2},{3,11},{11,3},{4,12},{12,4},... | collective-permute-start | bytes 110600 | tf_op jit(solution)/shard_map/ppermute | solution.py:624
  50.7 0.9 %collective-permute-done.3.theirs_ref = bf16[2,72,128]{2,1,0:T(8,128)(2,1)S(1)} collective-permute-done((bf16[2,72,128]{2,1,0:T(8,128)(2,1)S(1)}, bf16[2,72,128]{2,1,0:T(8,128)(2,1)S(1)}, u32[]{:S(2)}, u32[]{:S(2)}) %collective-permute-start.3) | collective-permute-done | bytes 36896 | tf_op jit(solution)/shard_map/ppermute | solution.py:624
  51.6 0.7 %shard_map.114 = (f32[4,8,576]{2,1,0:T(8,128)}, f32[4,32,64]{2,1,0:T(8,128)}, f32[4,8,256]{2,1,0:T(8,128)}) custom-call(bf16[2,72,128]{2,1,0:T(8,128)(2,1)S(1)} %reduce_sum.25.mine_ref, bf16[2,72,128]{2,1,0:T(8,128)(2,1)S(1)} %collective-permute-done.3.theirs_ref), custom_call_target="tpu_custom_call" | custom-call | bytes 1048576 | tf_op jit(solution)/shard_map/pallas_call | solution.py:51
  (3 shorter events, 0.1 us)
Async XLA Ops:
  2.1 4.0 %collective-permute-start = (bf16[64,128]{1,0:T(8,128)(2,1)S(1)}, bf16[64,128]{1,0:T(8,128)(2,1)S(1)}, u32[]{:S(2)}, u32[]{:S(2)}) collective-permute-start(bf16[64,128]{1,0:T(8,128)(2,1)S(1)} %get-tuple-element.42), channel_id=1, source_target_pairs={{0,8},{8,0},{1,9},{9,1},{2,10},{10,2},{3,11},{11,3},{4,12},{12,4},... | collective-permute-start | bytes 49160 | tf_op jit(solution)/shard_map/ppermute | solution.py:553
  3.6 3.2 %collective-permute-start.1 = (bf16[64,128]{1,0:T(8,128)(2,1)S(1)}, bf16[64,128]{1,0:T(8,128)(2,1)S(1)}, u32[]{:S(2)}, u32[]{:S(2)}) collective-permute-start(bf16[64,128]{1,0:T(8,128)(2,1)S(1)} %get-tuple-element.43), channel_id=1, source_target_pairs={{8,16},{24,32},{40,48},{56,64},{72,80},{88,96},{104,112},{120,0},{... | collective-permute-start | bytes 49160 | tf_op jit(solution)/shard_map/ppermute | solution.py:555
  18.5 4.3 %collective-permute-start.2 = (bf16[1152,128]{1,0:T(8,128)(2,1)S(1)}, bf16[1152,128]{1,0:T(8,128)(2,1)S(1)}, u32[]{:S(2)}, u32[]{:S(2)}) collective-permute-start(bf16[1152,128]{1,0:T(8,128)(2,1)S(1)} %get-tuple-element.56), channel_id=1, source_target_pairs={{0,8},{8,0},{1,9},{9,1},{2,10},{10,2},{3,11},{11,3},{4,12},{12,4},... | collective-permute-start | bytes 884744 | tf_op jit(solution)/shard_map/ppermute | solution.py:608
  47.2 4.3 %collective-permute-start.3 = (bf16[2,72,128]{2,1,0:T(8,128)(2,1)S(1)}, bf16[2,72,128]{2,1,0:T(8,128)(2,1)S(1)}, u32[]{:S(2)}, u32[]{:S(2)}) collective-permute-start(bf16[2,72,128]{2,1,0:T(8,128)(2,1)S(1)} %reduce_sum.25.mine_ref), channel_id=1, source_target_pairs={{0,8},{8,0},{1,9},{9,1},{2,10},{10,2},{3,11},{11,3},{4,12},{12,4},... | collective-permute-start | bytes 110600 | tf_op jit(solution)/shard_map/ppermute | solution.py:624

commit v8 on v7

--- a/solution.py
+++ b/solution.py
@@ -30,7 +30,7 @@
 GELU_PARTS = 4
 GROUP = 3
 BACKWARD_LAG = 8
-TURN = 8
+TURN = 6
 
 
 LON = ("y", "xl", "core")
@@ -82,13 +82,14 @@
         copies.append(pltpu.make_async_copy(source, target, sems.at[i + 1]))
     for copy in copies:
         copy.start()
-    for copy in copies[0:3]:
-        copy.wait()
+    copies[1].wait()
+    spread(wide_f, targets[0])
+    copies[2].wait()
+    spread(wide_g, targets[1])
+    copies[0].wait()
     sector = (lax.axis_index("y") * 2 + lax.axis_index("xl")) * 2 + lax.axis_index("core")
     flip = orient_s[sector]
     flag_ref[...] = jnp.full((8, 128), flip, jnp.int32)
-    spread(wide_f, targets[0])
-    spread(wide_g, targets[1])
     lane = lax.broadcasted_iota(jnp.int32, (C, 128), 1)
     low = jnp.zeros((C, 128), F32)
     high = jnp.zeros((C, 128), F32)

time: 52.5 us -> 52.8 us (level)
  no operation moved by 1% of the time
where the time goes in v8:
time: 52.8 us; the launch traced here: 52.6 us
  blocking collectives  24.2 us (46%)
  Pallas kernels  17.2 us (33%)
  starting transfers between devices  8.75 us (17%)
  waiting for transfers between devices  1.58 us (3%)
  between operations  0.69 us (1%)
    pallas_call x5, Pallas kernels, call(): pl.pallas_call(body, out_shape=outs, in_specs=specs, out_specs=jax.tree.m...  17.2 us
    all_to_all x1, blocking collectives, local(): lax.all_to_all((share + blank).astype(BF), ('xl', 'ens'), 0, 0, tiled=True)  15.7 us
    all_to_all x1, blocking collectives, local(): parts = lax.all_to_all(parts, ('y', 'xl'), 0, 0, tiled=True)  8.47 us
    ppermute x1, starting transfers between devices, local(): theirs = lax.ppermute(mine, 'core', [(0, 1), (1, 0)])  3.47 us
    ppermute x1, starting transfers between devices, local(): came = lax.ppermute(other, 'core', [(0, 1), (1, 0)])  2.51 us
    ppermute x1, starting transfers between devices, local(): inner = lax.ppermute(inner, 'core', [(0, 1), (1, 0)])  1.5 us
    ppermute x1, starting transfers between devices, local(): lax.ppermute(outer, LON, across + [(target, source) for source, target in...  1.27 us
  transfers between devices with their start and end apart: 4, of which 2 were waited for; matrix products, arithmetic and copies ran while one was open for 0% of the time, Pallas kernels for 6%

profile of v8, /device:TPU:1, one launch (start us, length us, event | category | flops | bytes accessed | tf_op | source)
XLA Modules:
  0.0 52.6 jit_solution(15544853878859729242)
XLA Ops:
  0.6 1.5 %shard_map.110 = (bf16[64,128]{1,0:T(8,128)(2,1)S(1)}, bf16[64,128]{1,0:T(8,128)(2,1)S(1)}, s32[8,128]{1,0:T(8,128)S(1)}, bf16[64,8,256]{2,1,0:T(8,128)(2,1)S(1)...) custom-call(s32[16]{0:T(128)} %refs_0_.1, ...), custom_call_target="tpu_custom_call" | custom-call | bytes 1048576 | tf_op jit(solution)/shard_map/pallas_call | solution.py:51
  2.1 1.5 %collective-permute-start = (bf16[64,128]{1,0:T(8,128)(2,1)S(1)}, bf16[64,128]{1,0:T(8,128)(2,1)S(1)}, u32[]{:S(2)}, u32[]{:S(2)}) collective-permute-start(bf16[64,128]{1,0:T(8,128)(2,1)S(1)} %get-tuple-element.42), channel_id=1, source_target_pairs={{0,8},{8,0},{1,9},{9,1},{2,10},{10,2},{3,11},{11,3},{4,12},{12,4},... | collective-permute-start | bytes 49160 | tf_op jit(solution)/shard_map/ppermute | solution.py:554
  3.6 1.3 %collective-permute-start.1 = (bf16[64,128]{1,0:T(8,128)(2,1)S(1)}, bf16[64,128]{1,0:T(8,128)(2,1)S(1)}, u32[]{:S(2)}, u32[]{:S(2)}) collective-permute-start(bf16[64,128]{1,0:T(8,128)(2,1)S(1)} %get-tuple-element.43), channel_id=1, source_target_pairs={{8,16},{24,32},{40,48},{56,64},{72,80},{88,96},{104,112},{120,0},{... | collective-permute-start | bytes 49160 | tf_op jit(solution)/shard_map/ppermute | solution.py:556
  4.9 1.2 %shard_map.111 = (bf16[64,2176]{1,0:T(8,128)(2,1)S(1)}, bf16[64,2176]{1,0:T(8,128)(2,1)S(1)}, bf16[4,192,192]{2,1,0:T(8,128)(2,1)S(1)}, bf16[4,192,192]{2,1,0:T(...) custom-call(s32[8,128]{1,0:T(8,128)S(1)} %get-tuple-element.33.flag_, ...), custom_call_target="tpu_custom_call" | custom-call | flops 134217728 | bytes 1048576 | tf_op jit(solution)/shard_map/pallas_call | solution.py:51
  6.1 0.0 collective-permute-done.inner_ref
  6.1 0.7 %collective-permute-done.1.outer_ref = bf16[64,128]{1,0:T(8,128)(2,1)S(1)} collective-permute-done((bf16[64,128]{1,0:T(8,128)(2,1)S(1)}, bf16[64,128]{1,0:T(8,128)(2,1)S(1)}, u32[]{:S(2)}, u32[]{:S(2)}) %collective-permute-start.1) | collective-permute-done | bytes 16416 | tf_op jit(solution)/shard_map/ppermute | solution.py:556
  6.8 12.0 %shard_map.112 = (bf16[64,2176]{1,0:T(8,128)(2,1)S(1)}, bf16[64,2176]{1,0:T(8,128)(2,1)S(1)}, bf16[64,2176]{1,0:T(8,128)(2,1)S(1)}, bf16[1152,128]{1,0:T(8,128)(2,1)S(1)}, bf16[1152,128]{1,0:T(8,128)(2,1)S(1)}) custom-call(bf16[64,2176]{1,0:T(8,128)(2,1)S(1)} %get-tuple-element.40.field_ref, bf16[64,2176]{1,0:T(8,128)(2,1)S(1)} %get-tuple-element.41.slope_ref, ...), custom_call_target="tpu_custom_call" | custom-call | flops 8589934592 | bytes 1048576 | tf_op jit(solution)/shard_map/pallas_call | solution.py:51
  18.8 2.5 %collective-permute-start.2 = (bf16[1152,128]{1,0:T(8,128)(2,1)S(1)}, bf16[1152,128]{1,0:T(8,128)(2,1)S(1)}, u32[]{:S(2)}, u32[]{:S(2)}) collective-permute-start(bf16[1152,128]{1,0:T(8,128)(2,1)S(1)} %get-tuple-element.56), channel_id=1, source_target_pairs={{0,8},{8,0},{1,9},{9,1},{2,10},{10,2},{3,11},{11,3},{4,12},{12,4},... | collective-permute-start | bytes 884744 | tf_op jit(solution)/shard_map/ppermute | solution.py:609
  21.3 1.8 %shard_map.113 = (bf16[64,8,256]{2,1,0:T(8,128)(2,1)}, bf16[64,8,256]{2,1,0:T(8,128)(2,1)}, f32[72,128]{1,0:T(8,128)S(1)}) custom-call(s32[8,128]{1,0:T(8,128)S(1)} %get-tuple-element.33.flag_ref, bf16[64,2176]{1,0:T(8,128)(2,1)S(1)} %get-tuple-element.50.flat_ref, bf16[64,2176]{1,0:T(8,128)(2,1)S(1)} %get-tuple-element.51.up_in, ...), custom_call_target="tpu_custom_call" | custom-call | flops 1073741824 | bytes 1048576 | tf_op jit(solution)/shard_map/pallas_call | solution.py:51
  23.1 0.0 collective-permute-done.2
  23.1 0.1 convert_add_fusion
  23.2 0.1 add_convert_fusion
  23.2 15.7 %all_to_all.10 = bf16[16,72,128]{2,1,0:T(8,128)(2,1)S(1)} all-to-all(bf16[16,72,128]{2,1,0:T(8,128)(2,1)S(1)} %add_convert_fusion), channel_id=1, replica_groups=mesh['y'=4,'xl'=2,'core'=2,'ens'=8] {'xl','ens'}, dimensions={0} | all-to-all | bytes 589824 | tf_op jit(solution)/shard_map/all_to_all | solution.py:619
  39.1 8.5 %all_to_all.11 = bf16[8,72,128]{2,1,0:T(8,128)(2,1)S(1)} all-to-all(bf16[8,72,128]{2,1,0:T(8,128)(2,1)S(1)} %broadcast_in_dim.15), channel_id=1, replica_groups=mesh['y'=4,'xl'=2,'core'=2,'ens'=8] {'y','xl'}, dimensions={0} | all-to-all | bytes 294912 | tf_op jit(solution)/shard_map/all_to_all | solution.py:623
  47.6 3.5 %collective-permute-start.3 = (bf16[2,72,128]{2,1,0:T(8,128)(2,1)S(1)}, bf16[2,72,128]{2,1,0:T(8,128)(2,1)S(1)}, u32[]{:S(2)}, u32[]{:S(2)}) collective-permute-start(bf16[2,72,128]{2,1,0:T(8,128)(2,1)S(1)} %reduce_sum.25.mine_ref), channel_id=1, source_target_pairs={{0,8},{8,0},{1,9},{9,1},{2,10},{10,2},{3,11},{11,3},{4,12},{12,4},... | collective-permute-start | bytes 110600 | tf_op jit(solution)/shard_map/ppermute | solution.py:625
  51.0 0.9 %collective-permute-done.3.theirs_ref = bf16[2,72,128]{2,1,0:T(8,128)(2,1)S(1)} collective-permute-done((bf16[2,72,128]{2,1,0:T(8,128)(2,1)S(1)}, bf16[2,72,128]{2,1,0:T(8,128)(2,1)S(1)}, u32[]{:S(2)}, u32[]{:S(2)}) %collective-permute-start.3) | collective-permute-done | bytes 36896 | tf_op jit(solution)/shard_map/ppermute | solution.py:625
  51.9 0.7 %shard_map.114 = (f32[4,8,576]{2,1,0:T(8,128)}, f32[4,32,64]{2,1,0:T(8,128)}, f32[4,8,256]{2,1,0:T(8,128)}) custom-call(bf16[2,72,128]{2,1,0:T(8,128)(2,1)S(1)} %reduce_sum.25.mine_ref, bf16[2,72,128]{2,1,0:T(8,128)(2,1)S(1)} %collective-permute-done.3.theirs_ref), custom_call_target="tpu_custom_call" | custom-call | bytes 1048576 | tf_op jit(solution)/shard_map/pallas_call | solution.py:51
  (3 shorter events, 0.1 us)
Async XLA Ops:
  2.1 4.0 %collective-permute-start = (bf16[64,128]{1,0:T(8,128)(2,1)S(1)}, bf16[64,128]{1,0:T(8,128)(2,1)S(1)}, u32[]{:S(2)}, u32[]{:S(2)}) collective-permute-start(bf16[64,128]{1,0:T(8,128)(2,1)S(1)} %get-tuple-element.42), channel_id=1, source_target_pairs={{0,8},{8,0},{1,9},{9,1},{2,10},{10,2},{3,11},{11,3},{4,12},{12,4},... | collective-permute-start | bytes 49160 | tf_op jit(solution)/shard_map/ppermute | solution.py:554
  3.6 3.2 %collective-permute-start.1 = (bf16[64,128]{1,0:T(8,128)(2,1)S(1)}, bf16[64,128]{1,0:T(8,128)(2,1)S(1)}, u32[]{:S(2)}, u32[]{:S(2)}) collective-permute-start(bf16[64,128]{1,0:T(8,128)(2,1)S(1)} %get-tuple-element.43), channel_id=1, source_target_pairs={{8,16},{24,32},{40,48},{56,64},{72,80},{88,96},{104,112},{120,0},{... | collective-permute-start | bytes 49160 | tf_op jit(solution)/shard_map/ppermute | solution.py:556
  18.8 4.3 %collective-permute-start.2 = (bf16[1152,128]{1,0:T(8,128)(2,1)S(1)}, bf16[1152,128]{1,0:T(8,128)(2,1)S(1)}, u32[]{:S(2)}, u32[]{:S(2)}) collective-permute-start(bf16[1152,128]{1,0:T(8,128)(2,1)S(1)} %get-tuple-element.56), channel_id=1, source_target_pairs={{0,8},{8,0},{1,9},{9,1},{2,10},{10,2},{3,11},{11,3},{4,12},{12,4},... | collective-permute-start | bytes 884744 | tf_op jit(solution)/shard_map/ppermute | solution.py:609
  47.6 4.3 %collective-permute-start.3 = (bf16[2,72,128]{2,1,0:T(8,128)(2,1)S(1)}, bf16[2,72,128]{2,1,0:T(8,128)(2,1)S(1)}, u32[]{:S(2)}, u32[]{:S(2)}) collective-permute-start(bf16[2,72,128]{2,1,0:T(8,128)(2,1)S(1)} %reduce_sum.25.mine_ref), channel_id=1, source_target_pairs={{0,8},{8,0},{1,9},{9,1},{2,10},{10,2},{3,11},{11,3},{4,12},{12,4},... | collective-permute-start | bytes 110600 | tf_op jit(solution)/shard_map/ppermute | solution.py:625
